TPU v7x, 32 devices: a whole 2x2x4 slice. The times are simulated.
32 devices in a mesh: batch: 8 (over y, x, core), blk: 4 (over z).
Axes of the slice: x: 2, y: 2, z: 4, core: 2. Of those that a mesh axis runs over, the one named last changes fastest.
Arguments:
- hidden_in: bfloat16 [64, 512, 768], P('batch', 'blk'), may hold values from -6 to 6
- lengths: int32 [64, 8], P('batch'), may hold values from 0 to 512, as said below
- qkv_weight: bfloat16 [768, 2304], replicated, may hold values from -0.21875 to 0.21875
- qv_bias: bfloat16 [2, 768], replicated, may hold values from -3 to 3
- out_weight: bfloat16 [768, 768], replicated, may hold values from -0.875 to 0.875
- out_bias: bfloat16 [768], replicated, may hold values from -2 to 2
- attn_gain: bfloat16 [768], replicated, may hold values from 0.5 to 1.5
- attn_shift: bfloat16 [768], replicated, may hold values from -2 to 2
- up_weight: bfloat16 [768, 3072], replicated, may hold values from -0.21875 to 0.21875
- up_bias: bfloat16 [3072], replicated, may hold values from -3 to 3
- down_weight: bfloat16 [3072, 768], replicated, may hold values from -0.109375 to 0.109375
- down_bias: bfloat16 [768], replicated, may hold values from -2 to 2
- ffn_gain: bfloat16 [768], replicated, may hold values from 0.5 to 1.5
- ffn_shift: bfloat16 [768], replicated, may hold values from -2 to 2
- head_weight: bfloat16 [768], replicated, may hold values from -0.21875 to 0.21875
- head_bias: bfloat16 [1], replicated, may hold values from -3 to 3
- hidden_cot: bfloat16 [64, 512, 768], P('batch', 'blk'), may hold values from -6 to 6
- term_cot: float32 [64, 512], P('batch', 'blk'), may hold values from -6 to 6
Outputs:
- hidden_out: bfloat16 [64, 512, 768], P('batch', 'blk')
- term_weight: float32 [64, 512], P('batch', 'blk')
- grad_hidden: float32 [64, 512, 768], P('batch', 'blk')
- grad_qkv_weight: float32 [768, 2304], replicated
- grad_qv_bias: float32 [2, 768], replicated
- grad_out_weight: float32 [768, 768], replicated
- grad_out_bias: float32 [768], replicated
- grad_attn_gain: float32 [768], replicated
- grad_attn_shift: float32 [768], replicated
- grad_up_weight: float32 [768, 3072], replicated
- grad_up_bias: float32 [3072], replicated
- grad_down_weight: float32 [3072, 768], replicated
- grad_down_bias: float32 [768], replicated
- grad_ffn_gain: float32 [768], replicated
- grad_ffn_shift: float32 [768], replicated
- grad_head_weight: float32 [768], replicated
- grad_head_bias: float32 [1], replicated
Inputs may be any that keep to these rules, and one draw needn't show every extreme that they name: Row r of lengths holds, in order, the token counts of the passages packed into row r from its first slot on; they add up to 512 or less, and the remaining slots are padding.
All inputs are finite; a program needn't handle non-finite values.
Results may differ from a plain program's by a relative error of at most 0.018.
Values may be sent and summed in bfloat16 or wider, within the bound.
No kernel may reach another device: no remote copies, remote signals or barrier semaphores. Data moves between devices by JAX's collectives and lax.ppermute only.
A program may use at most 256 MiB of HBM per device.

v0:
```python
import jax
import jax.numpy as jnp
from jax import lax
from jax.sharding import PartitionSpec as P

HEADS = 12
HD = 64


epsilon = 1e-06
masked_score = -1e30


def layer_norm(values, norm_gain, norm_shift):
    center = values - jnp.mean(values, axis=-1, keepdims=True)
    variance = jnp.mean(center * center, axis=-1, keepdims=True)
    return center * lax.rsqrt(variance + epsilon) * norm_gain + norm_shift


def norm_backward(values, norm_gain, norm_shift, upstream):
    result, pullback = jax.vjp(layer_norm, values, norm_gain, norm_shift)
    return pullback(upstream)


def gelu_exact(values):
    return jax.nn.gelu(values, approximate=False)


def document_ids(lengths, slot_count):
    passage_ends = jnp.cumsum(lengths, axis=-1)
    slot_index = jnp.arange(slot_count, dtype=jnp.int32)
    return jnp.sum((passage_ends[..., None, :] <= slot_index[:, None]).astype(jnp.int32), axis=-1)


def split_heads(tensor, row_count, per_map, length):
    return tensor.reshape(row_count // per_map, per_map, length, HEADS, HD)


def per_device(
    hidden_in,
    lengths,
    qkv_weight,
    qv_bias,
    out_weight,
    out_bias,
    attn_gain,
    attn_shift,
    up_weight,
    up_bias,
    down_weight,
    down_bias,
    ffn_gain,
    ffn_shift,
    head_weight,
    head_bias,
    hidden_cot,
    term_cot,
):
    row_count, seg_len, model_width = hidden_in.shape
    slot_count = seg_len * lax.axis_size("blk")
    per_map = max(1, min(row_count, 512 // seg_len))
    group_count = row_count // per_map
    score_scale = HD ** (-0.5)
    key_doc = document_ids(lengths, slot_count)
    query_doc = lax.dynamic_slice_in_dim(key_doc, lax.axis_index("blk") * seg_len, seg_len, 1)
    query_docs = query_doc.reshape(group_count, per_map, seg_len)
    key_docs = key_doc.reshape(group_count, per_map, slot_count)
    token_count = row_count * seg_len

    def masked_scores(queries, keys_part, q_doc, k_doc):
        scores = (
            jnp.einsum("rqhd,rkhd->rhqk", queries, keys_part, preferred_element_type=jnp.float32)
            * score_scale
        )
        same_doc = q_doc[:, None, :, None] == k_doc[:, None, None, :]
        return jnp.where(same_doc, scores, masked_score)

    def attend_group(pieces):
        queries, keys_part, vals_part, q_doc, k_doc = pieces
        scores = masked_scores(queries, keys_part, q_doc, k_doc)
        row_max = jnp.max(scores, axis=-1, keepdims=True)
        weights = jnp.exp(scores - row_max)
        row_total = jnp.sum(weights, axis=-1, keepdims=True)
        probs_low = (weights / row_total).astype(jnp.bfloat16)
        mixed = jnp.einsum(
            "rhqk,rkhd->rqhd", probs_low, vals_part, preferred_element_type=jnp.float32
        )
        return (mixed, (row_max + jnp.log(row_total))[..., 0])

    def attend_back(pieces):
        queries, keys_part, vals_part, q_doc, k_doc, log_total, upstream = pieces
        scores = masked_scores(queries, keys_part, q_doc, k_doc)
        probs = jnp.exp(scores - log_total[..., None])
        probs_low = probs.astype(jnp.bfloat16)
        dprobs = jnp.einsum(
            "rqhd,rkhd->rhqk", upstream, vals_part, preferred_element_type=jnp.float32
        )
        vals_grad = jnp.einsum(
            "rhqk,rqhd->rkhd", probs_low, upstream, preferred_element_type=jnp.float32
        )
        inner_sum = jnp.sum(probs * dprobs, axis=-1, keepdims=True)
        score_grad = (probs * (dprobs - inner_sum)).astype(jnp.bfloat16)
        query_grad = (
            jnp.einsum("rhqk,rkhd->rqhd", score_grad, keys_part, preferred_element_type=jnp.float32)
            * score_scale
        )
        key_grad = (
            jnp.einsum("rhqk,rqhd->rkhd", score_grad, queries, preferred_element_type=jnp.float32)
            * score_scale
        )
        return (query_grad, key_grad, vals_grad)

    tokens = hidden_in.reshape(token_count, model_width)
    bias_query = qv_bias[0].astype(jnp.float32)
    qkv_add = jnp.concatenate(
        [bias_query, jnp.zeros_like(bias_query), qv_bias[1].astype(jnp.float32)]
    )
    projected = (jnp.dot(tokens, qkv_weight, preferred_element_type=jnp.float32) + qkv_add).astype(
        jnp.bfloat16
    )
    query_heads = split_heads(projected[:, :model_width], row_count, per_map, seg_len)
    key_vals = projected[:, model_width:].reshape(row_count, seg_len, 2 * model_width)
    all_kv = lax.all_gather(key_vals, "blk", axis=1, tiled=True)
    key_heads = split_heads(all_kv[..., :model_width], row_count, per_map, slot_count)
    val_heads = split_heads(all_kv[..., model_width:], row_count, per_map, slot_count)
    mixed, log_total = lax.map(
        attend_group, (query_heads, key_heads, val_heads, query_docs, key_docs)
    )
    attended = mixed.reshape(token_count, model_width).astype(jnp.bfloat16)
    gain_attn = attn_gain.astype(jnp.float32)
    shift_attn = attn_shift.astype(jnp.float32)
    gain_ffn = ffn_gain.astype(jnp.float32)
    shift_ffn = ffn_shift.astype(jnp.float32)
    first_sum = (
        tokens.astype(jnp.float32)
        + jnp.dot(attended, out_weight, preferred_element_type=jnp.float32)
        + out_bias.astype(jnp.float32)
    )
    normed = layer_norm(first_sum, gain_attn, shift_attn)
    normed_low = normed.astype(jnp.bfloat16)
    gate_pre = jnp.dot(normed_low, up_weight, preferred_element_type=jnp.float32) + up_bias.astype(
        jnp.float32
    )
    activated = gelu_exact(gate_pre).astype(jnp.bfloat16)
    second_sum = (
        normed
        + jnp.dot(activated, down_weight, preferred_element_type=jnp.float32)
        + down_bias.astype(jnp.float32)
    )
    final_out = layer_norm(second_sum, gain_ffn, shift_ffn)
    head_vec = head_weight.astype(jnp.float32)
    logits = (
        jnp.dot(final_out, head_vec, precision=lax.Precision.HIGHEST)
        + head_bias.astype(jnp.float32)[0]
    )
    term_weight = jax.nn.softplus(logits)
    term_grad = term_cot.reshape(token_count) * jax.nn.sigmoid(logits)
    grad_head_weight = jnp.dot(term_grad, final_out, precision=lax.Precision.HIGHEST)
    grad_head_bias = jnp.sum(term_grad, keepdims=True)
    final_grad = (
        hidden_cot.reshape(token_count, model_width).astype(jnp.float32)
        + term_grad[:, None] * head_vec
    )
    second_grad, grad_ffn_gain, grad_ffn_shift = norm_backward(
        second_sum, gain_ffn, shift_ffn, final_grad
    )
    ffn_grad = second_grad.astype(jnp.bfloat16)
    grad_down_bias = jnp.sum(ffn_grad, axis=0, dtype=jnp.float32)
    grad_down_weight = jnp.einsum(
        "tf,td->fd", activated, ffn_grad, preferred_element_type=jnp.float32
    )
    act_grad = jnp.einsum("td,fd->tf", ffn_grad, down_weight, preferred_element_type=jnp.float32)
    gelu_pull = jax.vjp(gelu_exact, gate_pre)[1]
    gate_grad = gelu_pull(act_grad)[0].astype(jnp.bfloat16)
    grad_up_bias = jnp.sum(gate_grad, axis=0, dtype=jnp.float32)
    grad_up_weight = jnp.einsum(
        "td,tf->df", normed_low, gate_grad, preferred_element_type=jnp.float32
    )
    normed_grad = (
        jnp.einsum("tf,df->td", gate_grad, up_weight, preferred_element_type=jnp.float32)
        + second_grad
    )
    first_grad, grad_attn_gain, grad_attn_shift = norm_backward(
        first_sum, gain_attn, shift_attn, normed_grad
    )
    attn_grad = first_grad.astype(jnp.bfloat16)
    grad_out_bias = jnp.sum(attn_grad, axis=0, dtype=jnp.float32)
    grad_out_weight = jnp.einsum(
        "td,te->de", attended, attn_grad, preferred_element_type=jnp.float32
    )
    mixed_grad = jnp.einsum(
        "te,de->td", attn_grad, out_weight, preferred_element_type=jnp.float32
    ).astype(jnp.bfloat16)
    back_keys = split_heads(all_kv[..., :model_width], row_count, per_map, slot_count)
    back_vals = split_heads(all_kv[..., model_width:], row_count, per_map, slot_count)
    upstream_heads = split_heads(mixed_grad, row_count, per_map, seg_len)
    query_grad, key_grad, vals_grad = lax.map(
        attend_back,
        (query_heads, back_keys, back_vals, query_docs, key_docs, log_total, upstream_heads),
    )
    slot_grads = jnp.concatenate(
        [
            key_grad.reshape(row_count, slot_count, model_width),
            vals_grad.reshape(row_count, slot_count, model_width),
        ],
        axis=-1,
    )
    local_kv_grad = (
        lax.psum_scatter(slot_grads.astype(jnp.bfloat16), "blk", scatter_dimension=1, tiled=True)
        .astype(jnp.float32)
        .reshape(token_count, 2 * model_width)
    )
    proj_grad = jnp.concatenate(
        [query_grad.reshape(token_count, model_width), local_kv_grad], axis=-1
    ).astype(jnp.bfloat16)
    grad_qv_bias = jnp.stack(
        [
            jnp.sum(proj_grad[:, :model_width], axis=0, dtype=jnp.float32),
            jnp.sum(proj_grad[:, 2 * model_width :], axis=0, dtype=jnp.float32),
        ]
    )
    grad_qkv_weight = jnp.einsum("td,te->de", tokens, proj_grad, preferred_element_type=jnp.float32)
    grad_hidden = (
        jnp.einsum("te,de->td", proj_grad, qkv_weight, preferred_element_type=jnp.float32)
        + first_grad
    )
    vectors = lax.psum(
        (
            grad_qv_bias,
            grad_out_bias,
            grad_attn_gain,
            grad_attn_shift,
            grad_up_bias,
            grad_down_bias,
            grad_ffn_gain,
            grad_ffn_shift,
            grad_head_weight,
            grad_head_bias,
        ),
        ("batch", "blk"),
    )
    shares = (
        lax.psum_scatter(grad_qkv_weight, "batch", scatter_dimension=0, tiled=True),
        lax.psum_scatter(grad_out_weight, "batch", scatter_dimension=0, tiled=True),
        lax.psum_scatter(grad_up_weight, "batch", scatter_dimension=0, tiled=True),
        lax.psum_scatter(grad_down_weight, "batch", scatter_dimension=0, tiled=True),
    )
    shares = (
        lax.psum(shares[0].astype(jnp.bfloat16), "blk").astype(jnp.float32),
        lax.psum(shares[1].astype(jnp.bfloat16), "blk").astype(jnp.float32),
        lax.psum(shares[2].astype(jnp.bfloat16), "blk").astype(jnp.float32),
        lax.psum(shares[3].astype(jnp.bfloat16), "blk").astype(jnp.float32),
    )
    matrices = (
        lax.all_gather(shares[0].astype(jnp.bfloat16), "batch", axis=0, tiled=True).astype(
            jnp.float32
        ),
        lax.all_gather(shares[1].astype(jnp.bfloat16), "batch", axis=0, tiled=True).astype(
            jnp.float32
        ),
        lax.all_gather(shares[2].astype(jnp.bfloat16), "batch", axis=0, tiled=True).astype(
            jnp.float32
        ),
        lax.all_gather(shares[3].astype(jnp.bfloat16), "batch", axis=0, tiled=True).astype(
            jnp.float32
        ),
    )
    return (
        final_out.astype(jnp.bfloat16).reshape(row_count, seg_len, model_width),
        term_weight.reshape(row_count, seg_len),
        grad_hidden.reshape(row_count, seg_len, model_width),
        matrices[0],
        vectors[0],
        matrices[1],
        vectors[1],
        vectors[2],
        vectors[3],
        matrices[2],
        vectors[4],
        matrices[3],
        vectors[5],
        vectors[6],
        vectors[7],
        vectors[8],
        vectors[9],
    )


def solution(mesh):
    return jax.shard_map(
        per_device,
        mesh=mesh,
        in_specs=(
            P("batch", "blk", None),
            P("batch", None),
            P(),
            P(),
            P(),
            P(),
            P(),
            P(),
            P(),
            P(),
            P(),
            P(),
            P(),
            P(),
            P(),
            P(),
            P("batch", "blk", None),
            P("batch", "blk"),
        ),
        out_specs=(
            P("batch", "blk", None),
            P("batch", "blk"),
            P("batch", "blk", None),
            P(),
            P(),
            P(),
            P(),
            P(),
            P(),
            P(),
            P(),
            P(),
            P(),
            P(),
            P(),
            P(),
            P(),
        ),
        check_vma=False,
    )
```

profile of v0, /device:TPU:0, one launch (start us, length us, event | category | flops | bytes accessed | tf_op | source)
XLA Modules:
  0.0 1270.7 jit_solution(5246466175577713890)
XLA Ops:
  9.2 5.9 add_convert_fusion.1
  20.7 2.7 slice.34
  33.2 2.7 copy.79
  35.9 3.9 reshape.229
  39.8 3.0 copy.81
  44.0 196.3 %all-gather.6.cloned.1.call-done = bf16[8,512,1536]{2,1,0:T(8,128)(2,1)} async-done(((bf16[8,128,1536]{2,1,0:T(8,128)(2,1)}), bf16[8,512,1536]{2,1,0:T(8,128)(2,1)}) %all-gather.6.cloned.1.call-update) | async-done | bytes 12582928 | tf_op jit(solution)/shard_map/all_gather | solution.py:123
  240.3 10.3 fusion.80
  250.6 8.6 copy.80
  259.2 8.6 copy.78
  269.4 31.8 %while.26 = (s32[]{:T(128)}, bf16[2,4,128,12,64]{2,4,3,1,0:T(8,128)(2,1)}, f32[2,4,12,128]{3,2,1,0:T(8,128)}, bf16[2,4,512,12,64]{2,4,3,1,0:T(8,128)(2,1)}, s32[...) while((s32[]{:T(128)}, ...), condition=%wide.region_5.6_spmd, body=%wide.region_2.5_spmd.sunk | while | flops 843311104 | bytes 79569176 | solution.py:126
  270.5 4.9 fusion.122
  275.4 3.5 fusion.123
  278.9 4.6 bitcast_dynamic-update-slice_fusion.10
  286.4 4.9 fusion.122
  291.3 3.5 fusion.123
  294.8 4.6 bitcast_dynamic-update-slice_fusion.10
  301.2 3.8 copy.82
  305.0 3.8 convert_element_type.149
  308.8 4.1 fusion.81
  313.6 38.4 %multiply_convert_fusion.1 = (bf16[1024,3072]{1,0:T(8,128)(2,1)S(1)}, f32[1024,3072]{1,0:T(8,128)}, f32[1024,3072]{1,0:T(8,128)}) fusion(f32[3072]{0:T(1024)S(1)} %copy-done.41, bf16[768,3072]{1,0:T(8,128)(2,1)} %param.30, f32[1024,768]{1,0:T(8,128)S(1)} %get-tuple-element.350, f32[768]{0:T(1024)S(1)} %copy-done.36, f32[768]{0:T(1024)S(1)} %copy-done.27, ...), kind=kOutput, calls=%fused_computation.65 | convolution fusion | flops 5043388416 | bytes 39348224 | tf_op jit(solution)/shard_map/dot_general | solution.py:141
  352.1 5.5 fusion.82
  363.9 2.9 fusion.78
  370.5 18.9 %convert_reduce_fusion = (f32[3072]{0:T(1024)}, bf16[1024,3072]{1,0:T(8,128)(2,1)}) fusion(f32[1024,3072]{1,0:T(8,128)} %get-tuple-element.340, bf16[1024,768]{1,0:T(8,128)(2,1)} %get-tuple-element.332, bf16[3072,768]{1,0:T(8,128)(2,1)} %param.32, f32[1024,3072]{1,0:T(8,128)} %get-tuple-element.351, f32[3072]{0:T(1024)S(1)} %copy-done.42), kind=kOutput, calls=%fused_computation.63 | convolution fusion | flops 4885312512 | bytes 37773312 | tf_op jit(solution)/shard_map/td,fd->tf/dot_general | solution.py:172
  389.4 10.6 multiply_reduce_fusion.2
  410.5 3.8 reshape.234
  415.8 79.8 %while.27 = (s32[]{:T(128)}, bf16[2,4,128,12,64]{2,4,3,1,0:T(8,128)(2,1)}, bf16[2,4,512,12,64]{2,4,3,1,0:T(8,128)(2,1)}, bf16[2,4,512,12,64]{2,4,3,1,0:T(8,128)(...) while((s32[]{:T(128)}, ...), condition=%wide.region_16.17_spmd, body=%wide.region_14.16_spmd.sunk | while | flops 2062673920 | bytes 167978256 | solution.py:197
  419.2 4.0 fusion.131
  423.1 4.7 bitcast_dynamic-update-slice_fusion.14
  427.9 9.0 multiply_reduce_fusion.8
  436.9 9.8 multiply_convert_fusion.3
  446.8 6.3 bitcast_dynamic-update-slice_fusion.12
  453.1 2.6 bitcast_dynamic-update-slice_fusion.13
  458.9 4.0 fusion.131
  462.9 4.8 bitcast_dynamic-update-slice_fusion.14
  467.6 9.0 multiply_reduce_fusion.8
  476.7 9.8 multiply_convert_fusion.3
  486.5 6.3 bitcast_dynamic-update-slice_fusion.12
  492.9 2.7 bitcast_dynamic-update-slice_fusion.13
  495.6 13.2 %pad_maximum_fusion = bf16[8,512,1536]{1,2,0:T(8,128)(2,1)} fusion(bf16[8,512,768]{1,2,0:T(8,128)(2,1)} %bitcast.195, bf16[8,512,768]{1,2,0:T(8,128)(2,1)} %bitcast.196), kind=kLoop, calls=%fused_computation.62 | loop fusion | flops 25165824 | bytes 25165824 | tf_op jit(solution)/shard_map/concatenate | solution.py:201
  508.8 17.1 %copy.90 = bf16[8,512,1536]{2,0,1:T(8,128)(2,1)} copy(bf16[8,512,1536]{1,2,0:T(8,128)(2,1)} %pad_maximum_fusion) | data formatting | bytes 25165824
  525.9 12.9 %copy.96 = bf16[64,8,8,1536]{3,1,2,0:T(8,128)(2,1)} copy(bf16[64,8,8,1536]{3,2,1,0:T(8,128)(2,1)} %bitcast.189) | data formatting | bytes 25165824
  539.3 4.8 fusion.83
  544.3 11.1 fusion.72
  555.4 9.9 fusion.84
  565.6 3.8 copy.86
  569.4 3.8 reshape.235
  575.8 173.3 %reduce-scatter.16.cloned.1.call-done = bf16[128,12288]{1,0:T(8,128)(2,1)} async-done(((bf16[512,12288]{1,0:T(8,128)(2,1)}), bf16[128,12288]{1,0:T(8,128)(2,1)}) %reduce-scatter.16.cloned.1.call-update) | async-done | bytes 3145744
  749.1 3.0 copy.97
  754.7 6.2 convolution_bitcast_fusion
  760.9 8.3 copy.92
  769.3 27.2 %reduce-scatter.10.cloned.1.call-done = f32[96,768]{1,0:T(8,128)} async-done(((f32[768,768]{1,0:T(8,128)}), f32[96,768]{1,0:T(8,128)}) %reduce-scatter.10.cloned.1.call-update) | async-done | bytes 294928 | tf_op jit(solution)/shard_map/reduce_scatter | solution.py:244
  798.2 79.2 %reduce-scatter.12.cloned.1.call-done = f32[96,3072]{1,0:T(8,128)} async-done(((f32[768,3072]{1,0:T(8,128)}), f32[96,3072]{1,0:T(8,128)}) %reduce-scatter.12.cloned.1.call-update) | async-done | bytes 1179664 | tf_op jit(solution)/shard_map/reduce_scatter | solution.py:245
  879.5 78.7 %reduce-scatter.14.cloned.1.call-done = f32[384,768]{1,0:T(8,128)} async-done(((f32[3072,768]{1,0:T(8,128)}), f32[384,768]{1,0:T(8,128)}) %reduce-scatter.14.cloned.1.call-update) | async-done | bytes 1179664 | tf_op jit(solution)/shard_map/reduce_scatter | solution.py:246
  960.3 67.2 %reduce-scatter.18.cloned.1.call-done = f32[96,2304]{1,0:T(8,128)} async-done(((f32[768,2304]{1,0:T(8,128)}), f32[96,2304]{1,0:T(8,128)}) %reduce-scatter.18.cloned.1.call-update) | async-done | bytes 884752
  1029.8 83.2 %all-reduce.4.cloned.1.call-done = (bf16[96,2304]{0,1:T(8,128)(2,1)}, bf16[96,768]{1,0:T(8,128)(2,1)}, bf16[96,3072]{1,0:T(8,128)(2,1)}, bf16[384,768]{1,0:T(8,128)(2,1)}) async-done(((bf16[96,2304]{0,1:T(8,128)(2,1)}, bf16[96,768]{1,0:T(8,128)(2,1)}, bf16[96,3072]{1,0:T(8,128)(2,1)}, bf16[384,768]{1,0:T(8,128)(2,1)}), (bf16[96,2304]{0,1:T(8,128)(2,1)}, bf16[96,768]{1,0:T(8,128)(2,1)}, ...) | async-done | bytes 1769488 | tf_op jit(solution)/shard_map/psum | solution.py:249
  1120.9 4.6 fusion.66
  1125.8 41.4 %all-reduce = (f32[2,768]{1,0:T(2,128)}, f32[768]{0:T(1024)}, f32[768]{0:T(1024)}, f32[768]{0:T(1024)}, f32[3072]{0:T(1024)}, /*index=5*/f32[768]{0:T(1024)}, f3...) all-reduce(f32[2,768]{1,0:T(2,128)S(1)} %pad_maximum_fusion.7, ...), channel_id=1, replica_groups=mesh['batch'=8,'blk'=4] {'batch','blk'}, use_global_device_ids=true, to_apply=%region_22.23 | all-reduce | flops 9985 | bytes 79880 | tf_op jit(solution)/shard_map/psum | solution.py:227
  1167.2 8.9 add_add_fusion.4
  1176.1 2.8 convert_element_type.172
  1178.9 5.5 convert_element_type.168
  1184.4 31.3 %all-gather.14.cloned.1.call-done = bf16[3072,768]{1,0:T(8,128)(2,1)} async-done(((bf16[384,768]{1,0:T(8,128)(2,1)}), bf16[3072,768]{1,0:T(8,128)(2,1)}) %all-gather.14.cloned.1.call-update) | async-done | bytes 4718608 | tf_op jit(solution)/shard_map/all_gather | solution.py:264
  1215.8 6.8 convert_element_type.178
  1222.6 34.0 %all-gather.12.cloned.1.call-done = bf16[768,3072]{1,0:T(8,128)(2,1)} async-done(((bf16[96,3072]{1,0:T(8,128)(2,1)}), bf16[768,3072]{1,0:T(8,128)(2,1)}) %all-gather.12.cloned.1.call-update) | async-done | bytes 4718608 | tf_op jit(solution)/shard_map/all_gather | solution.py:261
  1256.6 7.4 convert_element_type.175
  (230 shorter events, 76.4 us)
Async XLA Ops:
  7.2 233.1 %all-gather.6.cloned.1.call-start = ((), (), s32[]{:S(2)}) async-start(), calls=%async_computation.5 | async-start | bytes 15728640 | tf_op jit(solution)/shard_map/all_gather | solution.py:123
  19.2 4.8 copy-start.47
  19.2 5.4 copy-start.48
  19.2 8.6 copy-start.46
  19.2 729.8 %reduce-scatter.16.cloned.1.call-start = ((), (), s32[]{:S(2)}) async-start(), calls=%async_computation.13 | async-start | bytes 15728640
  269.4 9.5 slice-start
  270.5 8.4 slice-start.1
  275.3 3.6 copy-start.12
  278.9 4.6 copy-start.19
  285.3 9.5 slice-start
  286.4 8.4 slice-start.1
  291.2 3.6 copy-start.12
  294.8 4.6 copy-start.19
  301.2 11.7 copy-start.17
  308.8 4.7 copy-start.27
  308.8 4.7 copy-start.36
  308.8 4.7 copy-start.41
  308.8 43.2 %slice-start.2 = ((s8[4718592]{0:T(1024)(128)(4,1)}), s8[4194304]{0:T(1024)(128)(4,1)S(1)}, s32[]{:S(2)}) async-start(s8[4718592]{0:T(1024)(128)(4,1)} %bitcast.203), calls=%async_computation.18 | async-start | bytes 8388608
  312.9 87.0 %copy-start.4 = (f32[1024,768]{1,0:T(8,128)}, f32[1024,768]{1,0:T(8,128)S(1)}, u32[]{:S(2)}) copy-start(f32[1024,768]{1,0:T(8,128)S(1)} %get-tuple-element.350) | copy-start | bytes 9437188
  313.0 87.0 %copy-start.21 = (f32[1024]{0:T(1024)}, f32[1024]{0:T(1024)S(1)}, u32[]{:S(2)}) copy-start(f32[1024]{0:T(1024)S(1)} %broadcast_multiply_fusion.1) | copy-start | bytes 12292
  313.5 86.4 %copy-start.23 = (f32[1024]{0:T(1024)}, f32[1024]{0:T(1024)S(1)}, u32[]{:S(2)}) copy-start(f32[1024]{0:T(1024)S(1)} %fusion.68) | copy-start | bytes 12292
  313.5 38.4 %copy-start.45 = (f32[768]{0:T(1024)S(1)}, f32[768]{0:T(1024)}, u32[]{:S(2)}) copy-start(f32[768]{0:T(1024)} %convert_element_type.156) | copy-start | bytes 9220
  313.6 38.4 %slice-start.3 = ((s8[4718592]{0:T(1024)(128)(4,1)}), s8[524288]{0:T(1024)(128)(4,1)S(1)}, s32[]{:S(2)}) async-start(s8[4718592]{0:T(1024)(128)(4,1)} %bitcast.203), calls=%async_computation.19 | async-start | bytes 1048576
  352.0 5.5 copy-start.51
  352.0 6.1 copy-start.29
  352.0 6.1 copy-start.35
  352.0 6.1 copy-start.40
  357.5 6.3 copy-start.3
  357.5 2.7 copy-start.44
  357.5 4.0 copy-start.5
  357.6 4.0 copy-start.38
  357.6 6.3 copy-start.25
  358.1 8.6 copy-start.31
  361.6 5.2 copy-start.33
  366.7 3.8 copy-start.42
  401.5 3.8 copy-start.50
  407.9 8.0 copy-start.18
  436.9 9.8 copy-start.10
  446.8 6.3 copy-start.1
  446.8 6.3 copy-start.2
  453.1 2.7 copy-start.11
  476.7 9.8 copy-start.10
  486.5 6.3 copy-start.1
  486.5 6.3 copy-start.2
  492.9 2.7 copy-start.11
  538.8 5.4 copy-start.22
  538.9 5.4 copy-start.24
  538.9 5.4 copy-start.28
  538.9 5.4 copy-start.37
  538.9 257.6 %reduce-scatter.10.cloned.1.call-start = ((), (), s32[]{:S(2)}) async-start(), calls=%async_computation.7 | async-start | bytes 2654208 | tf_op jit(solution)/shard_map/reduce_scatter | solution.py:244
  544.2 333.2 %reduce-scatter.12.cloned.1.call-start = ((), (), s32[]{:S(2)}) async-start(), calls=%async_computation.9 | async-start | bytes 10616832 | tf_op jit(solution)/shard_map/reduce_scatter | solution.py:245
  555.4 402.8 %reduce-scatter.14.cloned.1.call-start = ((), (), s32[]{:S(2)}) async-start(), calls=%async_computation.11 | async-start | bytes 10616832 | tf_op jit(solution)/shard_map/reduce_scatter | solution.py:246
  565.4 462.1 %reduce-scatter.18.cloned.1.call-start = ((), (), s32[]{:S(2)}) async-start(), calls=%async_computation.14 | async-start | bytes 7962624
  752.1 2.6 copy-start.15
  769.2 343.8 %all-reduce.4.cloned.1.call-start = ((), (), s32[]{:S(2)}) async-start(), calls=%async_computation.15 | async-start | bytes 3833856 | tf_op jit(solution)/shard_map/psum | solution.py:249
  879.5 238.9 %copy-start.34 = (f32[1024]{0:T(1024)S(1)}, f32[1024]{0:T(1024)}, u32[]{:S(2)}) copy-start(f32[1024]{0:T(1024)} %copy-done.33) | copy-start | bytes 12292
  960.3 160.5 %copy-start.26 = (f32[1024]{0:T(1024)S(1)}, f32[1024]{0:T(1024)}, u32[]{:S(2)}) copy-start(f32[1024]{0:T(1024)} %copy-done.25) | copy-start | bytes 12292
  960.3 160.5 %copy-start.30 = (f32[768]{0:T(1024)S(1)}, f32[768]{0:T(1024)}, u32[]{:S(2)}) copy-start(f32[768]{0:T(1024)} %convert_element_type.157) | copy-start | bytes 9220
  960.3 160.5 %copy-start.32 = (f32[1024]{0:T(1024)S(1)}, f32[1024]{0:T(1024)}, u32[]{:S(2)}) copy-start(f32[1024]{0:T(1024)} %copy-done.31) | copy-start | bytes 12292
  1029.8 146.3 %all-gather.10.cloned.1.call-start = ((), (), s32[]{:S(2)}) async-start(), calls=%async_computation.8 | async-start | bytes 1327104 | tf_op jit(solution)/shard_map/all_gather | solution.py:258
  1113.0 65.9 %all-gather.8.cloned.1.call-start = ((), (), s32[]{:S(2)}) async-start(), calls=%async_computation.6 | async-start | bytes 3981312 | tf_op jit(solution)/shard_map/all_gather | solution.py:255
  1115.2 100.6 %all-gather.14.cloned.1.call-start = ((), (), s32[]{:S(2)}) async-start(), calls=%async_computation.12 | async-start | bytes 5308416 | tf_op jit(solution)/shard_map/all_gather | solution.py:264
  1115.8 140.8 %all-gather.12.cloned.1.call-start = ((), (), s32[]{:S(2)}) async-start(), calls=%async_computation.10 | async-start | bytes 5308416 | tf_op jit(solution)/shard_map/all_gather | solution.py:261
  1116.5 9.0 copy-start.9
  (13 other events, 21.3 us)
Sparse Core Ops, SparseCore 0:
  19.3 220.9 all-gather.5
  539.0 210.0 reduce-scatter.15
  753.0 43.4 reduce-scatter.9
  800.8 76.4 reduce-scatter.11
  881.7 76.4 reduce-scatter.13
  962.0 65.5 reduce-scatter.17
  1031.3 81.6 all-reduce.3
  1114.9 23.4 all-gather.9
  1140.8 34.2 all-gather.7
  1176.8 38.8 all-gather.13
  1217.7 38.9 all-gather.11
where the time goes:
time: 1280 us; the launch traced here: 1270 us
  waiting for transfers between devices  772 us (60%)
  matrix products  206 us (16%)
  local copies, waits for them, and re-layouts  139 us (11%)
  other arithmetic  95.9 us (7%)
  blocking collectives  41.4 us (3%)
  between operations  15.4 us (1%)
    unnamed x13, waiting for transfers between devices  242 us
    all_gather x1, waiting for transfers between devices, per_device(): all_kv = lax.all_gather(key_vals, 'blk', axis=1, tiled=True)  196 us
    psum x1, waiting for transfers between devices, per_device(): lax.psum(shares[0].astype(jnp.bfloat16), 'blk').astype(jnp.float32)  83.2 us
    reduce_scatter x1, waiting for transfers between devices, per_device(): lax.psum_scatter(grad_up_weight, 'batch', scatter_dimension=0, tiled=True)  79.2 us
    reduce_scatter x1, waiting for transfers between devices, per_device(): lax.psum_scatter(grad_down_weight, 'batch', scatter_dimension=0, tiled=True)  78.7 us
    unnamed x98, local copies, waits for them, and re-layouts  53.7 us
    psum x1, blocking collectives, per_device(): lax.psum((grad_qv_bias, grad_out_bias, grad_attn_gain, grad_attn_shift, g...  41.4 us
    dot_general x1, matrix products, per_device(): jnp.dot(normed_low, up_weight, preferred_element_type=jnp.float32)  38.4 us
  transfers between devices with their start and end apart: 11, of which 9 were waited for; matrix products, arithmetic and copies ran while one was open for 9% of the time, Pallas kernels for 0%

commit v1 on v0

v1 whole, which is shorter than its diff:
```python
import jax
import jax.numpy as jnp
from jax import lax
from jax.sharding import PartitionSpec as P

HEADS = 12
HD = 64


epsilon = 1e-06
masked_score = -1e30


def layer_norm(values, norm_gain, norm_shift):
    center = values - jnp.mean(values, axis=-1, keepdims=True)
    variance = jnp.mean(center * center, axis=-1, keepdims=True)
    return center * lax.rsqrt(variance + epsilon) * norm_gain + norm_shift


def norm_backward(values, norm_gain, norm_shift, upstream):
    result, pullback = jax.vjp(layer_norm, values, norm_gain, norm_shift)
    return pullback(upstream)


def gelu_exact(values):
    return jax.nn.gelu(values, approximate=False)


def document_ids(lengths, slot_count):
    passage_ends = jnp.cumsum(lengths, axis=-1)
    slot_index = jnp.arange(slot_count, dtype=jnp.int32)
    return jnp.sum((passage_ends[..., None, :] <= slot_index[:, None]).astype(jnp.int32), axis=-1)


AXES = ("batch", "blk")


def bits_of(count):
    return max(count - 1, 0).bit_length()


def is_power(count):
    return count & (count - 1) == 0


def flat_perm(sizes, partner):
    pairs = []
    for b in range(sizes[0]):
        for z in range(sizes[1]):
            to_b, to_z = partner(b, z)
            pairs.append((b * sizes[1] + z, to_b * sizes[1] + to_z))
    return pairs


def move(array, sizes, partner):
    return lax.ppermute(array, AXES, flat_perm(sizes, partner))


def segment_exchange(blocks, sizes):
    nz = sizes[1]
    return [blocks[0]] + [
        move(blocks[k], sizes, lambda b, z, k=k: (b, (z + k) % nz)) for k in range(1, nz)
    ]


def segment_return(blocks, sizes):
    nz = sizes[1]
    return [blocks[0]] + [
        move(blocks[k], sizes, lambda b, z, k=k: (b, (z - k) % nz)) for k in range(1, nz)
    ]


def to_rows(local, sizes):
    nz = sizes[1]
    z = lax.axis_index("blk")
    parts = local.reshape((nz, local.shape[0] // nz) + local.shape[1:])
    blocks = [lax.dynamic_index_in_dim(parts, (z + k) % nz, 0, False) for k in range(nz)]
    return jnp.stack(segment_exchange(blocks, sizes), axis=1)


def to_segments(rows, sizes):
    nz = sizes[1]
    z = lax.axis_index("blk")
    blocks = segment_return([rows[:, k] for k in range(nz)], sizes)
    out = jnp.zeros((nz,) + blocks[0].shape, rows.dtype)
    for k in range(nz):
        out = lax.dynamic_update_index_in_dim(out, blocks[k], (z + k) % nz, 0)
    return out.reshape((nz * rows.shape[0],) + rows.shape[2:])


def halving_steps(sizes):
    batch_bits, blk_bits = bits_of(sizes[0]), bits_of(sizes[1])
    middle = list(range(1, batch_bits))
    forward = [("b", 0)] if batch_bits else []
    steps = [(step, step) for step in forward]
    steps += [(("b", p), ("b", q)) for p, q in zip(middle, reversed(middle))]
    steps += [(("z", p), ("z", p)) for p in range(blk_bits)]
    return steps


def step_partner(step):
    def partner(b, z):
        axis, bit = step[b & 1]
        return (b ^ (1 << bit), z) if axis == "b" else (b, z ^ (1 << bit))

    return partner


def own_bit(step):
    b, z = lax.axis_index("batch"), lax.axis_index("blk")

    def value(part):
        return ((b if part[0] == "b" else z) >> part[1]) & 1

    return jnp.where(b & 1 == 1, value(step[1]), value(step[0]))


def sum_all(array, sizes):
    steps = halving_steps(sizes)
    part = array.astype(jnp.bfloat16)
    for step in steps:
        bit = own_bit(step)
        halves = part.reshape((2, part.shape[0] // 2) + part.shape[1:])
        keep = lax.dynamic_index_in_dim(halves, bit, 0, False)
        send = lax.dynamic_index_in_dim(halves, 1 - bit, 0, False)
        got = move(send, sizes, step_partner(step))
        part = (keep.astype(jnp.float32) + got.astype(jnp.float32)).astype(jnp.bfloat16)
    for step in reversed(steps):
        bit = own_bit(step)
        got = move(part, sizes, step_partner(step))
        low = jnp.where(bit == 0, part, got)
        high = jnp.where(bit == 0, got, part)
        part = jnp.concatenate([low, high], axis=0)
    return part.astype(jnp.float32)


def sum_small(array, sizes):
    for step in halving_steps(sizes):
        array = array + move(array, sizes, step_partner(step))
    return array


def per_device(
    hidden_in,
    lengths,
    qkv_weight,
    qv_bias,
    out_weight,
    out_bias,
    attn_gain,
    attn_shift,
    up_weight,
    up_bias,
    down_weight,
    down_bias,
    ffn_gain,
    ffn_shift,
    head_weight,
    head_bias,
    hidden_cot,
    term_cot,
):
    row_count, seg_len, model_width = hidden_in.shape
    sizes = (lax.axis_size("batch"), lax.axis_size("blk"))
    nz = sizes[1]
    own_rows = row_count // nz
    slot_count = seg_len * nz
    score_scale = HD ** (-0.5)
    blk_index = lax.axis_index("blk")
    doc_all = document_ids(lengths, slot_count)
    doc_mine = lax.dynamic_slice_in_dim(doc_all, blk_index * own_rows, own_rows, 0)
    doc_mine = doc_mine.reshape(own_rows, nz, seg_len)
    docs = jnp.stack(
        [
            lax.dynamic_index_in_dim(doc_mine, (blk_index - k) % nz, 1, False)
            for k in range(nz)
        ],
        axis=1,
    ).reshape(own_rows, slot_count)
    token_count = own_rows * slot_count
    same_doc = (docs[:, :, None] == docs[:, None, :])[:, None]
    tokens = to_rows(hidden_in, sizes).reshape(token_count, model_width)
    cot = to_rows(hidden_cot, sizes).reshape(token_count, model_width)
    term_cot_rows = to_rows(term_cot, sizes).reshape(token_count)

    bias_query = qv_bias[0].astype(jnp.float32)
    qkv_add = jnp.concatenate(
        [bias_query, jnp.zeros_like(bias_query), qv_bias[1].astype(jnp.float32)]
    )
    projected = (jnp.dot(tokens, qkv_weight, preferred_element_type=jnp.float32) + qkv_add).astype(
        jnp.bfloat16
    )
    heads = projected.reshape(own_rows, slot_count, 3, HEADS, HD)
    queries, keys_part, vals_part = heads[:, :, 0], heads[:, :, 1], heads[:, :, 2]
    scores = (
        jnp.einsum("rqhd,rkhd->rhqk", queries, keys_part, preferred_element_type=jnp.float32)
        * score_scale
    )
    scores = jnp.where(same_doc, scores, masked_score)
    row_max = jnp.max(scores, axis=-1, keepdims=True)
    weights = jnp.exp(scores - row_max)
    row_total = jnp.sum(weights, axis=-1, keepdims=True)
    probs_low = (weights / row_total).astype(jnp.bfloat16)
    mixed = jnp.einsum("rhqk,rkhd->rqhd", probs_low, vals_part, preferred_element_type=jnp.float32)
    attended = mixed.reshape(token_count, model_width).astype(jnp.bfloat16)
    gain_attn = attn_gain.astype(jnp.float32)
    shift_attn = attn_shift.astype(jnp.float32)
    gain_ffn = ffn_gain.astype(jnp.float32)
    shift_ffn = ffn_shift.astype(jnp.float32)
    first_sum = (
        tokens.astype(jnp.float32)
        + jnp.dot(attended, out_weight, preferred_element_type=jnp.float32)
        + out_bias.astype(jnp.float32)
    )
    normed = layer_norm(first_sum, gain_attn, shift_attn)
    normed_low = normed.astype(jnp.bfloat16)
    gate_pre = jnp.dot(normed_low, up_weight, preferred_element_type=jnp.float32) + up_bias.astype(
        jnp.float32
    )
    activated = gelu_exact(gate_pre).astype(jnp.bfloat16)
    second_sum = (
        normed
        + jnp.dot(activated, down_weight, preferred_element_type=jnp.float32)
        + down_bias.astype(jnp.float32)
    )
    final_out = layer_norm(second_sum, gain_ffn, shift_ffn)
    head_vec = head_weight.astype(jnp.float32)
    logits = (
        jnp.dot(final_out, head_vec, precision=lax.Precision.HIGHEST)
        + head_bias.astype(jnp.float32)[0]
    )
    term_weight = jax.nn.softplus(logits)
    term_grad = term_cot_rows * jax.nn.sigmoid(logits)
    grad_head_weight = jnp.dot(term_grad, final_out, precision=lax.Precision.HIGHEST)
    grad_head_bias = jnp.sum(term_grad, keepdims=True)
    final_grad = (
        cot.astype(jnp.float32)
        + term_grad[:, None] * head_vec
    )
    second_grad, grad_ffn_gain, grad_ffn_shift = norm_backward(
        second_sum, gain_ffn, shift_ffn, final_grad
    )
    ffn_grad = second_grad.astype(jnp.bfloat16)
    grad_down_bias = jnp.sum(ffn_grad, axis=0, dtype=jnp.float32)
    grad_down_weight = jnp.einsum(
        "tf,td->fd", activated, ffn_grad, preferred_element_type=jnp.float32
    )
    act_grad = jnp.einsum("td,fd->tf", ffn_grad, down_weight, preferred_element_type=jnp.float32)
    gelu_pull = jax.vjp(gelu_exact, gate_pre)[1]
    gate_grad = gelu_pull(act_grad)[0].astype(jnp.bfloat16)
    grad_up_bias = jnp.sum(gate_grad, axis=0, dtype=jnp.float32)
    grad_up_weight = jnp.einsum(
        "td,tf->df", normed_low, gate_grad, preferred_element_type=jnp.float32
    )
    normed_grad = (
        jnp.einsum("tf,df->td", gate_grad, up_weight, preferred_element_type=jnp.float32)
        + second_grad
    )
    first_grad, grad_attn_gain, grad_attn_shift = norm_backward(
        first_sum, gain_attn, shift_attn, normed_grad
    )
    attn_grad = first_grad.astype(jnp.bfloat16)
    grad_out_bias = jnp.sum(attn_grad, axis=0, dtype=jnp.float32)
    grad_out_weight = jnp.einsum(
        "td,te->de", attended, attn_grad, preferred_element_type=jnp.float32
    )
    mixed_grad = jnp.einsum(
        "te,de->td", attn_grad, out_weight, preferred_element_type=jnp.float32
    ).astype(jnp.bfloat16)
    upstream = mixed_grad.reshape(own_rows, slot_count, HEADS, HD)
    dprobs = jnp.einsum("rqhd,rkhd->rhqk", upstream, vals_part, preferred_element_type=jnp.float32)
    vals_grad = jnp.einsum(
        "rhqk,rqhd->rkhd", probs_low, upstream, preferred_element_type=jnp.float32
    )
    probs = probs_low.astype(jnp.float32)
    inner_sum = jnp.sum(probs * dprobs, axis=-1, keepdims=True)
    score_grad = (probs * (dprobs - inner_sum)).astype(jnp.bfloat16)
    query_grad = (
        jnp.einsum("rhqk,rkhd->rqhd", score_grad, keys_part, preferred_element_type=jnp.float32)
        * score_scale
    )
    key_grad = (
        jnp.einsum("rhqk,rqhd->rkhd", score_grad, queries, preferred_element_type=jnp.float32)
        * score_scale
    )
    proj_grad = (
        jnp.stack([query_grad, key_grad, vals_grad], axis=2)
        .reshape(token_count, 3 * model_width)
        .astype(jnp.bfloat16)
    )
    grad_qv_bias = jnp.stack(
        [
            jnp.sum(proj_grad[:, :model_width], axis=0, dtype=jnp.float32),
            jnp.sum(proj_grad[:, 2 * model_width :], axis=0, dtype=jnp.float32),
        ]
    )
    grad_qkv_weight = jnp.einsum("td,te->de", tokens, proj_grad, preferred_element_type=jnp.float32)
    grad_hidden = (
        jnp.einsum("te,de->td", proj_grad, qkv_weight, preferred_element_type=jnp.float32)
        + first_grad
    )
    vectors = (
        grad_qv_bias,
        grad_out_bias,
        grad_attn_gain,
        grad_attn_shift,
        grad_up_bias,
        grad_down_bias,
        grad_ffn_gain,
        grad_ffn_shift,
        grad_head_weight,
        grad_head_bias,
    )
    packed = jnp.concatenate([v.reshape(-1) for v in vectors])
    packed = jnp.pad(packed, (0, -packed.size % 1024)).reshape(-1, 128)
    packed = sum_small(packed, sizes).reshape(-1)
    summed, offset = [], 0
    for v in vectors:
        summed.append(packed[offset : offset + v.size].reshape(v.shape))
        offset += v.size
    vectors = summed
    matrices = [
        sum_all(g, sizes)
        for g in (grad_down_weight, grad_up_weight, grad_out_weight, grad_qkv_weight)
    ][::-1]
    shape4 = (own_rows, nz, seg_len, model_width)
    return (
        to_segments(final_out.astype(jnp.bfloat16).reshape(shape4), sizes),
        to_segments(term_weight.reshape(shape4[:3]), sizes),
        to_segments(grad_hidden.astype(jnp.bfloat16).reshape(shape4), sizes).astype(jnp.float32),
        matrices[0],
        vectors[0],
        matrices[1],
        vectors[1],
        vectors[2],
        vectors[3],
        matrices[2],
        vectors[4],
        matrices[3],
        vectors[5],
        vectors[6],
        vectors[7],
        vectors[8],
        vectors[9],
    )


def solution(mesh):
    return jax.shard_map(
        per_device,
        mesh=mesh,
        in_specs=(
            P("batch", "blk", None),
            P("batch", None),
            P(),
            P(),
            P(),
            P(),
            P(),
            P(),
            P(),
            P(),
            P(),
            P(),
            P(),
            P(),
            P(),
            P(),
            P("batch", "blk", None),
            P("batch", "blk"),
        ),
        out_specs=(
            P("batch", "blk", None),
            P("batch", "blk"),
            P("batch", "blk", None),
            P(),
            P(),
            P(),
            P(),
            P(),
            P(),
            P(),
            P(),
            P(),
            P(),
            P(),
            P(),
            P(),
            P(),
        ),
        check_vma=False,
    )
```

time: 1280 us -> 637 us (0.50)
  waiting for transfers between devices: 772 us -> 169 us
  starting transfers between devices: 1.24 us -> 87.3 us
  blocking collectives: 41.4 us -> 0 us
  matrix products: 206 us -> 166 us
  local copies, waits for them, and re-layouts: 139 us -> 103 us
    all_gather x5 -> x0, waiting for transfers between devices: 262 us -> none  [the longest x1 196 us: per_device(): all_kv = lax.all_gather(key_vals, 'blk', axis=1, tiled=True)]
    unnamed x13 -> x0, waiting for transfers between devices: 242 us -> none
    reduce_scatter x3 -> x0, waiting for transfers between devices: 185 us -> none  [the longest x1 79.2 us: per_device(): lax.psum_scatter(grad_up_weight, 'batch', scatter_dimension=0, tiled=True)]
    ppermute x0 -> x63, waiting for transfers between devices: none -> 169 us  [move(): return lax.ppermute(array, AXES, flat_perm(sizes, partner))]
    ppermute x0 -> x63, starting transfers between devices: none -> 87.3 us  [move(): return lax.ppermute(array, AXES, flat_perm(sizes, partner))]
    psum x1 -> x0, waiting for transfers between devices: 83.2 us -> none  [per_device(): lax.psum(shares[0].astype(jnp.bfloat16), 'blk').astype(jnp.float32)]
    psum x1 -> x0, blocking collectives: 41.4 us -> none  [per_device(): lax.psum((grad_qv_bias, grad_out_bias, grad_attn_gain, grad_attn_shift, g...]
    dot_general x14 -> x5, matrix products: 72.4 us -> 39.3 us  [the longest x1 13 us: per_device(): jnp.einsum('rqhd,rkhd->rhqk', upstream, vals_part, preferred_element_type...]
  transfers between devices with their start and end apart: 11 -> 63, of which waited for: 9 -> 31; matrix products, arithmetic and copies ran while one was open for 9% -> 31% of each run, Pallas kernels for 0% -> 0%
where the time goes in v1:
time: 637 us; the launch traced here: 628 us
  waiting for transfers between devices  169 us (27%)
  matrix products  166 us (26%)
  local copies, waits for them, and re-layouts  103 us (16%)
  other arithmetic  99.3 us (16%)
  starting transfers between devices  87.3 us (14%)
    ppermute x63, waiting for transfers between devices, move(): return lax.ppermute(array, AXES, flat_perm(sizes, partner))  169 us
    ppermute x63, starting transfers between devices, move(): return lax.ppermute(array, AXES, flat_perm(sizes, partner))  87.3 us
    dot_general x1, matrix products, per_device(): jnp.dot(normed_low, up_weight, preferred_element_type=jnp.float32)  35.1 us
    unnamed x151, local copies, waits for them, and re-layouts  27.8 us
    convert_element_type x1, other arithmetic, per_device(): score_grad = (probs * (dprobs - inner_sum)).astype(jnp.bfloat16)  21.2 us
    dot_general x1, matrix products, per_device(): jnp.einsum('td,fd->tf', ffn_grad, down_weight, preferred_element_type=jnp...  17.2 us
    sub x1, matrix products, per_device(): weights = jnp.exp(scores - row_max)  16.4 us
    convert_element_type x4, other arithmetic, sum_all(): return part.astype(jnp.float32)  14.5 us
  transfers between devices with their start and end apart: 63, of which 31 were waited for; matrix products, arithmetic and copies ran while one was open for 31% of the time, Pallas kernels for 0%

profile of v1, /device:TPU:0, one launch (start us, length us, event | category | flops | bytes accessed | tf_op | source)
XLA Modules:
  0.0 627.7 jit_solution(14276997348633851326)
XLA Ops:
  2.2 5.0 collective-permute-start.14
  7.3 2.5 dynamic-slice_bitcast_fusion.17
  34.2 3.8 collective-permute-start.11
  38.0 3.5 collective-permute-done.12
  41.5 14.3 %collective-permute-start.10 = (bf16[2,128,768]{2,1,0:T(8,128)(2,1)}, bf16[2,128,768]{2,1,0:T(8,128)(2,1)}, u32[]{:S(2)}, u32[]{:S(2)}) collective-permute-start(bf16[2,128,768]{2,1,0:T(8,128)(2,1)} %get-tuple-element.61), channel_id=1, source_target_pairs={{0,2},{1,3},{2,0},{3,1},{4,6},{5,7},{6,4},{7,5},{8,10},{9,11},{10,... | collective-permute-start | bytes 1179656 | tf_op jit(solution)/shard_map/ppermute | solution.py:56
  59.8 5.5 add_convert_fusion.1
  65.3 6.6 %copy.57 = bf16[1024,2304]{0,1:T(8,128)(2,1)} copy(bf16[1024,2304]{1,0:T(8,128)(2,1)} %add_convert_fusion.1) | data formatting | bytes 9437184 | tf_op jit(solution)/shard_map/convert_element_type | solution.py:190
  71.9 8.8 %reshape.311 = bf16[2,512,3,12,64]{1,0,4,3,2:T(2,128)(2,1)} reshape(bf16[1024,2304]{0,1:T(8,128)(2,1)} %copy.57) | data formatting | bytes 9437184 | tf_op jit(solution)/shard_map/reshape | solution.py:193
  80.7 6.4 %fusion.71 = (bf16[2,512,1,12,64]{1,0,4,3,2:T(2,128)(2,1)}, bf16[2,512,1,12,64]{1,0,4,3,2:T(2,128)(2,1)}, bf16[2,512,1,12,64]{1,0,4,3,2:T(2,128)(2,1)}) fusion(bf16[2,512,3,12,64]{1,0,4,3,2:T(2,128)(2,1)} %reshape.311), kind=kLoop, calls=%fused_computation.297 | loop fusion | bytes 9437184 | tf_op jit(solution)/shard_map/slice | solution.py:194
  87.1 16.4 %fusion.73 = (f32[2,12,512]{2,1,0:T(8,128)}, f32[2,12,512,512]{2,3,1,0:T(8,128)}) fusion(pred[2,512,512]{1,2,0:T(8,128)(4,1)} %broadcast_compare_fusion, bf16[2,512,1,12,64]{1,0,4,3,2:T(2,128)(2,1)} %get-tuple-element.45, bf16[2,512,1,12,64]{1,0,4,3,2:T(2,128)(2,1)} %get-tuple-element.46), kind=kOutput, calls=%fused_computation.299 | convolution fusion | flops 830472704 | bytes 28884992 | tf_op jit(solution)/shard_map/sub | solution.py:201
  103.5 10.9 %divide_convert_fusion = bf16[2,12,512,512]{2,3,1,0:T(8,128)(2,1)S(1)} fusion(f32[2,12,512,512]{2,3,1,0:T(8,128)} %get-tuple-element.119, f32[2,12,512]{2,1,0:T(8,128)} %get-tuple-element.118), kind=kLoop, calls=%fused_computation.5 | loop fusion | flops 12582912 | bytes 37797888 | tf_op jit(solution)/shard_map/convert_element_type | solution.py:203
  116.4 2.6 copy-done.1
  124.4 35.1 %multiply_convert_fusion = (bf16[1024,3072]{1,0:T(8,128)(2,1)S(1)}, f32[1024,3072]{1,0:T(8,128)}, f32[1024,3072]{1,0:T(8,128)}) fusion(f32[3072]{0:T(1024)S(1)} %copy-done.47, bf16[768,3072]{1,0:T(8,128)(2,1)S(1)} %bitcast.417, f32[1024,768]{1,0:T(8,128)S(1)} %get-tuple-element.39, f32[768]{0:T(1024)S(1)} %copy-done.48, f32[768]{0:T(1024)S(1)} %convert_element_type.409, ...), kind=kOutput, calls=%fused_computation.13 | convolution fusion | flops 5043388416 | bytes 39348224 | tf_op jit(solution)/shard_map/dot_general | solution.py:217
  159.6 5.4 fusion.74
  169.2 3.4 multiply_reduce_fusion
  172.6 4.0 fusion.68
  179.2 7.0 %convolution_convert_fusion = bf16[3072,768]{1,0:T(8,128)(2,1)} fusion(bf16[1024,3072]{1,0:T(8,128)(2,1)S(1)} %get-tuple-element.36, bf16[1024,768]{1,0:T(8,128)(2,1)S(1)} %get-tuple-element.29), kind=kOutput, calls=%fused_computation.32 | convolution fusion | flops 4834197504 | bytes 12582912 | tf_op jit(solution)/shard_map/tf,td->fd/dot_general | solution.py:245
  186.2 17.2 %convert_reduce_fusion = (f32[3072]{0:T(1024)}, bf16[1024,3072]{1,0:T(8,128)(2,1)}) fusion(f32[1024,3072]{1,0:T(8,128)} %get-tuple-element.37, bf16[1024,768]{1,0:T(8,128)(2,1)} %copy-done.24, bf16[3072,768]{1,0:T(8,128)(2,1)} %param.28, f32[1024,3072]{1,0:T(8,128)} %get-tuple-element.120, f32[3072]{0:T(1024)} %convert_element_type.412), kind=kOutput, calls=%fused_computation.11 | convolution fusion | flops 4885312512 | bytes 37773312 | tf_op jit(solution)/shard_map/td,fd->tf/dot_general | solution.py:248
  203.4 10.7 %multiply_reduce_fusion.1 = (f32[768]{0:T(1024)}, f32[1024]{0:T(1024)S(1)}, f32[768]{0:T(1024)}, f32[1024,768]{1,0:T(8,128)S(1)}) fusion(f32[1024,768]{1,0:T(8,128)S(1)} %get-tuple-element.39, f32[1024]{0:T(1024)S(1)} %fusion.55, f32[1024]{0:T(1024)S(1)} %broadcast_multiply_fusion.1, f32[768]{0:T(1024)S(1)} %copy-done.37, f32[1024,768]{1,0:T(8,128)} %copy-done.9, ...), kind=kOutput, calls=%fused_computation.51 | convolution fusion | flops 4839699456 | bytes 20472832 | tf_op jit(solution)/shard_map/tf,df->td/dot_general | solution.py:256
  214.1 7.8 %convolution_convert_fusion.1 = bf16[768,3072]{1,0:T(8,128)(2,1)} fusion(bf16[1024,3072]{1,0:T(8,128)(2,1)S(1)} %copy-done.56, f32[1024,768]{1,0:T(8,128)S(1)} %get-tuple-element.39, f32[768]{0:T(1024)S(1)} %copy-done.49, f32[768]{0:T(1024)S(1)} %copy-done.37, f32[1024]{0:T(1024)S(1)} %fusion.55, f32[1024]{0:T(1024)S(1)} %broadcast_multiply_fusion.1), kind=kOutput, calls=%fused_computation.33 | convolution fusion | flops 4838129664 | bytes 14170112 | tf_op jit(solution)/shard_map/td,tf->df/dot_general | solution.py:252
  228.9 2.6 convolution_convert_fusion.4
  231.4 2.6 copy.63
  234.0 3.8 reshape.320
  237.9 9.1 %convolution_bitcast_fusion = bf16[2,512,1,12,64]{1,4,3,0,2:T(8,128)(2,1)S(1)} fusion(bf16[2,12,512,512]{2,3,1,0:T(8,128)(2,1)} %copy-done.1, bf16[2,512,12,64]{1,0,3,2:T(2,128)(2,1)} %reshape.320), kind=kOutput, calls=%fused_computation.82 | convolution fusion | flops 805306368 | bytes 15728640 | tf_op jit(solution)/shard_map/rhqk,rqhd->rkhd/dot_general | solution.py:272
  247.0 13.0 %fusion.1 = (f32[2,12,512]{2,1,0:T(8,128)S(1)}, f32[2,12,512,512]{2,3,1,0:T(8,128)}) fusion(bf16[2,12,512,512]{2,3,1,0:T(8,128)(2,1)} %copy-done.1, bf16[2,512,1,12,64]{1,0,4,3,2:T(2,128)(2,1)S(1)} %copy-done.5, bf16[2,512,12,64]{1,0,3,2:T(2,128)(2,1)S(1)} %copy-done.6), kind=kOutput, calls=%fused_computation.3 | convolution fusion | flops 824168448 | bytes 40943616 | tf_op jit(solution)/shard_map/rqhd,rkhd->rhqk/dot_general | solution.py:271
  260.0 21.2 %fusion.2 = bf16[2,12,512,512]{2,3,1,0:T(8,128)(2,1)} fusion(f32[2,12,512,512]{2,3,1,0:T(8,128)} %get-tuple-element.125, f32[2,12,512]{2,1,0:T(8,128)S(1)} %get-tuple-element.124, f32[2,12,512,512]{2,3,1,0:T(8,128)} %get-tuple-element.119, f32[2,12,512]{2,1,0:T(8,128)S(1)} %copy-done.28), kind=kLoop, calls=%fused_computation.4 | loop fusion | flops 37748736 | bytes 63012864 | tf_op jit(solution)/shard_map/convert_element_type | solution.py:277
  281.2 8.6 %multiply_bitcast_fusion = bf16[2,512,1,12,64]{1,4,3,0,2:T(8,128)(2,1)S(1)} fusion(bf16[2,12,512,512]{2,3,1,0:T(8,128)(2,1)} %fusion.2, bf16[2,512,1,12,64]{1,0,4,3,2:T(2,128)(2,1)S(1)} %copy-done.14), kind=kOutput, calls=%fused_computation.56 | convolution fusion | flops 806879232 | bytes 15728640 | tf_op jit(solution)/shard_map/rhqk,rqhd->rkhd/dot_general | solution.py:283
  289.8 6.7 %multiply_bitcast_fusion.1 = bf16[2,512,1,12,64]{1,4,3,0,2:T(8,128)(2,1)S(1)} fusion(bf16[2,12,512,512]{2,3,1,0:T(8,128)(2,1)} %fusion.2, bf16[2,512,1,12,64]{1,0,4,3,2:T(2,128)(2,1)S(1)} %copy-done.10), kind=kOutput, calls=%fused_computation.57 | convolution fusion | flops 806879232 | bytes 15728640 | tf_op jit(solution)/shard_map/rhqk,rkhd->rqhd/dot_general | solution.py:279
  296.5 2.6 maximum_convert_fusion
  299.2 9.4 %copy.69 = bf16[2,512,3,12,64]{1,0,4,3,2:T(2,128)(2,1)} copy(bf16[2,512,3,12,64]{1,4,3,0,2:T(8,128)(2,1)} %maximum_convert_fusion) | data formatting | bytes 9437184 | tf_op jit(solution)/shard_map/convert_element_type | solution.py:289
  308.6 4.0 copy.79
  312.7 4.2 add_convert_fusion.2
  317.4 5.7 convolution_convert_fusion.2
  326.1 2.7 fusion.41
  332.2 3.4 collective-permute-start.8
  358.5 2.8 dynamic-slice_bitcast_fusion.2
  369.5 2.9 collective-permute-start.31
  379.4 15.7 %collective-permute-done.32 = f32[80,128]{1,0:T(8,128)S(1)} collective-permute-done((f32[80,128]{1,0:T(8,128)S(1)}, f32[80,128]{1,0:T(8,128)S(1)}, u32[]{:S(2)}, u32[]{:S(2)}) %collective-permute-start.32) | collective-permute-done | bytes 40992 | tf_op jit(solution)/shard_map/ppermute | solution.py:56
  415.0 16.0 %collective-permute-done.36 = bf16[48,768]{1,0:T(8,128)(2,1)S(1)} collective-permute-done((bf16[48,768]{1,0:T(8,128)(2,1)S(1)}, bf16[48,768]{1,0:T(8,128)(2,1)S(1)}, u32[]{:S(2)}, u32[]{:S(2)}) %collective-permute-start.36) | collective-permute-done | bytes 73760 | tf_op jit(solution)/shard_map/ppermute | solution.py:56
  438.3 2.8 collective-permute-start.38
  441.8 8.8 %collective-permute-done.38 = bf16[24,768]{1,0:T(8,128)(2,1)S(1)} collective-permute-done((bf16[24,768]{1,0:T(8,128)(2,1)S(1)}, bf16[24,768]{1,0:T(8,128)(2,1)S(1)}, u32[]{:S(2)}, u32[]{:S(2)}) %collective-permute-start.38) | collective-permute-done | bytes 36896 | tf_op jit(solution)/shard_map/ppermute | solution.py:56
  451.5 3.5 collective-permute-done.39
  458.8 3.1 collective-permute-done.40
  463.6 3.4 bitcast_convert_fusion
  467.0 6.5 %collective-permute-done.41 = bf16[192,768]{1,0:T(8,128)(2,1)S(1)} collective-permute-done((bf16[192,768]{1,0:T(8,128)(2,1)S(1)}, bf16[192,768]{1,0:T(8,128)(2,1)S(1)}, u32[]{:S(2)}, u32[]{:S(2)}) %collective-permute-start.41) | collective-permute-done | bytes 294944 | tf_op jit(solution)/shard_map/ppermute | solution.py:56
  474.7 2.6 fusion.13
  478.9 5.0 collective-permute-done.20
  485.2 5.3 collective-permute-done.21
  492.9 5.7 collective-permute-done.22
  500.3 4.2 collective-permute-done.23
  504.6 9.2 %collective-permute-done.44 = bf16[192,3072]{1,0:T(8,128)(2,1)S(1)} collective-permute-done((bf16[192,3072]{1,0:T(8,128)(2,1)S(1)}, bf16[192,3072]{1,0:T(8,128)(2,1)S(1)}, u32[]{:S(2)}, u32[]{:S(2)}) %collective-permute-start.44) | collective-permute-done | bytes 1179680 | tf_op jit(solution)/shard_map/ppermute | solution.py:56
  517.5 6.6 %collective-permute-done.45 = bf16[96,3072]{1,0:T(8,128)(2,1)S(1)} collective-permute-done((bf16[96,3072]{1,0:T(8,128)(2,1)S(1)}, bf16[96,3072]{1,0:T(8,128)(2,1)S(1)}, u32[]{:S(2)}, u32[]{:S(2)}) %collective-permute-start.45) | collective-permute-done | bytes 589856 | tf_op jit(solution)/shard_map/ppermute | solution.py:56
  525.2 3.7 collective-permute-done.25
  529.0 2.5 collective-permute-done.46
  531.7 8.2 %collective-permute-start.47 = (bf16[24,3072]{1,0:T(8,128)(2,1)S(1)}, bf16[24,3072]{1,0:T(8,128)(2,1)S(1)}, u32[]{:S(2)}, u32[]{:S(2)}) collective-permute-start(bf16[24,3072]{1,0:T(8,128)(2,1)S(1)} %dynamic-slice_bitcast_fusion.23), channel_id=1, source_target_pairs={{0,2},{1,3},{2,0},{3,1},{4,6},{5,7},{6,4},{7,5},{8,10},{9,11},{10,... | collective-permute-start | bytes 442376 | tf_op jit(solution)/shard_map/ppermute | solution.py:56
  540.1 10.0 %collective-permute-done.47 = bf16[24,3072]{1,0:T(8,128)(2,1)S(1)} collective-permute-done((bf16[24,3072]{1,0:T(8,128)(2,1)S(1)}, bf16[24,3072]{1,0:T(8,128)(2,1)S(1)}, u32[]{:S(2)}, u32[]{:S(2)}) %collective-permute-start.47) | collective-permute-done | bytes 147488 | tf_op jit(solution)/shard_map/ppermute | solution.py:56
  553.2 4.5 collective-permute-done.48
  560.2 4.4 collective-permute-done.49
  568.4 12.7 %collective-permute-done.50 = bf16[96,3072]{1,0:T(8,128)(2,1)S(1)} collective-permute-done((bf16[96,3072]{1,0:T(8,128)(2,1)S(1)}, bf16[96,3072]{1,0:T(8,128)(2,1)S(1)}, u32[]{:S(2)}, u32[]{:S(2)}) %collective-permute-start.50) | collective-permute-done | bytes 589856 | tf_op jit(solution)/shard_map/ppermute | solution.py:56
  583.1 10.5 %collective-permute-done.60 = bf16[384,768]{1,0:T(8,128)(2,1)S(1)} collective-permute-done((bf16[384,768]{1,0:T(8,128)(2,1)S(1)}, bf16[384,768]{1,0:T(8,128)(2,1)S(1)}, u32[]{:S(2)}, u32[]{:S(2)}) %collective-permute-start.60) | collective-permute-done | bytes 589856 | tf_op jit(solution)/shard_map/ppermute | solution.py:56
  600.3 10.0 %collective-permute-done.61 = bf16[768,768]{1,0:T(8,128)(2,1)S(1)} collective-permute-done((bf16[768,768]{1,0:T(8,128)(2,1)S(1)}, bf16[768,768]{1,0:T(8,128)(2,1)S(1)}, u32[]{:S(2)}, u32[]{:S(2)}) %collective-permute-start.61) | collective-permute-done | bytes 1179680 | tf_op jit(solution)/shard_map/ppermute | solution.py:56
  611.7 3.5 maximum_convert_fusion.3
  616.7 5.0 maximum_convert_fusion.1
  622.7 4.5 maximum_convert_fusion.2
  (406 shorter events, 164.4 us)
Async XLA Ops:
  2.2 26.8 %collective-permute-start.14 = (f32[2,128]{1,0:T(2,128)}, f32[2,128]{1,0:T(2,128)}, u32[]{:S(2)}, u32[]{:S(2)}) collective-permute-start(f32[2,128]{1,0:T(2,128)} %get-tuple-element.107), channel_id=1, source_target_pairs={{0,3},{1,0},{2,1},{3,2},{4,7},{5,4},{6,5},{7,6},{8,11},{9,8},{10,9... | collective-permute-start | bytes 3080 | tf_op jit(solution)/shard_map/ppermute | solution.py:56
  7.3 26.9 %collective-permute-start.13 = (f32[2,128]{1,0:T(2,128)}, f32[2,128]{1,0:T(2,128)}, u32[]{:S(2)}, u32[]{:S(2)}) collective-permute-start(f32[2,128]{1,0:T(2,128)} %get-tuple-element.108), channel_id=1, source_target_pairs={{0,2},{1,3},{2,0},{3,1},{4,6},{5,7},{6,4},{7,5},{8,10},{9,11},{10,... | collective-permute-start | bytes 3080 | tf_op jit(solution)/shard_map/ppermute | solution.py:56
  9.8 47.3 %collective-permute-start.2 = (bf16[2,128,768]{2,1,0:T(8,128)(2,1)}, bf16[2,128,768]{2,1,0:T(8,128)(2,1)}, u32[]{:S(2)}, u32[]{:S(2)}) collective-permute-start(bf16[2,128,768]{2,1,0:T(8,128)(2,1)} %get-tuple-element.67), channel_id=1, source_target_pairs={{0,3},{1,0},{2,1},{3,2},{4,7},{5,4},{6,5},{7,6},{8,11},{9,8},{10,9... | collective-permute-start | bytes 1179656 | tf_op jit(solution)/shard_map/ppermute | solution.py:56
  10.2 46.9 %collective-permute-start.1 = (bf16[2,128,768]{2,1,0:T(8,128)(2,1)}, bf16[2,128,768]{2,1,0:T(8,128)(2,1)}, u32[]{:S(2)}, u32[]{:S(2)}) collective-permute-start(bf16[2,128,768]{2,1,0:T(8,128)(2,1)} %get-tuple-element.68), channel_id=1, source_target_pairs={{0,2},{1,3},{2,0},{3,1},{4,6},{5,7},{6,4},{7,5},{8,10},{9,11},{10,... | collective-permute-start | bytes 1179656 | tf_op jit(solution)/shard_map/ppermute | solution.py:56
  12.7 44.4 %collective-permute-start = (bf16[2,128,768]{2,1,0:T(8,128)(2,1)}, bf16[2,128,768]{2,1,0:T(8,128)(2,1)}, u32[]{:S(2)}, u32[]{:S(2)}) collective-permute-start(bf16[2,128,768]{2,1,0:T(8,128)(2,1)} %get-tuple-element.69), channel_id=1, source_target_pairs={{0,1},{1,2},{2,3},{3,0},{4,5},{5,6},{6,7},{7,4},{8,9},{9,10},{10,1... | collective-permute-start | bytes 1179656 | tf_op jit(solution)/shard_map/ppermute | solution.py:56
  26.5 133.0 %copy-start.36 = (f32[768]{0:T(1024)}, f32[768]{0:T(1024)S(1)}, u32[]{:S(2)}) copy-start(f32[768]{0:T(1024)S(1)} %convert_element_type.409) | copy-start | bytes 9220
  29.1 12.4 %collective-permute-start.12 = (f32[2,128]{1,0:T(2,128)}, f32[2,128]{1,0:T(2,128)}, u32[]{:S(2)}, u32[]{:S(2)}) collective-permute-start(f32[2,128]{1,0:T(2,128)} %get-tuple-element.109), channel_id=1, source_target_pairs={{0,1},{1,2},{2,3},{3,0},{4,5},{5,6},{6,7},{7,4},{8,9},{9,10},{10,1... | collective-permute-start | bytes 3080 | tf_op jit(solution)/shard_map/ppermute | solution.py:56
  34.2 135.0 %collective-permute-start.11 = (bf16[2,128,768]{2,1,0:T(8,128)(2,1)}, bf16[2,128,768]{2,1,0:T(8,128)(2,1)}, u32[]{:S(2)}, u32[]{:S(2)}) collective-permute-start(bf16[2,128,768]{2,1,0:T(8,128)(2,1)} %get-tuple-element.60), channel_id=1, source_target_pairs={{0,3},{1,0},{2,1},{3,2},{4,7},{5,4},{6,5},{7,6},{8,11},{9,8},{10,9... | collective-permute-start | bytes 1179656 | tf_op jit(solution)/shard_map/ppermute | solution.py:56
  41.5 127.7 %collective-permute-start.10 = (bf16[2,128,768]{2,1,0:T(8,128)(2,1)}, bf16[2,128,768]{2,1,0:T(8,128)(2,1)}, u32[]{:S(2)}, u32[]{:S(2)}) collective-permute-start(bf16[2,128,768]{2,1,0:T(8,128)(2,1)} %get-tuple-element.61), channel_id=1, source_target_pairs={{0,2},{1,3},{2,0},{3,1},{4,6},{5,7},{6,4},{7,5},{8,10},{9,11},{10,... | collective-permute-start | bytes 1179656 | tf_op jit(solution)/shard_map/ppermute | solution.py:56
  57.1 112.1 %collective-permute-start.9 = (bf16[2,128,768]{2,1,0:T(8,128)(2,1)}, bf16[2,128,768]{2,1,0:T(8,128)(2,1)}, u32[]{:S(2)}, u32[]{:S(2)}) collective-permute-start(bf16[2,128,768]{2,1,0:T(8,128)(2,1)} %get-tuple-element.62), channel_id=1, source_target_pairs={{0,1},{1,2},{2,3},{3,0},{4,5},{5,6},{6,7},{7,4},{8,9},{9,10},{10,1... | collective-permute-start | bytes 1179656 | tf_op jit(solution)/shard_map/ppermute | solution.py:56
  331.2 38.3 %collective-permute-start.7 = (f32[2,128]{1,0:T(2,128)}, f32[2,128]{1,0:T(2,128)}, u32[]{:S(2)}, u32[]{:S(2)}) collective-permute-start(f32[2,128]{1,0:T(2,128)} %bitcast.28), channel_id=1, source_target_pairs={{0,2},{1,3},{2,0},{3,1},{4,6},{5,7},{6,4},{7,5},{8,10},{9,11},{10,... | collective-permute-start | bytes 3080 | tf_op jit(solution)/shard_map/ppermute | solution.py:56
  332.2 44.8 %collective-permute-start.8 = (f32[2,128]{1,0:T(2,128)}, f32[2,128]{1,0:T(2,128)}, u32[]{:S(2)}, u32[]{:S(2)}) collective-permute-start(f32[2,128]{1,0:T(2,128)} %bitcast.30), channel_id=1, source_target_pairs={{0,1},{1,2},{2,3},{3,0},{4,5},{5,6},{6,7},{7,4},{8,9},{9,10},{10,1... | collective-permute-start | bytes 3080 | tf_op jit(solution)/shard_map/ppermute | solution.py:56
  335.6 29.8 %collective-permute-start.6 = (f32[2,128]{1,0:T(2,128)}, f32[2,128]{1,0:T(2,128)}, u32[]{:S(2)}, u32[]{:S(2)}) collective-permute-start(f32[2,128]{1,0:T(2,128)} %bitcast.26), channel_id=1, source_target_pairs={{0,3},{1,0},{2,1},{3,2},{4,7},{5,4},{6,5},{7,6},{8,11},{9,8},{10,9... | collective-permute-start | bytes 3080 | tf_op jit(solution)/shard_map/ppermute | solution.py:56
  336.0 76.5 %collective-permute-start.5 = (bf16[2,128,768]{2,1,0:T(8,128)(2,1)}, bf16[2,128,768]{2,1,0:T(8,128)(2,1)}, u32[]{:S(2)}, u32[]{:S(2)}) collective-permute-start(bf16[2,128,768]{2,1,0:T(8,128)(2,1)} %get-tuple-element.63), channel_id=1, source_target_pairs={{0,1},{1,2},{2,3},{3,0},{4,5},{5,6},{6,7},{7,4},{8,9},{9,10},{10,1... | collective-permute-start | bytes 1179656 | tf_op jit(solution)/shard_map/ppermute | solution.py:56
  358.5 2.8 collective-permute-start.28
  361.4 4.1 collective-permute-start.29
  365.4 40.3 %collective-permute-start.4 = (bf16[2,128,768]{2,1,0:T(8,128)(2,1)}, bf16[2,128,768]{2,1,0:T(8,128)(2,1)}, u32[]{:S(2)}, u32[]{:S(2)}) collective-permute-start(bf16[2,128,768]{2,1,0:T(8,128)(2,1)} %get-tuple-element.64), channel_id=1, source_target_pairs={{0,2},{1,3},{2,0},{3,1},{4,6},{5,7},{6,4},{7,5},{8,10},{9,11},{10,... | collective-permute-start | bytes 1179656 | tf_op jit(solution)/shard_map/ppermute | solution.py:56
  365.4 4.1 collective-permute-start.30
  369.5 26.3 %collective-permute-start.33 = (bf16[384,768]{1,0:T(8,128)(2,1)S(1)}, bf16[384,768]{1,0:T(8,128)(2,1)S(1)}, u32[]{:S(2)}, u32[]{:S(2)}) collective-permute-start(bf16[384,768]{1,0:T(8,128)(2,1)S(1)} %dynamic-slice_bitcast_fusion.8), channel_id=1, source_target_pairs={{0,4},{1,5},{2,6},{3,7},{4,0},{5,1},{6,2},{7,3},{8,12},{9,13},{10,... | collective-permute-start | bytes 1769480 | tf_op jit(solution)/shard_map/ppermute | solution.py:56
  369.5 5.2 collective-permute-start.31
  374.7 26.1 %collective-permute-start.3 = (bf16[2,128,768]{2,1,0:T(8,128)(2,1)}, bf16[2,128,768]{2,1,0:T(8,128)(2,1)}, u32[]{:S(2)}, u32[]{:S(2)}) collective-permute-start(bf16[2,128,768]{2,1,0:T(8,128)(2,1)} %get-tuple-element.65), channel_id=1, source_target_pairs={{0,3},{1,0},{2,1},{3,2},{4,7},{5,4},{6,5},{7,6},{8,11},{9,8},{10,9... | collective-permute-start | bytes 1179656 | tf_op jit(solution)/shard_map/ppermute | solution.py:56
  377.0 18.2 %collective-permute-start.32 = (f32[80,128]{1,0:T(8,128)S(1)}, f32[80,128]{1,0:T(8,128)S(1)}, u32[]{:S(2)}, u32[]{:S(2)}) collective-permute-start(f32[80,128]{1,0:T(8,128)S(1)} %add.440), channel_id=1, source_target_pairs={{0,2},{1,3},{2,0},{3,1},{4,6},{5,7},{6,4},{7,5},{8,10},{9,11},{10,... | collective-permute-start | bytes 122888 | tf_op jit(solution)/shard_map/ppermute | solution.py:56
  395.2 79.5 %collective-permute-start.53 = (bf16[1536,768]{1,0:T(8,128)(2,1)}, bf16[1536,768]{1,0:T(8,128)(2,1)}, u32[]{:S(2)}, u32[]{:S(2)}) collective-permute-start(bf16[1536,768]{1,0:T(8,128)(2,1)} %dynamic-slice_bitcast_fusion), channel_id=1, source_target_pairs={{0,4},{1,5},{2,6},{3,7},{4,0},{5,1},{6,2},{7,3},{8,12},{9,13},{10,... | collective-permute-start | bytes 7077896 | tf_op jit(solution)/shard_map/ppermute | solution.py:56
  397.5 7.0 %collective-permute-start.34 = (bf16[192,768]{1,0:T(8,128)(2,1)}, bf16[192,768]{1,0:T(8,128)(2,1)}, u32[]{:S(2)}, u32[]{:S(2)}) collective-permute-start(bf16[192,768]{1,0:T(8,128)(2,1)} %dynamic-slice_bitcast_fusion.20), channel_id=1, source_target_pairs={{0,8},{1,9},{2,10},{3,11},{4,20},{5,21},{6,22},{7,23},{8,0},{9,1},... | collective-permute-start | bytes 884744 | tf_op jit(solution)/shard_map/ppermute | solution.py:56
  400.8 83.4 %collective-permute-start.43 = (bf16[384,3072]{1,0:T(8,128)(2,1)}, bf16[384,3072]{1,0:T(8,128)(2,1)S(1)}, u32[]{:S(2)}, u32[]{:S(2)}) collective-permute-start(bf16[384,3072]{1,0:T(8,128)(2,1)} %dynamic-slice_bitcast_fusion.1), channel_id=1, source_target_pairs={{0,4},{1,5},{2,6},{3,7},{4,0},{5,1},{6,2},{7,3},{8,12},{9,13},{10,... | collective-permute-start | bytes 7077896 | tf_op jit(solution)/shard_map/ppermute | solution.py:56
  404.6 33.7 %collective-permute-start.16 = (bf16[2,128,768]{2,1,0:T(8,128)(2,1)}, bf16[2,128,768]{2,1,0:T(8,128)(2,1)S(1)}, u32[]{:S(2)}, u32[]{:S(2)}) collective-permute-start(bf16[2,128,768]{2,1,0:T(8,128)(2,1)} %get-tuple-element.57), channel_id=1, source_target_pairs={{0,2},{1,3},{2,0},{3,1},{4,6},{5,7},{6,4},{7,5},{8,10},{9,11},{10,... | collective-permute-start | bytes 1179656 | tf_op jit(solution)/shard_map/ppermute | solution.py:56
  405.8 5.2 collective-permute-start.35
  411.0 20.0 %collective-permute-start.15 = (bf16[2,128,768]{2,1,0:T(8,128)(2,1)}, bf16[2,128,768]{2,1,0:T(8,128)(2,1)S(1)}, u32[]{:S(2)}, u32[]{:S(2)}) collective-permute-start(bf16[2,128,768]{2,1,0:T(8,128)(2,1)} %get-tuple-element.58), channel_id=1, source_target_pairs={{0,3},{1,0},{2,1},{3,2},{4,7},{5,4},{6,5},{7,6},{8,11},{9,8},{10,9... | collective-permute-start | bytes 1179656 | tf_op jit(solution)/shard_map/ppermute | solution.py:56
  412.6 18.4 %collective-permute-start.36 = (bf16[48,768]{1,0:T(8,128)(2,1)S(1)}, bf16[48,768]{1,0:T(8,128)(2,1)S(1)}, u32[]{:S(2)}, u32[]{:S(2)}) collective-permute-start(bf16[48,768]{1,0:T(8,128)(2,1)S(1)} %dynamic-slice_bitcast_fusion.26), channel_id=1, source_target_pairs={{0,1},{1,0},{2,3},{3,2},{4,5},{5,4},{6,7},{7,6},{8,9},{9,8},{10,11... | collective-permute-start | bytes 221192 | tf_op jit(solution)/shard_map/ppermute | solution.py:56
  431.0 25.8 %collective-permute-start.18 = (bf16[384,2304]{1,0:T(8,128)(2,1)S(1)}, bf16[384,2304]{1,0:T(8,128)(2,1)S(1)}, u32[]{:S(2)}, u32[]{:S(2)}) collective-permute-start(bf16[384,2304]{1,0:T(8,128)(2,1)S(1)} %copy-done.17), channel_id=1, source_target_pairs={{0,4},{1,5},{2,6},{3,7},{4,0},{5,1},{6,2},{7,3},{8,12},{9,13},{10,... | collective-permute-start | bytes 5308424 | tf_op jit(solution)/shard_map/ppermute | solution.py:56
  431.0 4.9 collective-permute-start.37
  435.9 14.8 %collective-permute-start.17 = (bf16[2,128,768]{2,1,0:T(8,128)(2,1)S(1)}, bf16[2,128,768]{2,1,0:T(8,128)(2,1)S(1)}, u32[]{:S(2)}, u32[]{:S(2)}) collective-permute-start(bf16[2,128,768]{2,1,0:T(8,128)(2,1)S(1)} %copy-done.26), channel_id=1, source_target_pairs={{0,1},{1,2},{2,3},{3,0},{4,5},{5,6},{6,7},{7,4},{8,9},{9,10},{10,1... | collective-permute-start | bytes 1179656 | tf_op jit(solution)/shard_map/ppermute | solution.py:56
  438.3 12.3 %collective-permute-start.38 = (bf16[24,768]{1,0:T(8,128)(2,1)S(1)}, bf16[24,768]{1,0:T(8,128)(2,1)S(1)}, u32[]{:S(2)}, u32[]{:S(2)}) collective-permute-start(bf16[24,768]{1,0:T(8,128)(2,1)S(1)} %fusion.54), channel_id=1, source_target_pairs={{0,2},{1,3},{2,0},{3,1},{4,6},{5,7},{6,4},{7,5},{8,10},{9,11},{10,... | collective-permute-start | bytes 110600 | tf_op jit(solution)/shard_map/ppermute | solution.py:56
  450.6 4.4 collective-permute-start.39
  455.1 6.8 %collective-permute-start.40 = (bf16[96,768]{1,0:T(8,128)(2,1)S(1)}, bf16[96,768]{1,0:T(8,128)(2,1)S(1)}, u32[]{:S(2)}, u32[]{:S(2)}) collective-permute-start(bf16[96,768]{1,0:T(8,128)(2,1)S(1)} %pad_maximum_fusion.16), channel_id=1, source_target_pairs={{0,16},{1,17},{2,18},{3,19},{4,12},{5,13},{6,14},{7,15},{8,24},{9,... | collective-permute-start | bytes 442376 | tf_op jit(solution)/shard_map/ppermute | solution.py:56
  457.3 16.5 %collective-permute-start.19 = (bf16[192,2304]{1,0:T(8,128)(2,1)S(1)}, bf16[192,2304]{1,0:T(8,128)(2,1)S(1)}, u32[]{:S(2)}, u32[]{:S(2)}) collective-permute-start(bf16[192,2304]{1,0:T(8,128)(2,1)S(1)} %dynamic-slice_bitcast_fusion.5), channel_id=1, source_target_pairs={{0,8},{1,9},{2,10},{3,11},{4,20},{5,21},{6,22},{7,23},{8,0},{9,1},... | collective-permute-start | bytes 2654216 | tf_op jit(solution)/shard_map/ppermute | solution.py:56
  462.0 11.5 %collective-permute-start.41 = (bf16[192,768]{1,0:T(8,128)(2,1)S(1)}, bf16[192,768]{1,0:T(8,128)(2,1)S(1)}, u32[]{:S(2)}, u32[]{:S(2)}) collective-permute-start(bf16[192,768]{1,0:T(8,128)(2,1)S(1)} %pad_maximum_fusion.12), channel_id=1, source_target_pairs={{0,8},{1,9},{2,10},{3,11},{4,20},{5,21},{6,22},{7,23},{8,0},{9,1},... | collective-permute-start | bytes 884744 | tf_op jit(solution)/shard_map/ppermute | solution.py:56
  473.7 124.8 %collective-permute-start.42 = (bf16[384,768]{1,0:T(8,128)(2,1)S(1)}, bf16[384,768]{1,0:T(8,128)(2,1)S(1)}, u32[]{:S(2)}, u32[]{:S(2)}) collective-permute-start(bf16[384,768]{1,0:T(8,128)(2,1)S(1)} %pad_maximum_fusion.8), channel_id=1, source_target_pairs={{0,4},{1,5},{2,6},{3,7},{4,0},{5,1},{6,2},{7,3},{8,12},{9,13},{10,... | collective-permute-start | bytes 1769480 | tf_op jit(solution)/shard_map/ppermute | solution.py:56
  474.1 9.8 %collective-permute-start.20 = (bf16[96,2304]{1,0:T(8,128)(2,1)S(1)}, bf16[96,2304]{1,0:T(8,128)(2,1)S(1)}, u32[]{:S(2)}, u32[]{:S(2)}) collective-permute-start(bf16[96,2304]{1,0:T(8,128)(2,1)S(1)} %dynamic-slice_bitcast_fusion.9), channel_id=1, source_target_pairs={{0,16},{1,17},{2,18},{3,19},{4,12},{5,13},{6,14},{7,15},{8,24},{9,... | collective-permute-start | bytes 1327112 | tf_op jit(solution)/shard_map/ppermute | solution.py:56
  477.4 21.3 %collective-permute-start.54 = (bf16[768,768]{1,0:T(8,128)(2,1)S(1)}, bf16[768,768]{1,0:T(8,128)(2,1)S(1)}, u32[]{:S(2)}, u32[]{:S(2)}) collective-permute-start(bf16[768,768]{1,0:T(8,128)(2,1)S(1)} %dynamic-slice_bitcast_fusion.3), channel_id=1, source_target_pairs={{0,8},{1,9},{2,10},{3,11},{4,20},{5,21},{6,22},{7,23},{8,0},{9,1},... | collective-permute-start | bytes 3538952 | tf_op jit(solution)/shard_map/ppermute | solution.py:56
  484.0 6.4 %collective-permute-start.21 = (bf16[48,2304]{1,0:T(8,128)(2,1)S(1)}, bf16[48,2304]{1,0:T(8,128)(2,1)S(1)}, u32[]{:S(2)}, u32[]{:S(2)}) collective-permute-start(bf16[48,2304]{1,0:T(8,128)(2,1)S(1)} %dynamic-slice_bitcast_fusion.21), channel_id=1, source_target_pairs={{0,1},{1,0},{2,3},{3,2},{4,5},{5,4},{6,7},{7,6},{8,9},{9,8},{10,11... | collective-permute-start | bytes 663560 | tf_op jit(solution)/shard_map/ppermute | solution.py:56
  490.6 8.0 %collective-permute-start.22 = (bf16[24,2304]{1,0:T(8,128)(2,1)S(1)}, bf16[24,2304]{1,0:T(8,128)(2,1)S(1)}, u32[]{:S(2)}, u32[]{:S(2)}) collective-permute-start(bf16[24,2304]{1,0:T(8,128)(2,1)S(1)} %dynamic-slice_bitcast_fusion.25), channel_id=1, source_target_pairs={{0,2},{1,3},{2,0},{3,1},{4,6},{5,7},{6,4},{7,5},{8,10},{9,11},{10,... | collective-permute-start | bytes 331784 | tf_op jit(solution)/shard_map/ppermute | solution.py:56
  491.1 22.6 %collective-permute-start.44 = (bf16[192,3072]{1,0:T(8,128)(2,1)S(1)}, bf16[192,3072]{1,0:T(8,128)(2,1)S(1)}, u32[]{:S(2)}, u32[]{:S(2)}) collective-permute-start(bf16[192,3072]{1,0:T(8,128)(2,1)S(1)} %dynamic-slice_bitcast_fusion.4), channel_id=1, source_target_pairs={{0,8},{1,9},{2,10},{3,11},{4,20},{5,21},{6,22},{7,23},{8,0},{9,1},... | collective-permute-start | bytes 3538952 | tf_op jit(solution)/shard_map/ppermute | solution.py:56
  498.6 5.8 collective-permute-start.23
  499.0 17.4 %collective-permute-start.55 = (bf16[384,768]{1,0:T(8,128)(2,1)S(1)}, bf16[384,768]{1,0:T(8,128)(2,1)S(1)}, u32[]{:S(2)}, u32[]{:S(2)}) collective-permute-start(bf16[384,768]{1,0:T(8,128)(2,1)S(1)} %dynamic-slice_bitcast_fusion.6), channel_id=1, source_target_pairs={{0,16},{1,17},{2,18},{3,19},{4,12},{5,13},{6,14},{7,15},{8,24},{9,... | collective-permute-start | bytes 1769480 | tf_op jit(solution)/shard_map/ppermute | solution.py:56
  504.5 10.1 %collective-permute-start.24 = (bf16[48,2304]{1,0:T(8,128)(2,1)S(1)}, bf16[48,2304]{1,0:T(8,128)(2,1)S(1)}, u32[]{:S(2)}, u32[]{:S(2)}) collective-permute-start(bf16[48,2304]{1,0:T(8,128)(2,1)S(1)} %pad_maximum_fusion.15), channel_id=1, source_target_pairs={{0,1},{1,0},{2,3},{3,2},{4,5},{5,4},{6,7},{7,6},{8,9},{9,8},{10,11... | collective-permute-start | bytes 663560 | tf_op jit(solution)/shard_map/ppermute | solution.py:56
  514.2 9.9 %collective-permute-start.45 = (bf16[96,3072]{1,0:T(8,128)(2,1)S(1)}, bf16[96,3072]{1,0:T(8,128)(2,1)S(1)}, u32[]{:S(2)}, u32[]{:S(2)}) collective-permute-start(bf16[96,3072]{1,0:T(8,128)(2,1)S(1)} %dynamic-slice_bitcast_fusion.7), channel_id=1, source_target_pairs={{0,16},{1,17},{2,18},{3,19},{4,12},{5,13},{6,14},{7,15},{8,24},{9,... | collective-permute-start | bytes 1769480 | tf_op jit(solution)/shard_map/ppermute | solution.py:56
  514.7 14.2 %collective-permute-start.25 = (bf16[96,2304]{1,0:T(8,128)(2,1)S(1)}, bf16[96,2304]{1,0:T(8,128)(2,1)S(1)}, u32[]{:S(2)}, u32[]{:S(2)}) collective-permute-start(bf16[96,2304]{1,0:T(8,128)(2,1)S(1)} %pad_maximum_fusion.11), channel_id=1, source_target_pairs={{0,16},{1,17},{2,18},{3,19},{4,12},{5,13},{6,14},{7,15},{8,24},{9,... | collective-permute-start | bytes 1327112 | tf_op jit(solution)/shard_map/ppermute | solution.py:56
  516.7 23.2 %collective-permute-start.56 = (bf16[192,768]{1,0:T(8,128)(2,1)S(1)}, bf16[192,768]{1,0:T(8,128)(2,1)S(1)}, u32[]{:S(2)}, u32[]{:S(2)}) collective-permute-start(bf16[192,768]{1,0:T(8,128)(2,1)S(1)} %dynamic-slice_bitcast_fusion.18), channel_id=1, source_target_pairs={{0,1},{1,0},{2,3},{3,2},{4,5},{5,4},{6,7},{7,6},{8,9},{9,8},{10,11... | collective-permute-start | bytes 884744 | tf_op jit(solution)/shard_map/ppermute | solution.py:56
  524.3 7.2 %collective-permute-start.46 = (bf16[48,3072]{1,0:T(8,128)(2,1)S(1)}, bf16[48,3072]{1,0:T(8,128)(2,1)S(1)}, u32[]{:S(2)}, u32[]{:S(2)}) collective-permute-start(bf16[48,3072]{1,0:T(8,128)(2,1)S(1)} %dynamic-slice_bitcast_fusion.19), channel_id=1, source_target_pairs={{0,1},{1,0},{2,3},{3,2},{4,5},{5,4},{6,7},{7,6},{8,9},{9,8},{10,11... | collective-permute-start | bytes 884744 | tf_op jit(solution)/shard_map/ppermute | solution.py:56
  531.7 18.4 %collective-permute-start.47 = (bf16[24,3072]{1,0:T(8,128)(2,1)S(1)}, bf16[24,3072]{1,0:T(8,128)(2,1)S(1)}, u32[]{:S(2)}, u32[]{:S(2)}) collective-permute-start(bf16[24,3072]{1,0:T(8,128)(2,1)S(1)} %dynamic-slice_bitcast_fusion.23), channel_id=1, source_target_pairs={{0,2},{1,3},{2,0},{3,1},{4,6},{5,7},{6,4},{7,5},{8,10},{9,11},{10,... | collective-permute-start | bytes 442376 | tf_op jit(solution)/shard_map/ppermute | solution.py:56
  540.0 11.9 %collective-permute-start.57 = (bf16[96,768]{1,0:T(8,128)(2,1)S(1)}, bf16[96,768]{1,0:T(8,128)(2,1)S(1)}, u32[]{:S(2)}, u32[]{:S(2)}) collective-permute-start(bf16[96,768]{1,0:T(8,128)(2,1)S(1)} %dynamic-slice_bitcast_fusion.22), channel_id=1, source_target_pairs={{0,2},{1,3},{2,0},{3,1},{4,6},{5,7},{6,4},{7,5},{8,10},{9,11},{10,... | collective-permute-start | bytes 442376 | tf_op jit(solution)/shard_map/ppermute | solution.py:56
  550.1 7.6 %collective-permute-start.48 = (bf16[24,3072]{1,0:T(8,128)(2,1)S(1)}, bf16[24,3072]{1,0:T(8,128)(2,1)S(1)}, u32[]{:S(2)}, u32[]{:S(2)}) collective-permute-start(bf16[24,3072]{1,0:T(8,128)(2,1)S(1)} %fusion.50), channel_id=1, source_target_pairs={{0,2},{1,3},{2,0},{3,1},{4,6},{5,7},{6,4},{7,5},{8,10},{9,11},{10,... | collective-permute-start | bytes 442376 | tf_op jit(solution)/shard_map/ppermute | solution.py:56
  552.0 8.1 %collective-permute-start.58 = (bf16[96,768]{1,0:T(8,128)(2,1)S(1)}, bf16[96,768]{1,0:T(8,128)(2,1)S(1)}, u32[]{:S(2)}, u32[]{:S(2)}) collective-permute-start(bf16[96,768]{1,0:T(8,128)(2,1)S(1)} %fusion.49), channel_id=1, source_target_pairs={{0,2},{1,3},{2,0},{3,1},{4,6},{5,7},{6,4},{7,5},{8,10},{9,11},{10,... | collective-permute-start | bytes 442376 | tf_op jit(solution)/shard_map/ppermute | solution.py:56
  557.8 6.8 %collective-permute-start.49 = (bf16[48,3072]{1,0:T(8,128)(2,1)S(1)}, bf16[48,3072]{1,0:T(8,128)(2,1)S(1)}, u32[]{:S(2)}, u32[]{:S(2)}) collective-permute-start(bf16[48,3072]{1,0:T(8,128)(2,1)S(1)} %pad_maximum_fusion.13), channel_id=1, source_target_pairs={{0,1},{1,0},{2,3},{3,2},{4,5},{5,4},{6,7},{7,6},{8,9},{9,8},{10,11... | collective-permute-start | bytes 884744 | tf_op jit(solution)/shard_map/ppermute | solution.py:56
  560.1 7.6 %collective-permute-start.59 = (bf16[192,768]{1,0:T(8,128)(2,1)S(1)}, bf16[192,768]{1,0:T(8,128)(2,1)S(1)}, u32[]{:S(2)}, u32[]{:S(2)}) collective-permute-start(bf16[192,768]{1,0:T(8,128)(2,1)S(1)} %pad_maximum_fusion.14), channel_id=1, source_target_pairs={{0,1},{1,0},{2,3},{3,2},{4,5},{5,4},{6,7},{7,6},{8,9},{9,8},{10,11... | collective-permute-start | bytes 884744 | tf_op jit(solution)/shard_map/ppermute | solution.py:56
  564.7 16.3 %collective-permute-start.50 = (bf16[96,3072]{1,0:T(8,128)(2,1)S(1)}, bf16[96,3072]{1,0:T(8,128)(2,1)S(1)}, u32[]{:S(2)}, u32[]{:S(2)}) collective-permute-start(bf16[96,3072]{1,0:T(8,128)(2,1)S(1)} %pad_maximum_fusion.9), channel_id=1, source_target_pairs={{0,16},{1,17},{2,18},{3,19},{4,12},{5,13},{6,14},{7,15},{8,24},{9,... | collective-permute-start | bytes 1769480 | tf_op jit(solution)/shard_map/ppermute | solution.py:56
  565.1 17.5 %collective-permute-start.26 = (bf16[192,2304]{1,0:T(8,128)(2,1)S(1)}, bf16[192,2304]{1,0:T(8,128)(2,1)S(1)}, u32[]{:S(2)}, u32[]{:S(2)}) collective-permute-start(bf16[192,2304]{1,0:T(8,128)(2,1)S(1)} %pad_maximum_fusion.7), channel_id=1, source_target_pairs={{0,8},{1,9},{2,10},{3,11},{4,20},{5,21},{6,22},{7,23},{8,0},{9,1},... | collective-permute-start | bytes 2654216 | tf_op jit(solution)/shard_map/ppermute | solution.py:56
  567.9 25.8 %collective-permute-start.60 = (bf16[384,768]{1,0:T(8,128)(2,1)S(1)}, bf16[384,768]{1,0:T(8,128)(2,1)S(1)}, u32[]{:S(2)}, u32[]{:S(2)}) collective-permute-start(bf16[384,768]{1,0:T(8,128)(2,1)S(1)} %pad_maximum_fusion.10), channel_id=1, source_target_pairs={{0,16},{1,17},{2,18},{3,19},{4,12},{5,13},{6,14},{7,15},{8,24},{9,... | collective-permute-start | bytes 1769480 | tf_op jit(solution)/shard_map/ppermute | solution.py:56
  581.3 16.3 %collective-permute-start.51 = (bf16[192,3072]{1,0:T(8,128)(2,1)S(1)}, bf16[192,3072]{1,0:T(8,128)(2,1)S(1)}, u32[]{:S(2)}, u32[]{:S(2)}) collective-permute-start(bf16[192,3072]{1,0:T(8,128)(2,1)S(1)} %pad_maximum_fusion.5), channel_id=1, source_target_pairs={{0,8},{1,9},{2,10},{3,11},{4,20},{5,21},{6,22},{7,23},{8,0},{9,1},... | collective-permute-start | bytes 3538952 | tf_op jit(solution)/shard_map/ppermute | solution.py:56
  583.1 27.9 %collective-permute-start.27 = (bf16[384,2304]{1,0:T(8,128)(2,1)S(1)}, bf16[384,2304]{1,0:T(8,128)(2,1)S(1)}, u32[]{:S(2)}, u32[]{:S(2)}) collective-permute-start(bf16[384,2304]{1,0:T(8,128)(2,1)S(1)} %pad_maximum_fusion.2), channel_id=1, source_target_pairs={{0,4},{1,5},{2,6},{3,7},{4,0},{5,1},{6,2},{7,3},{8,12},{9,13},{10,... | collective-permute-start | bytes 5308424 | tf_op jit(solution)/shard_map/ppermute | solution.py:56
  594.0 16.3 %collective-permute-start.61 = (bf16[768,768]{1,0:T(8,128)(2,1)S(1)}, bf16[768,768]{1,0:T(8,128)(2,1)S(1)}, u32[]{:S(2)}, u32[]{:S(2)}) collective-permute-start(bf16[768,768]{1,0:T(8,128)(2,1)S(1)} %pad_maximum_fusion.6), channel_id=1, source_target_pairs={{0,8},{1,9},{2,10},{3,11},{4,20},{5,21},{6,22},{7,23},{8,0},{9,1},... | collective-permute-start | bytes 3538952 | tf_op jit(solution)/shard_map/ppermute | solution.py:56
  598.4 16.8 %collective-permute-start.52 = (bf16[384,3072]{1,0:T(8,128)(2,1)S(1)}, bf16[384,3072]{1,0:T(8,128)(2,1)S(1)}, u32[]{:S(2)}, u32[]{:S(2)}) collective-permute-start(bf16[384,3072]{1,0:T(8,128)(2,1)S(1)} %pad_maximum_fusion), channel_id=1, source_target_pairs={{0,4},{1,5},{2,6},{3,7},{4,0},{5,1},{6,2},{7,3},{8,12},{9,13},{10,... | collective-permute-start | bytes 7077896 | tf_op jit(solution)/shard_map/ppermute | solution.py:56
  610.9 10.7 %collective-permute-start.62 = (bf16[1536,768]{1,0:T(8,128)(2,1)S(1)}, bf16[1536,768]{1,0:T(8,128)(2,1)S(1)}, u32[]{:S(2)}, u32[]{:S(2)}) collective-permute-start(bf16[1536,768]{1,0:T(8,128)(2,1)S(1)} %pad_maximum_fusion.1), channel_id=1, source_target_pairs={{0,4},{1,5},{2,6},{3,7},{4,0},{5,1},{6,2},{7,3},{8,12},{9,13},{10,... | collective-permute-start | bytes 7077896 | tf_op jit(solution)/shard_map/ppermute | solution.py:56
  (68 other events, 810.4 us)

commit v2 on v1

v2 whole, which is shorter than its diff:
```python
import functools

import jax
import jax.numpy as jnp
from jax import lax
from jax.experimental import pallas as pl
from jax.experimental.pallas import tpu as pltpu
from jax.sharding import PartitionSpec as P

HD = 64
AXES = ("batch", "blk")
epsilon = 1e-06
masked_score = -1e30
f32 = jnp.float32
bf16 = jnp.bfloat16
NT = (((1,), (1,)), ((), ()))
TN = (((0,), (0,)), ((), ()))

(
    V_QUERY,
    V_VALUE,
    V_OUT,
    V_GAIN1,
    V_SHIFT1,
    V_DOWN,
    V_GAIN2,
    V_SHIFT2,
    V_HEAD,
    V_HEAD_BIAS,
    V_UP,
) = range(11)


def dot(left, right, dims=None):
    if dims is None:
        return jnp.dot(left, right, preferred_element_type=f32)
    return lax.dot_general(left, right, dims, preferred_element_type=f32)


def call_params(mebibytes):
    return pltpu.CompilerParams(vmem_limit_bytes=mebibytes * 2**20)


def cost(flops, arrays):
    moved = sum(a.size * a.dtype.itemsize for a in arrays)
    return pl.CostEstimate(flops=int(flops), bytes_accessed=int(moved), transcendentals=0)


def whole(array, buffers=None):
    spec = {} if buffers is None else {"pipeline_mode": pl.Buffered(buffers)}
    return pl.BlockSpec(array.shape, lambda *i: (0,) * array.ndim, **spec)


def column_sum(values):
    return jnp.sum(values, axis=0, keepdims=True)


def row_mean(values):
    return jnp.mean(values, axis=-1, keepdims=True)


def to_column(row, count):
    return jnp.transpose(jnp.broadcast_to(row, (128, count)))[:, 0:1]


def to_row(column, count):
    return jnp.transpose(jnp.broadcast_to(column, (count, 128)))[0:1, :]


def attend_kernel(
    nz, own_rows, row, lengths, x_ref, wq, wk, wv, vec, q_ref, k_ref, v_ref, att_ref, p_ref, bias
):
    seg_len = x_ref.shape[0] // nz

    @pl.when(pl.program_id(0) == 0)
    def _():
        z = lax.axis_index("blk")
        mine = z * own_rows + row
        cols, rows = [], []
        for k in range(nz):
            base = lax.rem(z + (nz - k), nz) * seg_len
            col = lax.broadcasted_iota(jnp.int32, (seg_len, 1), 0) + base
            lane = lax.broadcasted_iota(jnp.int32, (1, seg_len), 1) + base
            end = jnp.int32(0)
            doc_col, doc_row = jnp.zeros_like(col), jnp.zeros_like(lane)
            for p in range(lengths.shape[1]):
                end = end + lengths[mine, p]
                doc_col += (col >= end).astype(jnp.int32)
                doc_row += (lane >= end).astype(jnp.int32)
            cols.append(doc_col)
            rows.append(doc_row)
        for i in range(nz):
            for j in range(nz):
                bias[pl.ds(i * seg_len, seg_len), pl.ds(j * seg_len, seg_len)] = jnp.where(
                    cols[i] == rows[j], 0.0, masked_score
                ).astype(f32)

    x = x_ref[...]
    q_ref[...] = (dot(x, wq[...]) + vec[V_QUERY : V_QUERY + 1, :]).astype(bf16)
    k_ref[...] = dot(x, wk[...]).astype(bf16)
    v_ref[...] = (dot(x, wv[...]) + vec[V_VALUE : V_VALUE + 1, :]).astype(bf16)
    first = lax.broadcasted_iota(jnp.int32, (1, 2 * HD), 1) < HD
    for pair in range(q_ref.shape[1] // (2 * HD)):
        cols = pl.ds(pair * 2 * HD, 2 * HD)
        q, k, v = q_ref[:, cols], k_ref[:, cols], v_ref[:, cols]
        outs = []
        for h in range(2):
            mine = first if h == 0 else jnp.logical_not(first)
            scaled = jnp.where(mine, q * jnp.asarray(HD**-0.5, bf16), jnp.zeros_like(q))
            scores = dot(scaled, k, NT) + bias[...]
            weights = jnp.exp(scores - jnp.max(scores, axis=1, keepdims=True))
            total = jnp.sum(weights, axis=1, keepdims=True)
            probs = (weights * (1.0 / total)).astype(bf16)
            p_ref[pair * 2 + h] = probs
            outs.append(dot(probs, v))
        att_ref[:, cols] = jnp.where(first, outs[0], outs[1]).astype(bf16)


def attend(x, lengths, wqkv, vec, nz, own_rows, row, width=256):
    n, d = x.shape
    steps, heads = d // width, width // HD

    def weight(part):
        return pl.BlockSpec((d, width), lambda j: (0, part * steps + j))

    token = pl.BlockSpec((n, width), lambda j: (0, j))
    return pl.pallas_call(
        functools.partial(attend_kernel, nz, own_rows, row),
        grid=(steps,),
        in_specs=[
            pl.BlockSpec(memory_space=pltpu.SMEM),
            whole(x),
            weight(0),
            weight(1),
            weight(2),
            pl.BlockSpec((vec.shape[0], width), lambda j: (0, j)),
        ],
        out_specs=[token] * 4 + [pl.BlockSpec((heads, n, n), lambda j: (j, 0, 0))],
        out_shape=[jax.ShapeDtypeStruct((n, d), bf16)] * 4
        + [jax.ShapeDtypeStruct((d // HD, n, n), bf16)],
        scratch_shapes=[pltpu.VMEM((n, n), f32)],
        compiler_params=call_params(24),
        cost_estimate=cost(12 * n * d * d, [x, wqkv]),
        name="attend",
    )(lengths, x, wqkv, wqkv, wqkv, vec)


def attend_back_kernel(
    g_ref, wo, q_ref, k_ref, v_ref, att_ref, p_ref, wq, wk, wv, dp_ref, gh_ref, sums, acc, up_s
):
    step = pl.program_id(0)
    up_s[...] = dot(g_ref[...], wo[...], NT).astype(bf16)
    first = lax.broadcasted_iota(jnp.int32, (1, 2 * HD), 1) < HD
    scale = HD**-0.5
    for pair in range(q_ref.shape[1] // (2 * HD)):
        cols = pl.ds(pair * 2 * HD, 2 * HD)
        q, k, v, up = q_ref[:, cols], k_ref[:, cols], v_ref[:, cols], up_s[:, cols]
        product = up.astype(f32) * att_ref[:, cols].astype(f32)
        dq, dk, dv = [], [], []
        for h in range(2):
            mine = first if h == 0 else jnp.logical_not(first)
            inner = jnp.sum(jnp.where(mine, product, 0.0), axis=1, keepdims=True)
            probs = p_ref[pair * 2 + h]
            dprobs = dot(jnp.where(mine, up, jnp.zeros_like(up)), v, NT)
            score_grad = (probs.astype(f32) * (dprobs - inner)).astype(bf16)
            dv.append(dot(probs, up, TN))
            dq.append(dot(score_grad, k))
            dk.append(dot(score_grad, q, TN))
        dp_ref[0, :, cols] = (jnp.where(first, dq[0], dq[1]) * scale).astype(bf16)
        dp_ref[1, :, cols] = (jnp.where(first, dk[0], dk[1]) * scale).astype(bf16)
        dp_ref[2, :, cols] = jnp.where(first, dv[0], dv[1]).astype(bf16)
    part = dot(dp_ref[0], wq[...], NT) + dot(dp_ref[1], wk[...], NT) + dot(dp_ref[2], wv[...], NT)
    sums[...] = jnp.zeros_like(sums)
    sums[0:1, :] = column_sum(dp_ref[0].astype(f32))
    sums[1:2, :] = column_sum(dp_ref[2].astype(f32))

    @pl.when(step == 0)
    def _():
        acc[...] = g_ref[...].astype(f32) + part

    @pl.when(step > 0)
    def _():
        acc[...] += part

    @pl.when(step == pl.num_programs(0) - 1)
    def _():
        gh_ref[...] = acc[...].astype(bf16)


def attend_back(g, wo, q, k, v, att, probs, wqkv, width=256):
    n, d = g.shape
    steps, heads = d // width, width // HD

    def weight(part):
        return pl.BlockSpec((d, width), lambda j: (0, part * steps + j))

    token = pl.BlockSpec((n, width), lambda j: (0, j))
    return pl.pallas_call(
        attend_back_kernel,
        grid=(steps,),
        in_specs=[
            whole(g),
            pl.BlockSpec((width, d), lambda j: (j, 0)),
            token,
            token,
            token,
            token,
            pl.BlockSpec((heads, n, n), lambda j: (j, 0, 0)),
            weight(0),
            weight(1),
            weight(2),
        ],
        out_specs=[
            pl.BlockSpec((3, n, width), lambda j: (0, 0, j)),
            whole(g),
            pl.BlockSpec((8, width), lambda j: (0, j)),
        ],
        out_shape=[
            jax.ShapeDtypeStruct((3, n, d), bf16),
            jax.ShapeDtypeStruct((n, d), bf16),
            jax.ShapeDtypeStruct((8, d), f32),
        ],
        scratch_shapes=[pltpu.VMEM((n, d), f32), pltpu.VMEM((n, width), bf16)],
        compiler_params=call_params(32),
        cost_estimate=cost(20 * n * d * d, [g, wo, q, k, v, att, probs, wqkv]),
        name="attend_back",
    )(g, wo, q, k, v, att, probs, wqkv, wqkv, wqkv)


def feed_kernel(x_ref, att_ref, wo, wu, wd, vec, hid, tw, act, slope, low, n1_ref, n2_ref, stats):
    n, d = x_ref.shape
    parts = act.shape[1] // d

    def row(i):
        return vec[i : i + 1, :]

    first_sum = x_ref[...].astype(f32) + dot(att_ref[...], wo[...]) + row(V_OUT)
    center = first_sum - row_mean(first_sum)
    scale1 = lax.rsqrt(row_mean(center * center) + epsilon)
    n1 = center * scale1
    n1_ref[...] = n1.astype(bf16)
    normed = n1 * row(V_GAIN1) + row(V_SHIFT1)
    normed_low = normed.astype(bf16)
    low[...] = normed_low
    second_sum = normed + row(V_DOWN)
    for c in range(parts):
        cols = pl.ds(c * d, d)
        gate = dot(normed_low, wu[:, cols]) + row(V_UP + c)
        below = 0.5 * (1.0 + lax.erf(gate * (0.5**0.5)))
        density = jnp.exp(-0.5 * gate * gate) * 0.3989422804014327
        active = (gate * below).astype(bf16)
        act[:, cols] = active
        slope[:, cols] = (below + gate * density).astype(bf16)
        second_sum += dot(active, wd[cols, :])
    center = second_sum - row_mean(second_sum)
    scale2 = lax.rsqrt(row_mean(center * center) + epsilon)
    n2 = center * scale2
    n2_ref[...] = n2.astype(bf16)
    final = n2 * row(V_GAIN2) + row(V_SHIFT2)
    hid[...] = final.astype(bf16)
    logits = jnp.sum(final * row(V_HEAD), axis=1, keepdims=True) + vec[V_HEAD_BIAS, 0]
    tw[...] = to_row(
        jnp.maximum(logits, 0.0) + jnp.log1p(jnp.exp(-jnp.abs(logits))), n
    )
    lane = lax.broadcasted_iota(jnp.int32, (1, 128), 1)
    stats[...] = jnp.where(lane == 0, scale1, jnp.where(lane == 1, scale2, logits))


def feed(x, att, wo, wu, wd, vec, tile):
    n, d = x.shape
    hidden = wu.shape[1]
    token = pl.BlockSpec((tile, d), lambda i: (i, 0))
    wide = pl.BlockSpec((tile, hidden), lambda i: (i, 0))
    return pl.pallas_call(
        feed_kernel,
        grid=(n // tile,),
        in_specs=[token, token, whole(wo, 1), whole(wu, 1), whole(wd, 1), whole(vec, 1)],
        out_specs=[
            token,
            pl.BlockSpec((1, tile), lambda i: (0, i)),
            wide,
            wide,
            token,
            token,
            token,
            pl.BlockSpec((tile, 128), lambda i: (i, 0)),
        ],
        out_shape=[
            jax.ShapeDtypeStruct((n, d), bf16),
            jax.ShapeDtypeStruct((1, n), f32),
            jax.ShapeDtypeStruct((n, hidden), bf16),
            jax.ShapeDtypeStruct((n, hidden), bf16),
            jax.ShapeDtypeStruct((n, d), bf16),
            jax.ShapeDtypeStruct((n, d), bf16),
            jax.ShapeDtypeStruct((n, d), bf16),
            jax.ShapeDtypeStruct((n, 128), f32),
        ],
        compiler_params=call_params(40),
        cost_estimate=cost(2 * n * d * (d + 2 * hidden), [x, att, wo, wu, wd]),
        name="feed",
    )(x, att, wo, wu, wd, vec)


def head_back_kernel(cot, term_cot, n2_ref, stats, vec, fg, sums):
    n = cot.shape[0]

    def row(i):
        return vec[i : i + 1, :]

    n2 = n2_ref[...].astype(f32)
    scale2, logits = stats[:, 1:2], stats[:, 2:3]
    term_grad = to_column(term_cot[...], n) * (1.0 / (1.0 + jnp.exp(-logits)))
    final_grad = cot[...].astype(f32) + term_grad * row(V_HEAD)
    gained = final_grad * row(V_GAIN2)
    grad = (gained - row_mean(gained) - n2 * row_mean(gained * n2)) * scale2
    grad_low = grad.astype(bf16)
    fg[...] = grad_low
    part = jnp.concatenate(
        [
            column_sum(final_grad * n2),
            column_sum(final_grad),
            column_sum(term_grad * (n2 * row(V_GAIN2) + row(V_SHIFT2))),
            column_sum(grad_low.astype(f32)),
            jnp.broadcast_to(jnp.sum(term_grad, axis=0, keepdims=True), (1, cot.shape[1])),
            jnp.zeros((3, cot.shape[1]), f32),
        ],
        axis=0,
    )

    @pl.when(pl.program_id(0) == 0)
    def _():
        sums[...] = part

    @pl.when(pl.program_id(0) > 0)
    def _():
        sums[...] += part


def head_back(cot, term_cot, n2, stats, vec, tile):
    n, d = cot.shape
    token = pl.BlockSpec((tile, d), lambda i: (i, 0))
    return pl.pallas_call(
        head_back_kernel,
        grid=(n // tile,),
        in_specs=[
            token,
            pl.BlockSpec((1, tile), lambda i: (0, i)),
            token,
            pl.BlockSpec((tile, 128), lambda i: (i, 0)),
            whole(vec, 1),
        ],
        out_specs=[token, pl.BlockSpec((8, d), lambda i: (0, 0))],
        out_shape=[jax.ShapeDtypeStruct((n, d), bf16), jax.ShapeDtypeStruct((8, d), f32)],
        compiler_params=call_params(16),
        cost_estimate=cost(20 * n * d, [cot, n2]),
        name="head_back",
    )(cot, term_cot, n2, stats, vec)


def feed_back_kernel(fg_ref, slope, n1_ref, stats, wu, wd, vec, gate_grad, ag, sums):
    d = fg_ref.shape[1]
    parts = slope.shape[1] // d
    fg = fg_ref[...]
    total = fg.astype(f32)
    ups = []
    for c in range(parts):
        cols = pl.ds(c * d, d)
        grad = (dot(fg, wd[cols, :], NT) * slope[:, cols].astype(f32)).astype(bf16)
        gate_grad[:, cols] = grad
        ups.append(column_sum(grad.astype(f32)))
        total += dot(grad, wu[:, cols], NT)
    n1 = n1_ref[...].astype(f32)
    gained = total * vec[V_GAIN1 : V_GAIN1 + 1, :]
    low = ((gained - row_mean(gained) - n1 * row_mean(gained * n1)) * stats[:, 0:1]).astype(bf16)
    ag[...] = low
    part = jnp.concatenate(
        [column_sum(total * n1), column_sum(total), column_sum(low.astype(f32))]
        + ups
        + [jnp.zeros((sums.shape[0] - 3 - parts, d), f32)],
        axis=0,
    )

    @pl.when(pl.program_id(0) == 0)
    def _():
        sums[...] = part

    @pl.when(pl.program_id(0) > 0)
    def _():
        sums[...] += part


def feed_back(fg, slope, n1, stats, wu, wd, vec, tile):
    n, d = fg.shape
    hidden = wu.shape[1]
    count = -(-(3 + hidden // d) // 8) * 8
    token = pl.BlockSpec((tile, d), lambda i: (i, 0))
    wide = pl.BlockSpec((tile, hidden), lambda i: (i, 0))
    return pl.pallas_call(
        feed_back_kernel,
        grid=(n // tile,),
        in_specs=[
            token,
            wide,
            token,
            pl.BlockSpec((tile, 128), lambda i: (i, 0)),
            whole(wu, 1),
            whole(wd, 1),
            whole(vec, 1),
        ],
        out_specs=[wide, token, pl.BlockSpec((count, d), lambda i: (0, 0))],
        out_shape=[
            jax.ShapeDtypeStruct((n, hidden), bf16),
            jax.ShapeDtypeStruct((n, d), bf16),
            jax.ShapeDtypeStruct((count, d), f32),
        ],
        compiler_params=call_params(40),
        cost_estimate=cost(4 * n * d * hidden, [fg, slope, n1, wu, wd]),
        name="feed_back",
    )(fg, slope, n1, stats, wu, wd, vec)


def weight_kernel(count, which, *refs):
    out = refs[-1]
    total = dot(refs[0][...], refs[count][...].reshape(refs[count].shape[-2:]), TN)
    for i in range(1, count):
        total += dot(refs[i][...], refs[count + i][...].reshape(refs[count].shape[-2:]), TN)
    out[...] = total.astype(bf16)


def weight_grad(lefts, rights, which, block):
    count = len(lefts)
    n, rows = lefts[0].shape
    half = rows // 2
    parts = rights[0].shape[0] if rights[0].ndim == 3 else 1
    width = rights[0].shape[-1]
    if rights[0].ndim == 3:
        grid = (parts, width // block)
        left = pl.BlockSpec((n, half), lambda p, j, w: (0, w[0]))
        right = pl.BlockSpec((1, n, block), lambda p, j, w: (p, 0, j))
        out = pl.BlockSpec((half, block), lambda p, j, w: (0, p * (width // block) + j))
    else:
        grid = (half // block,)
        left = pl.BlockSpec((n, block), lambda j, w: (0, w[0] * (half // block) + j))
        right = pl.BlockSpec((n, width), lambda j, w: (0, 0))
        out = pl.BlockSpec((block, width), lambda j, w: (j, 0))
    return pl.pallas_call(
        lambda w, *refs: weight_kernel(count, w, *refs),
        grid_spec=pltpu.PrefetchScalarGridSpec(
            num_scalar_prefetch=1,
            grid=grid,
            in_specs=[left] * count + [right] * count,
            out_specs=out,
        ),
        out_shape=jax.ShapeDtypeStruct((half, parts * width), bf16),
        compiler_params=call_params(32),
        cost_estimate=cost(2 * count * n * half * parts * width, list(rights)),
        name="weight_grad",
    )(which, *lefts, *rights)


def join_kernel(count, bit, mine, other, out):
    here = pl.program_id(0) // count == bit[0]
    out[...] = jnp.where(here, mine[...], other[...]).astype(out.dtype)


def join(mine, other, bit, dtype, block):
    rows, width = mine.shape
    count = rows // block

    def place(i, own):
        return jnp.clip(i - own * count, 0, count - 1)

    return pl.pallas_call(
        lambda b, *refs: join_kernel(count, b, *refs),
        grid_spec=pltpu.PrefetchScalarGridSpec(
            num_scalar_prefetch=1,
            grid=(2 * count,),
            in_specs=[
                pl.BlockSpec((block, width), lambda i, b: (place(i, b[0]), 0)),
                pl.BlockSpec((block, width), lambda i, b: (place(i, 1 - b[0]), 0)),
            ],
            out_specs=pl.BlockSpec((block, width), lambda i, b: (i, 0)),
        ),
        out_shape=jax.ShapeDtypeStruct((2 * rows, width), dtype),
        compiler_params=call_params(24),
        cost_estimate=cost(0, [mine, mine, mine, mine]),
        name="join",
    )(bit, mine, other)


def bits_of(count):
    return max(count - 1, 0).bit_length()


def move(array, sizes, partner):
    pairs = []
    for b in range(sizes[0]):
        for z in range(sizes[1]):
            to_b, to_z = partner(b, z)
            pairs.append((b * sizes[1] + z, to_b * sizes[1] + to_z))
    return lax.ppermute(array, AXES, pairs)


def send_round(blocks, sizes, sign):
    nz = sizes[1]
    return [blocks[0]] + [
        move(blocks[k], sizes, lambda b, z, k=k: (b, (z + sign * k) % nz)) for k in range(1, nz)
    ]


def to_rows(local, sizes, row):
    nz = sizes[1]
    z = lax.axis_index("blk")
    own_rows = local.shape[0] // nz
    blocks = [
        lax.dynamic_index_in_dim(local, ((z + k) % nz) * own_rows + row, 0, False)
        for k in range(nz)
    ]
    return send_round(blocks, sizes, 1)


def to_segments(rows, sizes):
    nz, own_rows = sizes[1], len(rows)
    z = lax.axis_index("blk")
    got = [send_round(row, sizes, -1) for row in rows]
    out = jnp.zeros((nz * own_rows,) + got[0][0].shape, got[0][0].dtype)
    for k in range(nz):
        for r in range(own_rows):
            out = lax.dynamic_update_index_in_dim(out, got[r][k], ((z + k) % nz) * own_rows + r, 0)
    return out


def halving_steps(sizes):
    batch_bits, blk_bits = bits_of(sizes[0]), bits_of(sizes[1])
    middle = [("b", bit) for bit in range(1, batch_bits)]
    steps = [(("b", 0), ("b", 0))] if batch_bits else []
    steps += list(zip(middle, reversed(middle)))
    return steps + [(("z", bit), ("z", bit)) for bit in range(blk_bits)]


def step_partner(step):
    def partner(b, z):
        axis, bit = step[b & 1]
        return (b ^ (1 << bit), z) if axis == "b" else (b, z ^ (1 << bit))

    return partner


def own_bit(step):
    b, z = lax.axis_index("batch"), lax.axis_index("blk")

    def value(part):
        return ((b if part[0] == "b" else z) >> part[1]) & 1

    return jnp.where(b & 1 == 1, value(step[1]), value(step[0])).astype(jnp.int32)


def add_halves(keep, got, bit):
    def half(which):
        shape = (2, keep.shape[0] // 2) + keep.shape[1:]
        mine = lax.dynamic_index_in_dim(keep.reshape(shape), which, 0, False)
        other = lax.dynamic_index_in_dim(got.reshape(shape), which, 0, False)
        return (mine.astype(f32) + other.astype(f32)).astype(bf16)

    return half(1 - bit), half(bit)


def sum_matrix(send, keep, sizes):
    steps = halving_steps(sizes)
    bits = [own_bit(step) for step in steps]
    for i, step in enumerate(steps):
        got = move(send, sizes, step_partner(step))
        if i + 1 < len(steps):
            send, keep = add_halves(keep, got, bits[i + 1])
        else:
            keep = (keep.astype(f32) + got.astype(f32)).astype(bf16)
    for i in reversed(range(len(steps))):
        got = move(keep, sizes, step_partner(steps[i]))
        if i > 0:
            bit = bits[i]
            keep = jnp.concatenate(
                [jnp.where(bit == 0, keep, got), jnp.where(bit == 0, got, keep)], axis=0
            )
        else:
            keep = join(keep, got, bits[i].reshape(1), f32, keep.shape[0] // 2)
    return keep


def sum_small(array, sizes):
    for step in halving_steps(sizes):
        array = array + move(array, sizes, step_partner(step))
    return array


def per_device(
    hidden_in,
    lengths,
    qkv_weight,
    qv_bias,
    out_weight,
    out_bias,
    attn_gain,
    attn_shift,
    up_weight,
    up_bias,
    down_weight,
    down_bias,
    ffn_gain,
    ffn_shift,
    head_weight,
    head_bias,
    hidden_cot,
    term_cot,
):
    row_count, seg_len, d = hidden_in.shape
    hidden = up_weight.shape[1]
    parts = hidden // d
    sizes = (lax.axis_size("batch"), lax.axis_size("blk"))
    nz = sizes[1]
    own_rows = row_count // nz
    n = seg_len * nz
    tile = n // 2
    rows = range(own_rows)
    core = (lax.axis_index("batch") & 1).astype(jnp.int32).reshape(1)

    x = [jnp.concatenate(to_rows(hidden_in, sizes, r), axis=0) for r in rows]
    cot = [jnp.concatenate(to_rows(hidden_cot, sizes, r), axis=0) for r in rows]
    own_slots = lax.all_gather(term_cot, "blk", axis=0)
    own_slots = jnp.stack([
        lax.dynamic_index_in_dim(own_slots, (lax.axis_index("blk") - k) % nz, 0, False)
        for k in range(nz)
    ], axis=1)
    own_slots = lax.dynamic_slice_in_dim(
        own_slots, lax.axis_index("blk") * own_rows, own_rows, 0
    ).reshape(own_rows, 1, n)

    vec = jnp.concatenate(
        [
            qv_bias,
            out_bias[None],
            attn_gain[None],
            attn_shift[None],
            down_bias[None],
            ffn_gain[None],
            ffn_shift[None],
            head_weight[None],
            jnp.broadcast_to(head_bias[None], (1, d)),
            up_bias.reshape(parts, d),
            jnp.zeros((-(V_UP + parts) % 8, d), bf16),
        ],
        axis=0,
    ).astype(f32)

    att, back = [], []
    for r in rows:
        q, k, v, a, probs = attend(x[r], lengths, qkv_weight, vec, nz, own_rows, r)
        att.append(a)
        back.append((q, k, v, a, probs))
    fed = [feed(x[r], att[r], out_weight, up_weight, down_weight, vec, tile) for r in rows]
    hid, term, act, slope, low, n1, n2, stats = zip(*fed)
    hidden_out = to_segments(
        [[hid[r][k * seg_len : (k + 1) * seg_len] for k in range(nz)] for r in rows], sizes
    )
    term_weight = to_segments(
        [[term[r][0, k * seg_len : (k + 1) * seg_len] for k in range(nz)] for r in rows], sizes
    )
    fg, head_sums = zip(
        *[head_back(cot[r], own_slots[r], n2[r], stats[r], vec, tile) for r in rows]
    )
    down = [weight_grad(act, fg, w, 384) for w in (1 - core, core)]
    gate_grad, ag, feed_sums = zip(
        *[feed_back(fg[r], slope[r], n1[r], stats[r], up_weight, down_weight, vec, tile) for r in rows]
    )
    up = [weight_grad(low, [g[None] for g in gate_grad], w, 768) for w in (1 - core, core)]
    out = [weight_grad(att, ag, w, 384) for w in (1 - core, core)]
    backs = [attend_back(ag[r], out_weight, *back[r], qkv_weight) for r in rows]
    proj_grad, gh, qv_sums = zip(*backs)
    qkv = [weight_grad(x, proj_grad, w, 768) for w in (1 - core, core)]
    grad_hidden = to_segments(
        [[gh[r][k * seg_len : (k + 1) * seg_len] for k in range(nz)] for r in rows], sizes
    ).astype(f32)

    early = sum_small(jnp.concatenate([sum(head_sums), sum(feed_sums)], axis=0), sizes)
    late = sum_small(sum(qv_sums), sizes)
    grad_down, grad_up, grad_out, grad_qkv = [
        sum_matrix(*pair, sizes) for pair in (down, up, out, qkv)
    ]
    return (
        hidden_out,
        term_weight,
        grad_hidden,
        grad_qkv,
        late[0:2],
        grad_out,
        early[10],
        early[8],
        early[9],
        grad_up,
        early[11 : 11 + parts].reshape(hidden),
        grad_down,
        early[3],
        early[0],
        early[1],
        early[2],
        early[4, 0:1],
    )


def solution(mesh):
    split = P("batch", "blk", None)
    flat = P("batch", "blk")
    return jax.shard_map(
        per_device,
        mesh=mesh,
        in_specs=(split, P("batch", None)) + (P(),) * 14 + (split, flat),
        out_specs=(split, flat, split) + (P(),) * 14,
        check_vma=False,
    )
```

time: 637 us -> 528 us (0.83)
  matrix products: 166 us -> 0 us
  Pallas kernels: 0 us -> 135 us
  other arithmetic: 99.3 us -> 19.9 us
  local copies, waits for them, and re-layouts: 103 us -> 54.3 us
  blocking collectives: 0 us -> 31.1 us
  waiting for transfers between devices: 169 us -> 193 us
    dot_general x19 -> x0, matrix products: 149 us -> none  [the longest x1 35.1 us: per_device(): jnp.dot(normed_low, up_weight, preferred_element_type=jnp.float32)]
    pallas_call x0 -> x22, Pallas kernels: none -> 135 us  [the longest x2 25.2 us: attend_back(): pl.pallas_call(attend_back_kernel, grid=(steps,), in_specs=[whole(g), pl....]
    convert_element_type x37 -> x22, other arithmetic: 69.8 us -> 5.66 us  [the longest x16 3.52 us: half(): return (mine.astype(f32) + other.astype(f32)).astype(bf16)]
    all_gather x0 -> x1, blocking collectives: none -> 31.1 us  [per_device(): own_slots = lax.all_gather(term_cot, 'blk', axis=0)]
    ppermute x63 -> x80, waiting for transfers between devices: 169 us -> 193 us  [move(): return lax.ppermute(array, AXES, pairs)]
    convert_element_type x4 -> x0, local copies, waits for them, and re-layouts: 20.3 us -> none  [the longest x1 9.43 us: per_device(): proj_grad = jnp.stack([query_grad, key_grad, vals_grad], axis=2).reshape(...]
    reduce_sum x11 -> x0, other arithmetic: 17.2 us -> none  [the longest x2 5.94 us: layer_norm(): center = values - jnp.mean(values, axis=-1, keepdims=True)]
    sub x1 -> x0, matrix products: 16.4 us -> none  [per_device(): weights = jnp.exp(scores - row_max)]
  transfers between devices with their start and end apart: 63 -> 80, of which waited for: 31 -> 41; matrix products, arithmetic and copies ran while one was open for 31% -> 7% of each run, Pallas kernels for 0% -> 20%
where the time goes in v2:
time: 528 us; the launch traced here: 522 us
  waiting for transfers between devices  193 us (37%)
  Pallas kernels  135 us (26%)
  starting transfers between devices  86.3 us (16%)
  local copies, waits for them, and re-layouts  54.3 us (10%)
  blocking collectives  31.1 us (6%)
  other arithmetic  19.9 us (4%)
    ppermute x80, waiting for transfers between devices, move(): return lax.ppermute(array, AXES, pairs)  193 us
    ppermute x80, starting transfers between devices, move(): return lax.ppermute(array, AXES, pairs)  86.3 us
    unnamed x180, local copies, waits for them, and re-layouts  32.3 us
    all_gather x1, blocking collectives, per_device(): own_slots = lax.all_gather(term_cot, 'blk', axis=0)  31.1 us
    pallas_call x2, Pallas kernels, attend_back(): pl.pallas_call(attend_back_kernel, grid=(steps,), in_specs=[whole(g), pl....  25.2 us
    pallas_call x2, Pallas kernels, feed(): pl.pallas_call(feed_kernel, grid=(n // tile,), in_specs=[token, token, wh...  25.1 us
    pallas_call x8, Pallas kernels, weight_grad(): pl.pallas_call(lambda w, *refs: weight_kernel(count, w, *refs), grid_spec...  22.9 us
    pallas_call x4, Pallas kernels, join(): pl.pallas_call(lambda b, *refs: join_kernel(count, b, *refs), grid_spec=p...  20.9 us
  transfers between devices with their start and end apart: 80, of which 41 were waited for; matrix products, arithmetic and copies ran while one was open for 7% of the time, Pallas kernels for 20%

profile of v2, /device:TPU:0, one launch (start us, length us, event | category | flops | bytes accessed | tf_op | source)
XLA Modules:
  0.0 522.5 jit_solution(10738691672211153025)
XLA Ops:
  0.9 2.4 dynamic-slice_bitcast_fusion.11
  3.3 3.0 collective-permute-start.3
  13.3 31.1 %all-gather = f32[32,128]{1,0:T(8,128)S(1)} all-gather(f32[8,128]{1,0:T(8,128)S(1)} %copy-done.77), channel_id=2, replica_groups=mesh['batch'=8,'blk'=4] {'blk'}, dimensions={0}, use_global_device_ids=true | all-gather | bytes 20480 | tf_op jit(solution)/shard_map/all_gather | solution.py:628
  46.9 3.1 collective-permute-start.20
  52.9 9.9 %attend.3 = (bf16[512,768]{1,0:T(8,128)(2,1)S(1)}, bf16[512,768]{1,0:T(8,128)(2,1)S(1)}, bf16[512,768]{1,0:T(8,128)(2,1)S(1)}, bf16[512,768]{1,0:T(8,128)(2,1)S(1)}, bf16[12,512,512]{2,1,0:T(8,128)(2,1)S(1)}) custom-call(s32[8,8]{1,0:T(8,128)S(1)} %copy-done.37, bf16[512,768]{1,0:T(8,128)(2,1)S(1)} %pad_maximum_fusion.7.x_ref.refs_1_, ...), custom_call_target="tpu_custom_call" | custom-call | flops 3623878656 | bytes 4325376 | tf_op jit(solution)/shard_map/attend/pallas_call | solution.py:127
  62.9 2.7 copy-done.38
  68.8 2.6 collective-permute-start.23
  72.4 9.9 %attend.2 = (bf16[512,768]{1,0:T(8,128)(2,1)S(1)}, bf16[512,768]{1,0:T(8,128)(2,1)S(1)}, bf16[512,768]{1,0:T(8,128)(2,1)S(1)}, bf16[512,768]{1,0:T(8,128)(2,1)S(1)}, bf16[12,512,512]{2,1,0:T(8,128)(2,1)S(1)}) custom-call(s32[8,8]{1,0:T(8,128)S(1)} %copy-done.37, bf16[512,768]{1,0:T(8,128)(2,1)S(1)} %pad_maximum_fusion.6.x_ref.refs_0_, ...), custom_call_target="tpu_custom_call" | custom-call | flops 3623878656 | bytes 4325376 | tf_op jit(solution)/shard_map/attend/pallas_call | solution.py:127
  82.4 2.7 copy-done.40
  87.0 12.8 %feed.2 = (bf16[512,768]{1,0:T(8,128)(2,1)S(1)}, f32[1,512]{1,0:T(1,128)S(1)}, bf16[512,3072]{1,0:T(8,128)(2,1)S(1)}, bf16[512,3072]{1,0:T(8,128)(2,1)S(1)}, bf1...) custom-call(bf16[512,768]{1,0:T(8,128)(2,1)S(1)} %pad_maximum_fusion, ...), custom_call_target="tpu_custom_call" | custom-call | flops 5435817984 | bytes 12189696 | tf_op jit(solution)/shard_map/feed/pallas_call | solution.py:274
  103.8 12.3 %feed.3 = (bf16[512,768]{1,0:T(8,128)(2,1)S(1)}, f32[1,512]{1,0:T(1,128)S(1)}, bf16[512,3072]{1,0:T(8,128)(2,1)S(1)}, bf16[512,3072]{1,0:T(8,128)(2,1)S(1)}, bf1...) custom-call(bf16[512,768]{1,0:T(8,128)(2,1)S(1)} %pad_maximum_fusion, ...), custom_call_target="tpu_custom_call" | custom-call | flops 5435817984 | bytes 12189696 | tf_op jit(solution)/shard_map/feed/pallas_call | solution.py:274
  121.6 2.6 copy-done.30
  124.2 8.6 %feed_back.2 = (bf16[512,3072]{1,0:T(8,128)(2,1)S(1)}, bf16[512,768]{1,0:T(8,128)(2,1)S(1)}, f32[8,768]{1,0:T(8,128)S(1)}) custom-call(bf16[512,768]{1,0:T(8,128)(2,1)S(1)} %get-tuple-element.67.fg_ref.refs_2_, bf16[512,3072]{1,0:T(8,128)(2,1)S(1)} %copy-done.57, bf16[512,768]{1,0:T(8,128)(2,1)S(1)} %get-tuple-element.69.n1_ref, ...), custom_call_target="tpu_custom_call" | custom-call | flops 4831838208 | bytes 14155776 | tf_op jit(solution)/shard_map/feed_back/pallas_call | solution.py:398
  136.1 2.3 copy-done.31
  140.3 8.4 %feed_back.3 = (bf16[512,3072]{1,0:T(8,128)(2,1)S(1)}, bf16[512,768]{1,0:T(8,128)(2,1)S(1)}, f32[8,768]{1,0:T(8,128)S(1)}) custom-call(bf16[512,768]{1,0:T(8,128)(2,1)S(1)} %get-tuple-element.78.fg_ref.refs_3_, bf16[512,3072]{1,0:T(8,128)(2,1)S(1)} %copy-done.55, bf16[512,768]{1,0:T(8,128)(2,1)S(1)} %get-tuple-element.80.n1_ref, ...), custom_call_target="tpu_custom_call" | custom-call | flops 4831838208 | bytes 14155776 | tf_op jit(solution)/shard_map/feed_back/pallas_call | solution.py:398
  151.9 3.9 weight_grad.12
  155.9 3.9 weight_grad.13
  159.9 3.6 weight_grad.14
  163.6 3.6 weight_grad.15
  171.0 2.8 copy-done.41
  173.8 12.7 %attend_back.2 = (bf16[3,512,768]{2,1,0:T(8,128)(2,1)S(1)}, bf16[512,768]{1,0:T(8,128)(2,1)S(1)}, f32[8,768]{1,0:T(8,128)S(1)}) custom-call(bf16[512,768]{1,0:T(8,128)(2,1)S(1)} %copy-done.17, bf16[768,768]{1,0:T(8,128)(2,1)S(1)} %copy-done.36, bf16[512,768]{1,0:T(8,128)(2,1)S(1)} %copy-done.49, bf16[512,768]{1,0:T(8,128)(2,1)S(1)} %copy-done.51, ...), custom_call_target="tpu_custom_call" | custom-call | flops 6039797760 | bytes 14942208 | tf_op jit(solution)/shard_map/attend_back/pallas_call | solution.py:198
  189.6 2.8 copy-done.39
  192.3 12.5 %attend_back.3 = (bf16[3,512,768]{2,1,0:T(8,128)(2,1)S(1)}, bf16[512,768]{1,0:T(8,128)(2,1)S(1)}, f32[8,768]{1,0:T(8,128)S(1)}) custom-call(bf16[512,768]{1,0:T(8,128)(2,1)S(1)} %copy-done.19, bf16[768,768]{1,0:T(8,128)(2,1)S(1)} %copy-done.36, bf16[512,768]{1,0:T(8,128)(2,1)S(1)} %copy-done.43, bf16[512,768]{1,0:T(8,128)(2,1)S(1)} %copy-done.45, ...), custom_call_target="tpu_custom_call" | custom-call | flops 6039797760 | bytes 14942208 | tf_op jit(solution)/shard_map/attend_back/pallas_call | solution.py:198
  207.3 2.6 weight_grad.8
  209.9 2.7 weight_grad.9
  219.0 2.3 collective-permute-done.42
  222.4 2.8 collective-permute-done.43
  251.9 7.0 %collective-permute-done.24 = bf16[128,768]{1,0:T(8,128)(2,1)S(1)} collective-permute-done((bf16[128,768]{1,0:T(8,128)(2,1)}, bf16[128,768]{1,0:T(8,128)(2,1)S(1)}, u32[]{:S(2)}, u32[]{:S(2)}) %collective-permute-start.24) | collective-permute-done | bytes 196640 | tf_op jit(solution)/shard_map/ppermute | solution.py:501
  261.4 3.5 collective-permute-start.8
  270.0 2.8 collective-permute-done.47
  272.8 9.8 %collective-permute-done.27 = bf16[128,768]{1,0:T(8,128)(2,1)S(1)} collective-permute-done((bf16[128,768]{1,0:T(8,128)(2,1)S(1)}, bf16[128,768]{1,0:T(8,128)(2,1)S(1)}, u32[]{:S(2)}, u32[]{:S(2)}) %collective-permute-start.27) | collective-permute-done | bytes 196640 | tf_op jit(solution)/shard_map/ppermute | solution.py:501
  283.7 3.2 collective-permute-done.48
  293.7 7.0 %collective-permute-done.29 = bf16[128,768]{1,0:T(8,128)(2,1)S(1)} collective-permute-done((bf16[128,768]{1,0:T(8,128)(2,1)S(1)}, bf16[128,768]{1,0:T(8,128)(2,1)S(1)}, u32[]{:S(2)}, u32[]{:S(2)}) %collective-permute-start.29) | collective-permute-done | bytes 196640 | tf_op jit(solution)/shard_map/ppermute | solution.py:501
  300.7 4.9 collective-permute-done.50
  307.9 4.1 collective-permute-done.51
  314.8 7.5 %collective-permute-done.32 = bf16[96,2304]{1,0:T(8,128)(2,1)S(1)} collective-permute-done((bf16[96,2304]{1,0:T(8,128)(2,1)S(1)}, bf16[96,2304]{1,0:T(8,128)(2,1)S(1)}, u32[]{:S(2)}, u32[]{:S(2)}) %collective-permute-start.32) | collective-permute-done | bytes 442400 | tf_op jit(solution)/shard_map/ppermute | solution.py:501
  325.2 5.0 collective-permute-done.33
  331.5 6.0 %collective-permute-done.34 = bf16[24,2304]{1,0:T(8,128)(2,1)S(1)} collective-permute-done((bf16[24,2304]{1,0:T(8,128)(2,1)S(1)}, bf16[24,2304]{1,0:T(8,128)(2,1)S(1)}, u32[]{:S(2)}, u32[]{:S(2)}) %collective-permute-start.34) | collective-permute-done | bytes 110624 | tf_op jit(solution)/shard_map/ppermute | solution.py:501
  341.1 19.5 %collective-permute-done.61 = bf16[192,3072]{1,0:T(8,128)(2,1)S(1)} collective-permute-done((bf16[192,3072]{1,0:T(8,128)(2,1)S(1)}, bf16[192,3072]{1,0:T(8,128)(2,1)S(1)}, u32[]{:S(2)}, u32[]{:S(2)}) %collective-permute-start.61) | collective-permute-done | bytes 1179680 | tf_op jit(solution)/shard_map/ppermute | solution.py:501
  364.8 6.2 %collective-permute-done.62 = bf16[96,3072]{1,0:T(8,128)(2,1)S(1)} collective-permute-done((bf16[96,3072]{1,0:T(8,128)(2,1)S(1)}, bf16[96,3072]{1,0:T(8,128)(2,1)S(1)}, u32[]{:S(2)}, u32[]{:S(2)}) %collective-permute-start.62) | collective-permute-done | bytes 589856 | tf_op jit(solution)/shard_map/ppermute | solution.py:501
  372.2 4.2 collective-permute-done.73
  376.5 4.3 collective-permute-done.63
  382.1 7.8 %collective-permute-done.74 = bf16[96,768]{1,0:T(8,128)(2,1)S(1)} collective-permute-done((bf16[96,768]{1,0:T(8,128)(2,1)S(1)}, bf16[96,768]{1,0:T(8,128)(2,1)S(1)}, u32[]{:S(2)}, u32[]{:S(2)}) %collective-permute-start.74) | collective-permute-done | bytes 147488 | tf_op jit(solution)/shard_map/ppermute | solution.py:501
  390.1 3.5 collective-permute-done.64
  393.7 4.3 collective-permute-done.75
  400.4 6.6 %collective-permute-done.76 = bf16[192,768]{1,0:T(8,128)(2,1)S(1)} collective-permute-done((bf16[192,768]{1,0:T(8,128)(2,1)S(1)}, bf16[192,768]{1,0:T(8,128)(2,1)S(1)}, u32[]{:S(2)}, u32[]{:S(2)}) %collective-permute-start.76) | collective-permute-done | bytes 294944 | tf_op jit(solution)/shard_map/ppermute | solution.py:501
  412.5 8.0 %collective-permute-done.77 = bf16[384,768]{1,0:T(8,128)(2,1)S(1)} collective-permute-done((bf16[384,768]{1,0:T(8,128)(2,1)S(1)}, bf16[384,768]{1,0:T(8,128)(2,1)S(1)}, u32[]{:S(2)}, u32[]{:S(2)}) %collective-permute-start.77) | collective-permute-done | bytes 589856 | tf_op jit(solution)/shard_map/ppermute | solution.py:501
  420.8 2.5 collective-permute-start.78
  423.3 9.9 %collective-permute-done.67 = bf16[96,3072]{1,0:T(8,128)(2,1)S(1)} collective-permute-done((bf16[96,3072]{1,0:T(8,128)(2,1)S(1)}, bf16[96,3072]{1,0:T(8,128)(2,1)S(1)}, u32[]{:S(2)}, u32[]{:S(2)}) %collective-permute-start.67) | collective-permute-done | bytes 589856 | tf_op jit(solution)/shard_map/ppermute | solution.py:501
  433.5 2.5 collective-permute-start.68
  435.9 6.7 %collective-permute-done.37 = bf16[96,2304]{1,0:T(8,128)(2,1)S(1)} collective-permute-done((bf16[96,2304]{1,0:T(8,128)(2,1)S(1)}, bf16[96,2304]{1,0:T(8,128)(2,1)S(1)}, u32[]{:S(2)}, u32[]{:S(2)}) %collective-permute-start.37) | collective-permute-done | bytes 442400 | tf_op jit(solution)/shard_map/ppermute | solution.py:501
  442.9 2.5 collective-permute-start.38
  446.1 4.1 collective-permute-done.68
  452.3 3.4 collective-permute-start.69
  455.7 3.9 collective-permute-done.38
  461.2 3.1 collective-permute-start.39
  467.4 3.7 collective-permute-done.53
  471.3 6.3 %collective-permute-done.58 = f32[16,768]{1,0:T(8,128)S(1)} collective-permute-done((f32[16,768]{1,0:T(8,128)S(1)}, f32[16,768]{1,0:T(8,128)S(1)}, u32[]{:S(2)}, u32[]{:S(2)}) %collective-permute-start.58) | collective-permute-done | bytes 49184 | tf_op jit(solution)/shard_map/ppermute | solution.py:501
  478.4 7.4 %collective-permute-done.10 = bf16[128,768]{1,0:T(8,128)(2,1)S(1)} collective-permute-done((bf16[128,768]{1,0:T(8,128)(2,1)S(1)}, bf16[128,768]{1,0:T(8,128)(2,1)S(1)}, u32[]{:S(2)}, u32[]{:S(2)}) %collective-permute-start.10) | collective-permute-done | bytes 196640 | tf_op jit(solution)/shard_map/ppermute | solution.py:501
  486.6 6.8 %collective-permute-done.11 = bf16[128,768]{1,0:T(8,128)(2,1)S(1)} collective-permute-done((bf16[128,768]{1,0:T(8,128)(2,1)S(1)}, bf16[128,768]{1,0:T(8,128)(2,1)S(1)}, u32[]{:S(2)}, u32[]{:S(2)}) %collective-permute-start.11) | collective-permute-done | bytes 196640 | tf_op jit(solution)/shard_map/ppermute | solution.py:501
  496.0 2.3 collective-permute-done.59
  503.1 5.6 %join.4 = f32[768,2304]{1,0:T(8,128)} custom-call(s32[1]{0:T(128)} %bitcast.52.b, bf16[384,2304]{1,0:T(8,128)(2,1)} %pad_maximum_fusion.2.refs_0_, bf16[384,2304]{1,0:T(8,128)(2,1)} %collective-permute-done.39.refs_1_), custom_call_target="tpu_custom_call" | custom-call | bytes 7077888 | tf_op jit(solution)/shard_map/join/pallas_call | solution.py:473
  508.6 6.9 %join.6 = f32[768,3072]{1,0:T(8,128)} custom-call(s32[1]{0:T(128)} %bitcast.52.b, bf16[384,3072]{1,0:T(8,128)(2,1)} %pad_maximum_fusion.refs_0_, bf16[384,3072]{1,0:T(8,128)(2,1)} %collective-permute-done.69.refs_1_), custom_call_target="tpu_custom_call" | custom-call | bytes 9437184 | tf_op jit(solution)/shard_map/join/pallas_call | solution.py:473
  515.5 6.5 %join.7 = f32[3072,768]{1,0:T(8,128)} custom-call(s32[1]{0:T(128)} %bitcast.52.b, bf16[1536,768]{1,0:T(8,128)(2,1)S(1)} %pad_maximum_fusion.1.refs_0_, bf16[1536,768]{1,0:T(8,128)(2,1)} %collective-permute-done.79.refs_1_), custom_call_target="tpu_custom_call" | custom-call | bytes 9437184 | tf_op jit(solution)/shard_map/join/pallas_call | solution.py:473
  (424 shorter events, 138.8 us)
Async XLA Ops:
  3.3 42.4 %collective-permute-start.3 = (bf16[128,768]{1,0:T(8,128)(2,1)}, bf16[128,768]{1,0:T(8,128)(2,1)S(1)}, u32[]{:S(2)}, u32[]{:S(2)}) collective-permute-start(bf16[128,768]{1,0:T(8,128)(2,1)} %get-tuple-element.135), channel_id=1, source_target_pairs={{0,1},{1,2},{2,3},{3,0},{4,5},{5,6},{6,7},{7,4},{8,9},{9,10},{10,1... | collective-permute-start | bytes 589832 | tf_op jit(solution)/shard_map/ppermute | solution.py:501
  6.3 60.2 %collective-permute-start.2 = (bf16[128,768]{1,0:T(8,128)(2,1)}, bf16[128,768]{1,0:T(8,128)(2,1)S(1)}, u32[]{:S(2)}, u32[]{:S(2)}) collective-permute-start(bf16[128,768]{1,0:T(8,128)(2,1)} %get-tuple-element.136), channel_id=1, source_target_pairs={{0,3},{1,0},{2,1},{3,2},{4,7},{5,4},{6,5},{7,6},{8,11},{9,8},{10,9... | collective-permute-start | bytes 589832 | tf_op jit(solution)/shard_map/ppermute | solution.py:501
  8.3 58.8 %collective-permute-start.1 = (bf16[128,768]{1,0:T(8,128)(2,1)}, bf16[128,768]{1,0:T(8,128)(2,1)}, u32[]{:S(2)}, u32[]{:S(2)}) collective-permute-start(bf16[128,768]{1,0:T(8,128)(2,1)} %get-tuple-element.137), channel_id=1, source_target_pairs={{0,2},{1,3},{2,0},{3,1},{4,6},{5,7},{6,4},{7,5},{8,10},{9,11},{10,... | collective-permute-start | bytes 589832 | tf_op jit(solution)/shard_map/ppermute | solution.py:501
  9.4 36.8 %collective-permute-start.5 = (bf16[128,768]{1,0:T(8,128)(2,1)S(1)}, bf16[128,768]{1,0:T(8,128)(2,1)S(1)}, u32[]{:S(2)}, u32[]{:S(2)}) collective-permute-start(bf16[128,768]{1,0:T(8,128)(2,1)S(1)} %get-tuple-element.140), channel_id=1, source_target_pairs={{0,3},{1,0},{2,1},{3,2},{4,7},{5,4},{6,5},{7,6},{8,11},{9,8},{10,9... | collective-permute-start | bytes 589832 | tf_op jit(solution)/shard_map/ppermute | solution.py:501
  10.7 36.1 %collective-permute-start.4 = (bf16[128,768]{1,0:T(8,128)(2,1)S(1)}, bf16[128,768]{1,0:T(8,128)(2,1)}, u32[]{:S(2)}, u32[]{:S(2)}) collective-permute-start(bf16[128,768]{1,0:T(8,128)(2,1)S(1)} %get-tuple-element.141), channel_id=1, source_target_pairs={{0,2},{1,3},{2,0},{3,1},{4,6},{5,7},{6,4},{7,5},{8,10},{9,11},{10,... | collective-permute-start | bytes 589832 | tf_op jit(solution)/shard_map/ppermute | solution.py:501
  45.7 23.1 %collective-permute-start = (bf16[128,768]{1,0:T(8,128)(2,1)S(1)}, bf16[128,768]{1,0:T(8,128)(2,1)S(1)}, u32[]{:S(2)}, u32[]{:S(2)}) collective-permute-start(bf16[128,768]{1,0:T(8,128)(2,1)S(1)} %get-tuple-element.138), channel_id=1, source_target_pairs={{0,1},{1,2},{2,3},{3,0},{4,5},{5,6},{6,7},{7,4},{8,9},{9,10},{10,1... | collective-permute-start | bytes 589832 | tf_op jit(solution)/shard_map/ppermute | solution.py:501
  46.1 86.7 %collective-permute-start.21 = (bf16[128,768]{1,0:T(8,128)(2,1)}, bf16[128,768]{1,0:T(8,128)(2,1)}, u32[]{:S(2)}, u32[]{:S(2)}) collective-permute-start(bf16[128,768]{1,0:T(8,128)(2,1)} %get-tuple-element.127), channel_id=1, source_target_pairs={{0,1},{1,2},{2,3},{3,0},{4,5},{5,6},{6,7},{7,4},{8,9},{9,10},{10,1... | collective-permute-start | bytes 589832 | tf_op jit(solution)/shard_map/ppermute | solution.py:501
  46.9 70.9 %collective-permute-start.20 = (bf16[128,768]{1,0:T(8,128)(2,1)}, bf16[128,768]{1,0:T(8,128)(2,1)}, u32[]{:S(2)}, u32[]{:S(2)}) collective-permute-start(bf16[128,768]{1,0:T(8,128)(2,1)} %get-tuple-element.128), channel_id=1, source_target_pairs={{0,3},{1,0},{2,1},{3,2},{4,7},{5,4},{6,5},{7,6},{8,11},{9,8},{10,9... | collective-permute-start | bytes 589832 | tf_op jit(solution)/shard_map/ppermute | solution.py:501
  66.5 51.9 %collective-permute-start.19 = (bf16[128,768]{1,0:T(8,128)(2,1)S(1)}, bf16[128,768]{1,0:T(8,128)(2,1)}, u32[]{:S(2)}, u32[]{:S(2)}) collective-permute-start(bf16[128,768]{1,0:T(8,128)(2,1)S(1)} %copy-done.74), channel_id=1, source_target_pairs={{0,2},{1,3},{2,0},{3,1},{4,6},{5,7},{6,4},{7,5},{8,10},{9,11},{10,... | collective-permute-start | bytes 589832 | tf_op jit(solution)/shard_map/ppermute | solution.py:501
  67.2 51.3 %collective-permute-start.18 = (bf16[128,768]{1,0:T(8,128)(2,1)S(1)}, bf16[128,768]{1,0:T(8,128)(2,1)}, u32[]{:S(2)}, u32[]{:S(2)}) collective-permute-start(bf16[128,768]{1,0:T(8,128)(2,1)S(1)} %copy-done.73), channel_id=1, source_target_pairs={{0,1},{1,2},{2,3},{3,0},{4,5},{5,6},{6,7},{7,4},{8,9},{9,10},{10,1... | collective-permute-start | bytes 589832 | tf_op jit(solution)/shard_map/ppermute | solution.py:501
  68.8 64.0 %collective-permute-start.23 = (bf16[128,768]{1,0:T(8,128)(2,1)S(1)}, bf16[128,768]{1,0:T(8,128)(2,1)}, u32[]{:S(2)}, u32[]{:S(2)}) collective-permute-start(bf16[128,768]{1,0:T(8,128)(2,1)S(1)} %copy-done.72), channel_id=1, source_target_pairs={{0,3},{1,0},{2,1},{3,2},{4,7},{5,4},{6,5},{7,6},{8,11},{9,8},{10,9... | collective-permute-start | bytes 589832 | tf_op jit(solution)/shard_map/ppermute | solution.py:501
  117.8 15.0 %collective-permute-start.22 = (bf16[128,768]{1,0:T(8,128)(2,1)S(1)}, bf16[128,768]{1,0:T(8,128)(2,1)}, u32[]{:S(2)}, u32[]{:S(2)}) collective-permute-start(bf16[128,768]{1,0:T(8,128)(2,1)S(1)} %copy-done.71), channel_id=1, source_target_pairs={{0,2},{1,3},{2,0},{3,1},{4,6},{5,7},{6,4},{7,5},{8,10},{9,11},{10,... | collective-permute-start | bytes 589832 | tf_op jit(solution)/shard_map/ppermute | solution.py:501
  169.3 59.4 %collective-permute-start.12 = (f32[128]{0:T(128)S(1)}, f32[128]{0:T(128)S(1)}, u32[]{:S(2)}, u32[]{:S(2)}) collective-permute-start(f32[128]{0:T(128)S(1)} %get-tuple-element.204), channel_id=1, source_target_pairs={{0,3},{1,0},{2,1},{3,2},{4,7},{5,4},{6,5},{7,6},{8,11},{9,8},{10,9... | collective-permute-start | bytes 1544 | tf_op jit(solution)/shard_map/ppermute | solution.py:501
  188.1 43.0 %collective-permute-start.15 = (f32[128]{0:T(128)}, f32[128]{0:T(128)}, u32[]{:S(2)}, u32[]{:S(2)}) collective-permute-start(f32[128]{0:T(128)} %get-tuple-element.199), channel_id=1, source_target_pairs={{0,2},{1,3},{2,0},{3,1},{4,6},{5,7},{6,4},{7,5},{8,10},{9,11},{10,... | collective-permute-start | bytes 1544 | tf_op jit(solution)/shard_map/ppermute | solution.py:501
  205.8 6.8 %collective-permute-start.40 = (f32[8,768]{1,0:T(8,128)S(1)}, f32[8,768]{1,0:T(8,128)S(1)}, u32[]{:S(2)}, u32[]{:S(2)}) collective-permute-start(f32[8,768]{1,0:T(8,128)S(1)} %add.542), channel_id=1, source_target_pairs={{0,4},{1,5},{2,6},{3,7},{4,0},{5,1},{6,2},{7,3},{8,12},{9,13},{10,... | collective-permute-start | bytes 73736 | tf_op jit(solution)/shard_map/ppermute | solution.py:501
  205.9 15.4 %collective-permute-start.55 = (f32[16,768]{1,0:T(8,128)S(1)}, f32[16,768]{1,0:T(8,128)S(1)}, u32[]{:S(2)}, u32[]{:S(2)}) collective-permute-start(f32[16,768]{1,0:T(8,128)S(1)} %pad_maximum_fusion.20), channel_id=1, source_target_pairs={{0,4},{1,5},{2,6},{3,7},{4,0},{5,1},{6,2},{7,3},{8,12},{9,13},{10,... | collective-permute-start | bytes 147464 | tf_op jit(solution)/shard_map/ppermute | solution.py:501
  215.8 10.5 %collective-permute-start.14 = (f32[128]{0:T(128)S(1)}, f32[128]{0:T(128)S(1)}, u32[]{:S(2)}, u32[]{:S(2)}) collective-permute-start(f32[128]{0:T(128)S(1)} %get-tuple-element.203), channel_id=1, source_target_pairs={{0,2},{1,3},{2,0},{3,1},{4,6},{5,7},{6,4},{7,5},{8,10},{9,11},{10,... | collective-permute-start | bytes 1544 | tf_op jit(solution)/shard_map/ppermute | solution.py:501
  221.2 29.1 %collective-permute-start.45 = (bf16[384,768]{1,0:T(8,128)(2,1)}, bf16[384,768]{1,0:T(8,128)(2,1)S(1)}, u32[]{:S(2)}, u32[]{:S(2)}) collective-permute-start(bf16[384,768]{1,0:T(8,128)(2,1)} %weight_grad.11), channel_id=1, source_target_pairs={{0,4},{1,5},{2,6},{3,7},{4,0},{5,1},{6,2},{7,3},{8,12},{9,13},{10,... | collective-permute-start | bytes 1769480 | tf_op jit(solution)/shard_map/ppermute | solution.py:501
  225.2 15.4 %collective-permute-start.56 = (f32[16,768]{1,0:T(8,128)}, f32[16,768]{1,0:T(8,128)}, u32[]{:S(2)}, u32[]{:S(2)}) collective-permute-start(f32[16,768]{1,0:T(8,128)} %fusion.27), channel_id=1, source_target_pairs={{0,8},{1,9},{2,10},{3,11},{4,20},{5,21},{6,22},{7,23},{8,0},{9,1},... | collective-permute-start | bytes 147464 | tf_op jit(solution)/shard_map/ppermute | solution.py:501
  226.4 15.1 %collective-permute-start.44 = (f32[8,768]{1,0:T(8,128)}, f32[8,768]{1,0:T(8,128)}, u32[]{:S(2)}, u32[]{:S(2)}) collective-permute-start(f32[8,768]{1,0:T(8,128)} %add.546), channel_id=1, source_target_pairs={{0,2},{1,3},{2,0},{3,1},{4,6},{5,7},{6,4},{7,5},{8,10},{9,11},{10,... | collective-permute-start | bytes 73736 | tf_op jit(solution)/shard_map/ppermute | solution.py:501
  236.6 52.8 %collective-permute-start.28 = (bf16[128,768]{1,0:T(8,128)(2,1)}, bf16[128,768]{1,0:T(8,128)(2,1)}, u32[]{:S(2)}, u32[]{:S(2)}) collective-permute-start(bf16[128,768]{1,0:T(8,128)(2,1)} %get-tuple-element.159), channel_id=1, source_target_pairs={{0,1},{1,2},{2,3},{3,0},{4,5},{5,6},{6,7},{7,4},{8,9},{9,10},{10,1... | collective-permute-start | bytes 589832 | tf_op jit(solution)/shard_map/ppermute | solution.py:501
  238.3 8.9 %collective-permute-start.6 = (bf16[128,768]{1,0:T(8,128)(2,1)}, bf16[128,768]{1,0:T(8,128)(2,1)}, u32[]{:S(2)}, u32[]{:S(2)}) collective-permute-start(bf16[128,768]{1,0:T(8,128)(2,1)} %get-tuple-element.167), channel_id=1, source_target_pairs={{0,3},{1,0},{2,1},{3,2},{4,7},{5,4},{6,5},{7,6},{8,11},{9,8},{10,9... | collective-permute-start | bytes 589832 | tf_op jit(solution)/shard_map/ppermute | solution.py:501
  240.5 46.4 %collective-permute-start.30 = (bf16[384,2304]{1,0:T(8,128)(2,1)}, bf16[384,2304]{1,0:T(8,128)(2,1)S(1)}, u32[]{:S(2)}, u32[]{:S(2)}) collective-permute-start(bf16[384,2304]{1,0:T(8,128)(2,1)} %copy-done.23), channel_id=1, source_target_pairs={{0,4},{1,5},{2,6},{3,7},{4,0},{5,1},{6,2},{7,3},{8,12},{9,13},{10,... | collective-permute-start | bytes 5308424 | tf_op jit(solution)/shard_map/ppermute | solution.py:501
  245.6 21.9 %collective-permute-start.26 = (bf16[128,768]{1,0:T(8,128)(2,1)}, bf16[128,768]{1,0:T(8,128)(2,1)S(1)}, u32[]{:S(2)}, u32[]{:S(2)}) collective-permute-start(bf16[128,768]{1,0:T(8,128)(2,1)} %get-tuple-element.160), channel_id=1, source_target_pairs={{0,2},{1,3},{2,0},{3,1},{4,6},{5,7},{6,4},{7,5},{8,10},{9,11},{10,... | collective-permute-start | bytes 589832 | tf_op jit(solution)/shard_map/ppermute | solution.py:501
  247.2 11.7 %collective-permute-start.24 = (bf16[128,768]{1,0:T(8,128)(2,1)}, bf16[128,768]{1,0:T(8,128)(2,1)S(1)}, u32[]{:S(2)}, u32[]{:S(2)}) collective-permute-start(bf16[128,768]{1,0:T(8,128)(2,1)} %get-tuple-element.161), channel_id=1, source_target_pairs={{0,3},{1,0},{2,1},{3,2},{4,7},{5,4},{6,5},{7,6},{8,11},{9,8},{10,9... | collective-permute-start | bytes 589832 | tf_op jit(solution)/shard_map/ppermute | solution.py:501
  250.3 11.1 %collective-permute-start.25 = (bf16[128,768]{1,0:T(8,128)(2,1)}, bf16[128,768]{1,0:T(8,128)(2,1)S(1)}, u32[]{:S(2)}, u32[]{:S(2)}) collective-permute-start(bf16[128,768]{1,0:T(8,128)(2,1)} %get-tuple-element.158), channel_id=1, source_target_pairs={{0,3},{1,0},{2,1},{3,2},{4,7},{5,4},{6,5},{7,6},{8,11},{9,8},{10,9... | collective-permute-start | bytes 589832 | tf_op jit(solution)/shard_map/ppermute | solution.py:501
  258.8 6.7 %collective-permute-start.46 = (bf16[192,768]{1,0:T(8,128)(2,1)S(1)}, bf16[192,768]{1,0:T(8,128)(2,1)S(1)}, u32[]{:S(2)}, u32[]{:S(2)}) collective-permute-start(bf16[192,768]{1,0:T(8,128)(2,1)S(1)} %get-tuple-element.151), channel_id=1, source_target_pairs={{0,8},{1,9},{2,10},{3,11},{4,20},{5,21},{6,22},{7,23},{8,0},{9,1},... | collective-permute-start | bytes 884744 | tf_op jit(solution)/shard_map/ppermute | solution.py:501
  261.4 205.3 %collective-permute-start.8 = (bf16[128,768]{1,0:T(8,128)(2,1)S(1)}, bf16[128,768]{1,0:T(8,128)(2,1)S(1)}, u32[]{:S(2)}, u32[]{:S(2)}) collective-permute-start(bf16[128,768]{1,0:T(8,128)(2,1)S(1)} %copy-done.65), channel_id=1, source_target_pairs={{0,2},{1,3},{2,0},{3,1},{4,6},{5,7},{6,4},{7,5},{8,10},{9,11},{10,... | collective-permute-start | bytes 589832 | tf_op jit(solution)/shard_map/ppermute | solution.py:501
  265.6 17.0 %collective-permute-start.27 = (bf16[128,768]{1,0:T(8,128)(2,1)S(1)}, bf16[128,768]{1,0:T(8,128)(2,1)S(1)}, u32[]{:S(2)}, u32[]{:S(2)}) collective-permute-start(bf16[128,768]{1,0:T(8,128)(2,1)S(1)} %copy-done.70), channel_id=1, source_target_pairs={{0,2},{1,3},{2,0},{3,1},{4,6},{5,7},{6,4},{7,5},{8,10},{9,11},{10,... | collective-permute-start | bytes 589832 | tf_op jit(solution)/shard_map/ppermute | solution.py:501
  272.8 40.8 %collective-permute-start.70 = (bf16[1536,768]{1,0:T(8,128)(2,1)}, bf16[1536,768]{1,0:T(8,128)(2,1)S(1)}, u32[]{:S(2)}, u32[]{:S(2)}) collective-permute-start(bf16[1536,768]{1,0:T(8,128)(2,1)} %copy-done.22), channel_id=1, source_target_pairs={{0,4},{1,5},{2,6},{3,7},{4,0},{5,1},{6,2},{7,3},{8,12},{9,13},{10,... | collective-permute-start | bytes 7077896 | tf_op jit(solution)/shard_map/ppermute | solution.py:501
  287.0 36.6 %collective-permute-start.60 = (bf16[384,3072]{1,0:T(8,128)(2,1)S(1)}, bf16[384,3072]{1,0:T(8,128)(2,1)S(1)}, u32[]{:S(2)}, u32[]{:S(2)}) collective-permute-start(bf16[384,3072]{1,0:T(8,128)(2,1)S(1)} %copy-done.21), channel_id=1, source_target_pairs={{0,4},{1,5},{2,6},{3,7},{4,0},{5,1},{6,2},{7,3},{8,12},{9,13},{10,... | collective-permute-start | bytes 7077896 | tf_op jit(solution)/shard_map/ppermute | solution.py:501
  289.4 17.7 %collective-permute-start.31 = (bf16[192,2304]{1,0:T(8,128)(2,1)S(1)}, bf16[192,2304]{1,0:T(8,128)(2,1)S(1)}, u32[]{:S(2)}, u32[]{:S(2)}) collective-permute-start(bf16[192,2304]{1,0:T(8,128)(2,1)S(1)} %get-tuple-element.113), channel_id=1, source_target_pairs={{0,8},{1,9},{2,10},{3,11},{4,20},{5,21},{6,22},{7,23},{8,0},{9,1},... | collective-permute-start | bytes 2654216 | tf_op jit(solution)/shard_map/ppermute | solution.py:501
  292.7 7.9 %collective-permute-start.29 = (bf16[128,768]{1,0:T(8,128)(2,1)S(1)}, bf16[128,768]{1,0:T(8,128)(2,1)S(1)}, u32[]{:S(2)}, u32[]{:S(2)}) collective-permute-start(bf16[128,768]{1,0:T(8,128)(2,1)S(1)} %copy-done.69), channel_id=1, source_target_pairs={{0,1},{1,2},{2,3},{3,0},{4,5},{5,6},{6,7},{7,4},{8,9},{9,10},{10,1... | collective-permute-start | bytes 589832 | tf_op jit(solution)/shard_map/ppermute | solution.py:501
  305.6 158.8 %collective-permute-start.7 = (bf16[128,768]{1,0:T(8,128)(2,1)S(1)}, bf16[128,768]{1,0:T(8,128)(2,1)S(1)}, u32[]{:S(2)}, u32[]{:S(2)}) collective-permute-start(bf16[128,768]{1,0:T(8,128)(2,1)S(1)} %copy-done.68), channel_id=1, source_target_pairs={{0,3},{1,0},{2,1},{3,2},{4,7},{5,4},{6,5},{7,6},{8,11},{9,8},{10,9... | collective-permute-start | bytes 589832 | tf_op jit(solution)/shard_map/ppermute | solution.py:501
  312.0 10.3 %collective-permute-start.32 = (bf16[96,2304]{1,0:T(8,128)(2,1)S(1)}, bf16[96,2304]{1,0:T(8,128)(2,1)S(1)}, u32[]{:S(2)}, u32[]{:S(2)}) collective-permute-start(bf16[96,2304]{1,0:T(8,128)(2,1)S(1)} %get-tuple-element.125), channel_id=1, source_target_pairs={{0,16},{1,17},{2,18},{3,19},{4,12},{5,13},{6,14},{7,15},{8,24},{9,... | collective-permute-start | bytes 1327112 | tf_op jit(solution)/shard_map/ppermute | solution.py:501
  313.6 17.8 %collective-permute-start.52 = (bf16[96,768]{1,0:T(8,128)(2,1)S(1)}, bf16[96,768]{1,0:T(8,128)(2,1)S(1)}, u32[]{:S(2)}, u32[]{:S(2)}) collective-permute-start(bf16[96,768]{1,0:T(8,128)(2,1)S(1)} %pad_maximum_fusion.18), channel_id=1, source_target_pairs={{0,16},{1,17},{2,18},{3,19},{4,12},{5,13},{6,14},{7,15},{8,24},{9,... | collective-permute-start | bytes 442376 | tf_op jit(solution)/shard_map/ppermute | solution.py:501
  322.3 17.0 %collective-permute-start.71 = (bf16[768,768]{1,0:T(8,128)(2,1)S(1)}, bf16[768,768]{1,0:T(8,128)(2,1)S(1)}, u32[]{:S(2)}, u32[]{:S(2)}) collective-permute-start(bf16[768,768]{1,0:T(8,128)(2,1)S(1)} %get-tuple-element.109), channel_id=1, source_target_pairs={{0,8},{1,9},{2,10},{3,11},{4,20},{5,21},{6,22},{7,23},{8,0},{9,1},... | collective-permute-start | bytes 3538952 | tf_op jit(solution)/shard_map/ppermute | solution.py:501
  323.6 6.6 %collective-permute-start.33 = (bf16[48,2304]{1,0:T(8,128)(2,1)S(1)}, bf16[48,2304]{1,0:T(8,128)(2,1)S(1)}, u32[]{:S(2)}, u32[]{:S(2)}) collective-permute-start(bf16[48,2304]{1,0:T(8,128)(2,1)S(1)} %get-tuple-element.155), channel_id=1, source_target_pairs={{0,1},{1,0},{2,3},{3,2},{4,5},{5,4},{6,7},{7,6},{8,9},{9,8},{10,11... | collective-permute-start | bytes 663560 | tf_op jit(solution)/shard_map/ppermute | solution.py:501
  330.2 30.4 %collective-permute-start.61 = (bf16[192,3072]{1,0:T(8,128)(2,1)S(1)}, bf16[192,3072]{1,0:T(8,128)(2,1)S(1)}, u32[]{:S(2)}, u32[]{:S(2)}) collective-permute-start(bf16[192,3072]{1,0:T(8,128)(2,1)S(1)} %get-tuple-element.111), channel_id=1, source_target_pairs={{0,8},{1,9},{2,10},{3,11},{4,20},{5,21},{6,22},{7,23},{8,0},{9,1},... | collective-permute-start | bytes 3538952 | tf_op jit(solution)/shard_map/ppermute | solution.py:501
  337.6 24.9 %collective-permute-start.35 = (bf16[24,2304]{1,0:T(8,128)(2,1)S(1)}, bf16[24,2304]{1,0:T(8,128)(2,1)S(1)}, u32[]{:S(2)}, u32[]{:S(2)}) collective-permute-start(bf16[24,2304]{1,0:T(8,128)(2,1)S(1)} %fusion.12), channel_id=1, source_target_pairs={{0,2},{1,3},{2,0},{3,1},{4,6},{5,7},{6,4},{7,5},{8,10},{9,11},{10,... | collective-permute-start | bytes 331784 | tf_op jit(solution)/shard_map/ppermute | solution.py:501
  339.6 23.0 %collective-permute-start.72 = (bf16[384,768]{1,0:T(8,128)(2,1)S(1)}, bf16[384,768]{1,0:T(8,128)(2,1)S(1)}, u32[]{:S(2)}, u32[]{:S(2)}) collective-permute-start(bf16[384,768]{1,0:T(8,128)(2,1)S(1)} %get-tuple-element.117), channel_id=1, source_target_pairs={{0,16},{1,17},{2,18},{3,19},{4,12},{5,13},{6,14},{7,15},{8,24},{9,... | collective-permute-start | bytes 1769480 | tf_op jit(solution)/shard_map/ppermute | solution.py:501
  361.0 9.9 %collective-permute-start.62 = (bf16[96,3072]{1,0:T(8,128)(2,1)S(1)}, bf16[96,3072]{1,0:T(8,128)(2,1)S(1)}, u32[]{:S(2)}, u32[]{:S(2)}) collective-permute-start(bf16[96,3072]{1,0:T(8,128)(2,1)S(1)} %get-tuple-element.121), channel_id=1, source_target_pairs={{0,16},{1,17},{2,18},{3,19},{4,12},{5,13},{6,14},{7,15},{8,24},{9,... | collective-permute-start | bytes 1769480 | tf_op jit(solution)/shard_map/ppermute | solution.py:501
  362.5 9.6 %collective-permute-start.36 = (bf16[48,2304]{1,0:T(8,128)(2,1)S(1)}, bf16[48,2304]{1,0:T(8,128)(2,1)S(1)}, u32[]{:S(2)}, u32[]{:S(2)}) collective-permute-start(bf16[48,2304]{1,0:T(8,128)(2,1)S(1)} %pad_maximum_fusion.17), channel_id=1, source_target_pairs={{0,1},{1,0},{2,3},{3,2},{4,5},{5,4},{6,7},{7,6},{8,9},{9,8},{10,11... | collective-permute-start | bytes 663560 | tf_op jit(solution)/shard_map/ppermute | solution.py:501
  362.7 13.7 %collective-permute-start.73 = (bf16[192,768]{1,0:T(8,128)(2,1)S(1)}, bf16[192,768]{1,0:T(8,128)(2,1)S(1)}, u32[]{:S(2)}, u32[]{:S(2)}) collective-permute-start(bf16[192,768]{1,0:T(8,128)(2,1)S(1)} %get-tuple-element.145), channel_id=1, source_target_pairs={{0,1},{1,0},{2,3},{3,2},{4,5},{5,4},{6,7},{7,6},{8,9},{9,8},{10,11... | collective-permute-start | bytes 884744 | tf_op jit(solution)/shard_map/ppermute | solution.py:501
  371.1 9.7 %collective-permute-start.63 = (bf16[48,3072]{1,0:T(8,128)(2,1)S(1)}, bf16[48,3072]{1,0:T(8,128)(2,1)S(1)}, u32[]{:S(2)}, u32[]{:S(2)}) collective-permute-start(bf16[48,3072]{1,0:T(8,128)(2,1)S(1)} %get-tuple-element.149), channel_id=1, source_target_pairs={{0,1},{1,0},{2,3},{3,2},{4,5},{5,4},{6,7},{7,6},{8,9},{9,8},{10,11... | collective-permute-start | bytes 884744 | tf_op jit(solution)/shard_map/ppermute | solution.py:501
  376.4 13.5 %collective-permute-start.74 = (bf16[96,768]{1,0:T(8,128)(2,1)S(1)}, bf16[96,768]{1,0:T(8,128)(2,1)S(1)}, u32[]{:S(2)}, u32[]{:S(2)}) collective-permute-start(bf16[96,768]{1,0:T(8,128)(2,1)S(1)} %fusion.17), channel_id=1, source_target_pairs={{0,2},{1,3},{2,0},{3,1},{4,6},{5,7},{6,4},{7,5},{8,10},{9,11},{10,... | collective-permute-start | bytes 442376 | tf_op jit(solution)/shard_map/ppermute | solution.py:501
  380.8 12.8 %collective-permute-start.64 = (bf16[24,3072]{1,0:T(8,128)(2,1)S(1)}, bf16[24,3072]{1,0:T(8,128)(2,1)S(1)}, u32[]{:S(2)}, u32[]{:S(2)}) collective-permute-start(bf16[24,3072]{1,0:T(8,128)(2,1)S(1)} %fusion.15), channel_id=1, source_target_pairs={{0,2},{1,3},{2,0},{3,1},{4,6},{5,7},{6,4},{7,5},{8,10},{9,11},{10,... | collective-permute-start | bytes 442376 | tf_op jit(solution)/shard_map/ppermute | solution.py:501
  390.0 8.1 %collective-permute-start.75 = (bf16[96,768]{1,0:T(8,128)(2,1)S(1)}, bf16[96,768]{1,0:T(8,128)(2,1)S(1)}, u32[]{:S(2)}, u32[]{:S(2)}) collective-permute-start(bf16[96,768]{1,0:T(8,128)(2,1)S(1)} %fusion.9), channel_id=1, source_target_pairs={{0,2},{1,3},{2,0},{3,1},{4,6},{5,7},{6,4},{7,5},{8,10},{9,11},{10,... | collective-permute-start | bytes 442376 | tf_op jit(solution)/shard_map/ppermute | solution.py:501
  398.2 8.8 %collective-permute-start.76 = (bf16[192,768]{1,0:T(8,128)(2,1)S(1)}, bf16[192,768]{1,0:T(8,128)(2,1)S(1)}, u32[]{:S(2)}, u32[]{:S(2)}) collective-permute-start(bf16[192,768]{1,0:T(8,128)(2,1)S(1)} %pad_maximum_fusion.16), channel_id=1, source_target_pairs={{0,1},{1,0},{2,3},{3,2},{4,5},{5,4},{6,7},{7,6},{8,9},{9,8},{10,11... | collective-permute-start | bytes 884744 | tf_op jit(solution)/shard_map/ppermute | solution.py:501
  399.9 10.3 %collective-permute-start.66 = (bf16[48,3072]{1,0:T(8,128)(2,1)S(1)}, bf16[48,3072]{1,0:T(8,128)(2,1)S(1)}, u32[]{:S(2)}, u32[]{:S(2)}) collective-permute-start(bf16[48,3072]{1,0:T(8,128)(2,1)S(1)} %pad_maximum_fusion.15), channel_id=1, source_target_pairs={{0,1},{1,0},{2,3},{3,2},{4,5},{5,4},{6,7},{7,6},{8,9},{9,8},{10,11... | collective-permute-start | bytes 884744 | tf_op jit(solution)/shard_map/ppermute | solution.py:501
  407.1 13.4 %collective-permute-start.77 = (bf16[384,768]{1,0:T(8,128)(2,1)S(1)}, bf16[384,768]{1,0:T(8,128)(2,1)S(1)}, u32[]{:S(2)}, u32[]{:S(2)}) collective-permute-start(bf16[384,768]{1,0:T(8,128)(2,1)S(1)} %pad_maximum_fusion.12), channel_id=1, source_target_pairs={{0,16},{1,17},{2,18},{3,19},{4,12},{5,13},{6,14},{7,15},{8,24},{9,... | collective-permute-start | bytes 1769480 | tf_op jit(solution)/shard_map/ppermute | solution.py:501
  410.3 22.8 %collective-permute-start.67 = (bf16[96,3072]{1,0:T(8,128)(2,1)S(1)}, bf16[96,3072]{1,0:T(8,128)(2,1)S(1)}, u32[]{:S(2)}, u32[]{:S(2)}) collective-permute-start(bf16[96,3072]{1,0:T(8,128)(2,1)S(1)} %pad_maximum_fusion.11), channel_id=1, source_target_pairs={{0,16},{1,17},{2,18},{3,19},{4,12},{5,13},{6,14},{7,15},{8,24},{9,... | collective-permute-start | bytes 1769480 | tf_op jit(solution)/shard_map/ppermute | solution.py:501
  412.2 30.5 %collective-permute-start.37 = (bf16[96,2304]{1,0:T(8,128)(2,1)S(1)}, bf16[96,2304]{1,0:T(8,128)(2,1)S(1)}, u32[]{:S(2)}, u32[]{:S(2)}) collective-permute-start(bf16[96,2304]{1,0:T(8,128)(2,1)S(1)} %pad_maximum_fusion.13), channel_id=1, source_target_pairs={{0,16},{1,17},{2,18},{3,19},{4,12},{5,13},{6,14},{7,15},{8,24},{9,... | collective-permute-start | bytes 1327112 | tf_op jit(solution)/shard_map/ppermute | solution.py:501
  420.8 24.5 %collective-permute-start.78 = (bf16[768,768]{1,0:T(8,128)(2,1)S(1)}, bf16[768,768]{1,0:T(8,128)(2,1)S(1)}, u32[]{:S(2)}, u32[]{:S(2)}) collective-permute-start(bf16[768,768]{1,0:T(8,128)(2,1)S(1)} %pad_maximum_fusion.4), channel_id=1, source_target_pairs={{0,8},{1,9},{2,10},{3,11},{4,20},{5,21},{6,22},{7,23},{8,0},{9,1},... | collective-permute-start | bytes 3538952 | tf_op jit(solution)/shard_map/ppermute | solution.py:501
  433.5 16.6 %collective-permute-start.68 = (bf16[192,3072]{1,0:T(8,128)(2,1)S(1)}, bf16[192,3072]{1,0:T(8,128)(2,1)S(1)}, u32[]{:S(2)}, u32[]{:S(2)}) collective-permute-start(bf16[192,3072]{1,0:T(8,128)(2,1)S(1)} %pad_maximum_fusion.3), channel_id=1, source_target_pairs={{0,8},{1,9},{2,10},{3,11},{4,20},{5,21},{6,22},{7,23},{8,0},{9,1},... | collective-permute-start | bytes 3538952 | tf_op jit(solution)/shard_map/ppermute | solution.py:501
  442.9 16.7 %collective-permute-start.38 = (bf16[192,2304]{1,0:T(8,128)(2,1)S(1)}, bf16[192,2304]{1,0:T(8,128)(2,1)S(1)}, u32[]{:S(2)}, u32[]{:S(2)}) collective-permute-start(bf16[192,2304]{1,0:T(8,128)(2,1)S(1)} %pad_maximum_fusion.5), channel_id=1, source_target_pairs={{0,8},{1,9},{2,10},{3,11},{4,20},{5,21},{6,22},{7,23},{8,0},{9,1},... | collective-permute-start | bytes 2654216 | tf_op jit(solution)/shard_map/ppermute | solution.py:501
  446.0 69.5 %collective-permute-start.79 = (bf16[1536,768]{1,0:T(8,128)(2,1)S(1)}, bf16[1536,768]{1,0:T(8,128)(2,1)}, u32[]{:S(2)}, u32[]{:S(2)}) collective-permute-start(bf16[1536,768]{1,0:T(8,128)(2,1)S(1)} %pad_maximum_fusion.1.refs_0_), channel_id=1, source_target_pairs={{0,4},{1,5},{2,6},{3,7},{4,0},{5,1},{6,2},{7,3},{8,12},{9,13},{10,... | collective-permute-start | bytes 7077896 | tf_op jit(solution)/shard_map/ppermute | solution.py:501
  452.3 56.3 %collective-permute-start.69 = (bf16[384,3072]{1,0:T(8,128)(2,1)}, bf16[384,3072]{1,0:T(8,128)(2,1)}, u32[]{:S(2)}, u32[]{:S(2)}) collective-permute-start(bf16[384,3072]{1,0:T(8,128)(2,1)} %pad_maximum_fusion.refs_0_), channel_id=1, source_target_pairs={{0,4},{1,5},{2,6},{3,7},{4,0},{5,1},{6,2},{7,3},{8,12},{9,13},{10,... | collective-permute-start | bytes 7077896 | tf_op jit(solution)/shard_map/ppermute | solution.py:501
  461.2 41.8 %collective-permute-start.39 = (bf16[384,2304]{1,0:T(8,128)(2,1)}, bf16[384,2304]{1,0:T(8,128)(2,1)}, u32[]{:S(2)}, u32[]{:S(2)}) collective-permute-start(bf16[384,2304]{1,0:T(8,128)(2,1)} %pad_maximum_fusion.2.refs_0_), channel_id=1, source_target_pairs={{0,4},{1,5},{2,6},{3,7},{4,0},{5,1},{6,2},{7,3},{8,12},{9,13},{10,... | collective-permute-start | bytes 5308424 | tf_op jit(solution)/shard_map/ppermute | solution.py:501
  464.4 6.8 %collective-permute-start.53 = (bf16[192,768]{1,0:T(8,128)(2,1)S(1)}, bf16[192,768]{1,0:T(8,128)(2,1)S(1)}, u32[]{:S(2)}, u32[]{:S(2)}) collective-permute-start(bf16[192,768]{1,0:T(8,128)(2,1)S(1)} %pad_maximum_fusion.14), channel_id=1, source_target_pairs={{0,8},{1,9},{2,10},{3,11},{4,20},{5,21},{6,22},{7,23},{8,0},{9,1},... | collective-permute-start | bytes 884744 | tf_op jit(solution)/shard_map/ppermute | solution.py:501
  466.7 11.0 %collective-permute-start.9 = (bf16[128,768]{1,0:T(8,128)(2,1)S(1)}, bf16[128,768]{1,0:T(8,128)(2,1)S(1)}, u32[]{:S(2)}, u32[]{:S(2)}) collective-permute-start(bf16[128,768]{1,0:T(8,128)(2,1)S(1)} %copy-done.67), channel_id=1, source_target_pairs={{0,2},{1,3},{2,0},{3,1},{4,6},{5,7},{6,4},{7,5},{8,10},{9,11},{10,... | collective-permute-start | bytes 589832 | tf_op jit(solution)/shard_map/ppermute | solution.py:501
  477.6 8.2 %collective-permute-start.10 = (bf16[128,768]{1,0:T(8,128)(2,1)S(1)}, bf16[128,768]{1,0:T(8,128)(2,1)S(1)}, u32[]{:S(2)}, u32[]{:S(2)}) collective-permute-start(bf16[128,768]{1,0:T(8,128)(2,1)S(1)} %copy-done.64), channel_id=1, source_target_pairs={{0,1},{1,2},{2,3},{3,0},{4,5},{5,6},{6,7},{7,4},{8,9},{9,10},{10,1... | collective-permute-start | bytes 589832 | tf_op jit(solution)/shard_map/ppermute | solution.py:501
  477.6 23.5 %collective-permute-start.54 = (bf16[384,768]{1,0:T(8,128)(2,1)S(1)}, bf16[384,768]{1,0:T(8,128)(2,1)S(1)}, u32[]{:S(2)}, u32[]{:S(2)}) collective-permute-start(bf16[384,768]{1,0:T(8,128)(2,1)S(1)} %pad_maximum_fusion.10.refs_0_), channel_id=1, source_target_pairs={{0,4},{1,5},{2,6},{3,7},{4,0},{5,1},{6,2},{7,3},{8,12},{9,13},{10,... | collective-permute-start | bytes 1769480 | tf_op jit(solution)/shard_map/ppermute | solution.py:501
  485.9 7.5 %collective-permute-start.11 = (bf16[128,768]{1,0:T(8,128)(2,1)S(1)}, bf16[128,768]{1,0:T(8,128)(2,1)S(1)}, u32[]{:S(2)}, u32[]{:S(2)}) collective-permute-start(bf16[128,768]{1,0:T(8,128)(2,1)S(1)} %copy-done.66), channel_id=1, source_target_pairs={{0,1},{1,2},{2,3},{3,0},{4,5},{5,6},{6,7},{7,4},{8,9},{9,10},{10,1... | collective-permute-start | bytes 589832 | tf_op jit(solution)/shard_map/ppermute | solution.py:501
  (106 other events, 901.6 us)

commit v3 on v2

v3 whole, which is shorter than its diff:
```python
import functools

import jax
import jax.numpy as jnp
from jax import lax
from jax.experimental import pallas as pl
from jax.experimental.pallas import tpu as pltpu
from jax.sharding import PartitionSpec as P

HD = 64
PACK = 16
AXES = ("batch", "blk")
epsilon = 1e-06
masked_score = -1e30
f32 = jnp.float32
bf16 = jnp.bfloat16
NT = (((1,), (1,)), ((), ()))
TN = (((0,), (0,)), ((), ()))

(
    V_QUERY,
    V_VALUE,
    V_OUT,
    V_GAIN1,
    V_SHIFT1,
    V_DOWN,
    V_GAIN2,
    V_SHIFT2,
    V_HEAD,
    V_HEAD_BIAS,
    V_UP,
) = range(11)


def dot(left, right, dims=None):
    if dims is None:
        return jnp.dot(left, right, preferred_element_type=f32)
    return lax.dot_general(left, right, dims, preferred_element_type=f32)


def call_params(mebibytes):
    return pltpu.CompilerParams(vmem_limit_bytes=mebibytes * 2**20)


TIMES = {
    "attend": 11,
    "feed": 20,
    "feed_back": 18,
    "head_back": 2,
    "attend_back": 13,
    "weight_rows": 5,
    "weight_up": 5,
    "weight_qkv": 3,
}


class Order:
    def __init__(self):
        self.token = None

    def run(self, kernel, args, in_specs, out_specs, out_shape, grid, memory, name, **extra):
        prefetch = extra.pop("prefetch", 0)
        scratch = extra.pop("scratch", ())
        single = not isinstance(out_shape, list)
        if single:
            out_specs, out_shape = [out_specs], [out_shape]
        count, made = len(args), len(out_shape)
        tokens = [] if self.token is None else [self.token]

        def body(*refs):
            outs = refs[count + len(tokens) :]
            outs[made][...] = jnp.zeros((8, 128), f32)
            kernel(*refs[:count], *outs[:made], *outs[made + 1 :])

        results = pl.pallas_call(
            body,
            grid_spec=pltpu.PrefetchScalarGridSpec(
                num_scalar_prefetch=prefetch,
                grid=grid,
                in_specs=list(in_specs) + [pl.BlockSpec(memory_space=pl.ANY)] * len(tokens),
                out_specs=list(out_specs) + [pl.BlockSpec((8, 128), lambda *i: (0, 0))],
                scratch_shapes=list(scratch),
            ),
            out_shape=list(out_shape) + [jax.ShapeDtypeStruct((8, 128), f32)],
            compiler_params=call_params(memory),
            cost_estimate=pl.CostEstimate(
                flops=int(TIMES.get(name, 1) * 1e10), bytes_accessed=1000, transcendentals=0
            ),
            name=name,
            **extra,
        )(*args, *tokens)
        self.token = results[-1]
        return results[0] if single else results[:-1]


def whole(array, buffers=None):
    spec = {} if buffers is None else {"pipeline_mode": pl.Buffered(buffers)}
    return pl.BlockSpec(array.shape, lambda *i: (0,) * array.ndim, **spec)


def in_vmem():
    return pl.BlockSpec(memory_space=pltpu.VMEM)


def in_hbm(array):
    return pltpu.with_memory_space_constraint(array, pltpu.HBM)


def column_sum(values):
    return jnp.sum(values, axis=0, keepdims=True)


def row_mean(values):
    return jnp.mean(values, axis=-1, keepdims=True)


def to_column(row, count):
    return jnp.transpose(jnp.broadcast_to(row, (128, count)))[:, 0:1]


def to_row(column, count):
    return jnp.transpose(jnp.broadcast_to(column, (count, 128)))[0:1, :]


def attend_kernel(nz, own_rows, row, lengths, *refs):
    blocks = refs[:nz]
    wq, wk, wv, vec = refs[nz : nz + 4]
    x_ref, q_ref, k_ref, v_ref, att_ref, p_ref, bias = refs[-7:]
    seg_len = blocks[0].shape[0]
    step = pl.program_id(0)
    width = q_ref.shape[1]

    @pl.when(step == 0)
    def _():
        z = lax.axis_index("blk")
        mine = z * own_rows + row
        cols, rows = [], []
        for k in range(nz):
            x_ref[pl.ds(k * seg_len, seg_len), :] = blocks[k][...]
            base = lax.rem(z + (nz - k), nz) * seg_len
            col = lax.broadcasted_iota(jnp.int32, (seg_len, 1), 0) + base
            lane = lax.broadcasted_iota(jnp.int32, (1, seg_len), 1) + base
            end = jnp.int32(0)
            doc_col, doc_row = jnp.zeros_like(col), jnp.zeros_like(lane)
            for p in range(lengths.shape[1]):
                end = end + lengths[mine, p]
                doc_col += (col >= end).astype(jnp.int32)
                doc_row += (lane >= end).astype(jnp.int32)
            cols.append(doc_col)
            rows.append(doc_row)
        for i in range(nz):
            for j in range(nz):
                bias[pl.ds(i * seg_len, seg_len), pl.ds(j * seg_len, seg_len)] = jnp.where(
                    cols[i] == rows[j], 0.0, masked_score
                ).astype(f32)

    x = x_ref[...]
    q_ref[...] = (dot(x, wq[...]) + vec[V_QUERY : V_QUERY + 1, :]).astype(bf16)
    k_ref[...] = dot(x, wk[...]).astype(bf16)
    v_ref[...] = (dot(x, wv[...]) + vec[V_VALUE : V_VALUE + 1, :]).astype(bf16)
    first = lax.broadcasted_iota(jnp.int32, (1, 2 * HD), 1) < HD
    for pair in range(width // (2 * HD)):
        cols = pl.ds(pair * 2 * HD, 2 * HD)
        q, k, v = q_ref[:, cols], k_ref[:, cols], v_ref[:, cols]
        outs = []
        for h in range(2):
            mine = first if h == 0 else jnp.logical_not(first)
            scaled = jnp.where(mine, q * jnp.asarray(HD**-0.5, bf16), jnp.zeros_like(q))
            scores = dot(scaled, k, NT) + bias[...]
            weights = jnp.exp(scores - jnp.max(scores, axis=1, keepdims=True))
            total = jnp.sum(weights, axis=1, keepdims=True)
            probs = (weights * (1.0 / total)).astype(bf16)
            p_ref[pair * 2 + h] = probs
            outs.append(dot(probs, v))
        att_ref[:, cols] = jnp.where(first, outs[0], outs[1]).astype(bf16)


def weight_columns(d, width, steps, part):
    return pl.BlockSpec((d, width), lambda j: (0, part * steps + j))


def attend(order, blocks, lengths, wqkv, vec, own_rows, row, before, width=256):
    seg_len, d = blocks[0].shape
    nz = len(blocks)
    n = nz * seg_len
    steps, heads = d // width, width // HD
    token = pl.BlockSpec((n, width), lambda j: (row, j))
    first = 1 + nz + 4
    return order.run(
        functools.partial(attend_kernel, nz, own_rows, row),
        [lengths, *blocks, *[in_hbm(wqkv)] * 3, vec, *before],
        [pl.BlockSpec(memory_space=pltpu.SMEM)]
        + [whole(b, 1) for b in blocks]
        + [weight_columns(d, width, steps, part) for part in range(3)]
        + [pl.BlockSpec((vec.shape[0], width), lambda j: (0, j))]
        + [pl.BlockSpec(memory_space=pl.ANY)] * len(before),
        [pl.BlockSpec((n, d), lambda j: (row, 0))]
        + [token] * 4
        + [pl.BlockSpec((heads, n, n), lambda j: (row * steps + j, 0, 0))],
        [jax.ShapeDtypeStruct((own_rows * n, d), bf16)] * 5
        + [pltpu.HBM((own_rows * d // HD, n, n), bf16)],
        (steps,),
        18,
        "attend",
        scratch=[pltpu.VMEM((n, n), f32)],
        input_output_aliases={first + i: i for i in range(len(before))},
    )


def attend_back_kernel(nz, steps, g_ref, wo, q_ref, k_ref, v_ref, att_ref, p_ref, wq, wk, wv, *refs):
    dp_ref, sums, acc, up_s = refs[-nz - 4 : -nz - 2] + refs[-2:]
    gh_refs = refs[-nz - 2 : -2]
    step = pl.program_id(0)
    width = q_ref.shape[1]

    def part(i):
        return pl.ds(pl.multiple_of((i * steps + step) * width, width), width)

    up_s[...] = dot(g_ref[...], wo[...], NT).astype(bf16)
    first = lax.broadcasted_iota(jnp.int32, (1, 2 * HD), 1) < HD
    scale = HD**-0.5
    grads = [[], [], []]
    for pair in range(width // (2 * HD)):
        cols = pl.ds(pair * 2 * HD, 2 * HD)
        q, k, v, up = q_ref[:, cols], k_ref[:, cols], v_ref[:, cols], up_s[:, cols]
        product = up.astype(f32) * att_ref[:, cols].astype(f32)
        dq, dk, dv = [], [], []
        for h in range(2):
            mine = first if h == 0 else jnp.logical_not(first)
            inner = jnp.sum(jnp.where(mine, product, 0.0), axis=1, keepdims=True)
            probs = p_ref[pair * 2 + h]
            dprobs = dot(jnp.where(mine, up, jnp.zeros_like(up)), v, NT)
            score_grad = (probs.astype(f32) * (dprobs - inner)).astype(bf16)
            dv.append(dot(probs, up, TN))
            dq.append(dot(score_grad, k))
            dk.append(dot(score_grad, q, TN))
        grads[0].append((jnp.where(first, dq[0], dq[1]) * scale).astype(bf16))
        grads[1].append((jnp.where(first, dk[0], dk[1]) * scale).astype(bf16))
        grads[2].append(jnp.where(first, dv[0], dv[1]).astype(bf16))
    grads = [jnp.concatenate(g, axis=1) for g in grads]
    total = 0
    for i, weight in enumerate((wq, wk, wv)):
        dp_ref[:, part(i)] = grads[i]
        total += dot(grads[i], weight[...], NT)
    sums[...] = jnp.zeros_like(sums)
    sums[0:1, :] = column_sum(grads[0].astype(f32))
    sums[1:2, :] = column_sum(grads[2].astype(f32))

    @pl.when(step == 0)
    def _():
        acc[...] = g_ref[...].astype(f32) + total

    @pl.when(step > 0)
    def _():
        acc[...] += total

    @pl.when(step == pl.num_programs(0) - 1)
    def _():
        seg_len = acc.shape[0] // nz
        for k in range(nz):
            gh_refs[k][0] = acc[pl.ds(k * seg_len, seg_len), :].astype(bf16)


def attend_back(order, g, wo, q, k, v, att, probs, wqkv, nz, own_rows, row, before, width=256):
    d = g.shape[1]
    n = g.shape[0] // own_rows
    steps, heads = d // width, width // HD
    seg_len = n // nz
    token = pl.BlockSpec((n, width), lambda j: (row, j))
    return order.run(
        functools.partial(attend_back_kernel, nz, steps),
        [g, wo, q, k, v, att, in_hbm(probs), *[in_hbm(wqkv)] * 3, *before],
        [
            pl.BlockSpec((n, d), lambda j: (row, 0), pipeline_mode=pl.Buffered(1)),
            pl.BlockSpec((width, d), lambda j: (j, 0)),
            token,
            token,
            token,
            token,
            pl.BlockSpec((heads, n, n), lambda j: (row * steps + j, 0, 0)),
        ]
        + [weight_columns(d, width, steps, i) for i in range(3)]
        + [pl.BlockSpec(memory_space=pl.ANY)] * len(before),
        [
            pl.BlockSpec((n, 3 * d), lambda j: (row, 0)),
            pl.BlockSpec((8, width), lambda j: (row, j)),
        ]
        + [pl.BlockSpec((1, seg_len, d), lambda j: (0, 0, 0))] * nz,
        [
            jax.ShapeDtypeStruct((own_rows * n, 3 * d), bf16),
            jax.ShapeDtypeStruct((own_rows * 8, d), f32),
        ]
        + [jax.ShapeDtypeStruct((1, seg_len, d), bf16)] * nz,
        (steps,),
        22,
        "attend_back",
        scratch=[pltpu.VMEM((n, d), f32), pltpu.VMEM((n, width), bf16)],
        input_output_aliases={10 + i: i for i in range(len(before))},
    )


def split_term(row):
    high = row.astype(bf16)
    rest = (row - high.astype(f32)).astype(bf16)
    return jnp.concatenate([high, rest, jnp.zeros((PACK - 2, row.shape[1]), bf16)], axis=0)


def join_term(rows):
    return rows[0:1].astype(f32) + rows[1:2].astype(f32)


def feed_kernel(nz, seg_len, x_ref, att_ref, wo, wu, wd, vec, *refs):
    act, slope, low, n1_ref, n2_ref, stats = refs[-nz - 6 : -nz]
    hid = refs[-nz:]
    n, d = x_ref.shape
    parts = act.shape[1] // d

    def row(i):
        return vec[i : i + 1, :]

    first_sum = x_ref[...].astype(f32) + dot(att_ref[...], wo[...]) + row(V_OUT)
    center = first_sum - row_mean(first_sum)
    scale1 = lax.rsqrt(row_mean(center * center) + epsilon)
    n1 = center * scale1
    n1_ref[...] = n1.astype(bf16)
    normed = n1 * row(V_GAIN1) + row(V_SHIFT1)
    normed_low = normed.astype(bf16)
    low[...] = normed_low
    second_sum = normed + row(V_DOWN)
    for c in range(parts):
        cols = pl.ds(c * d, d)
        gate = dot(normed_low, wu[:, cols]) + row(V_UP + c)
        below = 0.5 * (1.0 + lax.erf(gate * (0.5**0.5)))
        density = jnp.exp(-0.5 * gate * gate) * 0.3989422804014327
        active = (gate * below).astype(bf16)
        act[:, cols] = active
        slope[:, cols] = (below + gate * density).astype(bf16)
        second_sum += dot(active, wd[cols, :])
    center = second_sum - row_mean(second_sum)
    scale2 = lax.rsqrt(row_mean(center * center) + epsilon)
    n2 = center * scale2
    n2_ref[...] = n2.astype(bf16)
    final = n2 * row(V_GAIN2) + row(V_SHIFT2)
    logits = jnp.sum(final * row(V_HEAD), axis=1, keepdims=True) + vec[V_HEAD_BIAS, 0]
    term = jnp.maximum(logits, 0.0) + jnp.log1p(jnp.exp(-jnp.abs(logits)))
    count = n // seg_len
    for k in range(nz):

        @pl.when(lax.rem(pl.program_id(0), nz // count) == k // count)
        def _():
            rows = slice((k % count) * seg_len, (k % count + 1) * seg_len)
            hid[k][0, 0:seg_len, :] = final[rows].astype(bf16)
            hid[k][0, seg_len:, 0:seg_len] = split_term(to_row(term[rows], seg_len))

    lane = lax.broadcasted_iota(jnp.int32, (1, 128), 1)
    stats[...] = jnp.where(lane == 0, scale1, jnp.where(lane == 1, scale2, logits))


def feed(order, x, att, wo, wu, wd, vec, nz, own_rows):
    d = x.shape[1]
    n = x.shape[0] // own_rows
    seg_len = n // nz
    tile = seg_len * max(1, nz // 2)
    per_row = n // tile
    hidden = wu.shape[1]
    token = pl.BlockSpec((tile, d), lambda i: (i, 0))
    wide = pl.BlockSpec((tile, hidden), lambda i: (i, 0))
    total = own_rows * n
    return order.run(
        functools.partial(feed_kernel, nz, seg_len),
        [x, att, wo, wu, wd, vec],
        [token, token, in_vmem(), in_vmem(), in_vmem(), whole(vec, 1)],
        [wide, wide, token, token, token, pl.BlockSpec((tile, 128), lambda i: (i, 0))]
        + [pl.BlockSpec((1, seg_len + PACK, d), lambda i: (i // per_row, 0, 0))] * nz,
        [
            pltpu.HBM((total, hidden), bf16),
            pltpu.HBM((total, hidden), bf16),
            jax.ShapeDtypeStruct((total, d), bf16),
            jax.ShapeDtypeStruct((total, d), bf16),
            jax.ShapeDtypeStruct((total, d), bf16),
            jax.ShapeDtypeStruct((total, 128), f32),
        ]
        + [jax.ShapeDtypeStruct((own_rows, seg_len + PACK, d), bf16)] * nz,
        (total // tile,),
        22,
        "feed",
    )


def head_back_kernel(nz, n2_ref, stats, vec, *refs):
    cots, fg, sums = refs[:nz], refs[nz], refs[nz + 1]
    d = fg.shape[1]
    seg_len = fg.shape[0] // nz

    def row(i):
        return vec[i : i + 1, :]

    total = jnp.zeros(sums.shape, f32)
    for k in range(nz):
        tokens = pl.ds(k * seg_len, seg_len)
        n2 = n2_ref[tokens, :].astype(f32)
        scale2, logits = stats[tokens, 1:2], stats[tokens, 2:3]
        term_cot = to_column(join_term(cots[k][0, seg_len:, 0:seg_len]), seg_len)
        term_grad = term_cot * (1.0 / (1.0 + jnp.exp(-logits)))
        final_grad = cots[k][0, 0:seg_len, :].astype(f32) + term_grad * row(V_HEAD)
        gained = final_grad * row(V_GAIN2)
        grad = (gained - row_mean(gained) - n2 * row_mean(gained * n2)) * scale2
        grad_low = grad.astype(bf16)
        fg[tokens, :] = grad_low
        total += jnp.concatenate(
            [
                column_sum(final_grad * n2),
                column_sum(final_grad),
                column_sum(term_grad * (n2 * row(V_GAIN2) + row(V_SHIFT2))),
                column_sum(grad_low.astype(f32)),
                jnp.broadcast_to(column_sum(term_grad), (1, d)),
                jnp.zeros((3, d), f32),
            ],
            axis=0,
        )
    @pl.when(pl.program_id(0) == 0)
    def _():
        sums[...] = total

    @pl.when(pl.program_id(0) > 0)
    def _():
        sums[...] += total


def head_back(order, cots, n2, stats, vec):
    own_rows, _, d = cots[0].shape
    n = n2.shape[0] // own_rows
    nz = len(cots)
    token = pl.BlockSpec((n, d), lambda i: (i, 0))
    return order.run(
        functools.partial(head_back_kernel, nz),
        [n2, stats, vec, *cots],
        [token, pl.BlockSpec((n, 128), lambda i: (i, 0)), whole(vec, 1)]
        + [pl.BlockSpec((1,) + cots[0].shape[1:], lambda i: (i, 0, 0))] * nz,
        [token, pl.BlockSpec((8, d), lambda i: (0, 0))],
        [jax.ShapeDtypeStruct(n2.shape, bf16), jax.ShapeDtypeStruct((8, d), f32)],
        (own_rows,),
        12,
        "head_back",
    )


def feed_back_kernel(fg_ref, slope, n1_ref, stats, wu, wd, vec, gate_grad, ag, sums):
    d = fg_ref.shape[1]
    parts = slope.shape[1] // d
    fg = fg_ref[...]
    total = fg.astype(f32)
    ups = []
    for c in range(parts):
        cols = pl.ds(c * d, d)
        grad = (dot(fg, wd[cols, :], NT) * slope[:, cols].astype(f32)).astype(bf16)
        gate_grad[:, cols] = grad
        ups.append(column_sum(grad.astype(f32)))
        total += dot(grad, wu[:, cols], NT)
    n1 = n1_ref[...].astype(f32)
    gained = total * vec[V_GAIN1 : V_GAIN1 + 1, :]
    low = ((gained - row_mean(gained) - n1 * row_mean(gained * n1)) * stats[:, 0:1]).astype(bf16)
    ag[...] = low
    part = jnp.concatenate(
        [column_sum(total * n1), column_sum(total), column_sum(low.astype(f32))]
        + ups
        + [jnp.zeros((sums.shape[0] - 3 - parts, d), f32)],
        axis=0,
    )

    @pl.when(pl.program_id(0) == 0)
    def _():
        sums[...] = part

    @pl.when(pl.program_id(0) > 0)
    def _():
        sums[...] += part


def feed_back(order, fg, slope, n1, stats, wu, wd, vec, tile):
    n, d = fg.shape
    hidden = wu.shape[1]
    count = -(-(3 + hidden // d) // 8) * 8
    token = pl.BlockSpec((tile, d), lambda i: (i, 0))
    wide = pl.BlockSpec((tile, hidden), lambda i: (i, 0))
    return order.run(
        feed_back_kernel,
        [fg, in_hbm(slope), n1, stats, wu, wd, vec],
        [
            token,
            wide,
            token,
            pl.BlockSpec((tile, 128), lambda i: (i, 0)),
            in_vmem(),
            in_vmem(),
            whole(vec, 1),
        ],
        [wide, token, pl.BlockSpec((count, d), lambda i: (0, 0))],
        [pltpu.HBM((n, hidden), bf16), jax.ShapeDtypeStruct((n, d), bf16), jax.ShapeDtypeStruct((count, d), f32)],
        (n // tile,),
        20,
        "feed_back",
    )


def weight_rows_kernel(which, left, right, out):
    out[...] = dot(left[...], right[...], TN).astype(bf16)


def weight_rows(order, left, right, which, block):
    n, rows = left.shape
    half, width = rows // 2, right.shape[1]
    return order.run(
        weight_rows_kernel,
        [which, in_hbm(left), right],
        [
            pl.BlockSpec((n, block), lambda j, w: (0, w[0] * (half // block) + j)),
            whole(right, 1),
        ],
        pl.BlockSpec((block, width), lambda j, w: (j, 0)),
        jax.ShapeDtypeStruct((half, width), bf16),
        (half // block,),
        12,
        "weight_rows",
        prefetch=1,
    )


def weight_up_kernel(which, low, att, gate, ag, out):
    chunk = which[0] * 2 + pl.program_id(0)

    @pl.when(chunk < 3)
    def _():
        out[...] = dot(low[...], gate[...], TN).astype(bf16)

    @pl.when(chunk == 3)
    def _():
        width = ag.shape[1]
        out[:, 0:width] = dot(att[...], ag[...], TN).astype(bf16)
        out[:, width:] = jnp.zeros((out.shape[0], out.shape[1] - width), bf16)


def weight_up(order, low, att, gate, ag, which):
    n, d = low.shape
    width = gate.shape[1] // 3
    return order.run(
        weight_up_kernel,
        [which, low, att, in_hbm(gate), ag],
        [
            whole(low, 1),
            whole(att, 1),
            pl.BlockSpec((n, width), lambda j, w: (0, jnp.minimum(w[0] * 2 + j, 2))),
            whole(ag, 1),
        ],
        pl.BlockSpec((d, width), lambda j, w: (j, 0)),
        jax.ShapeDtypeStruct((2 * d, width), bf16),
        (2,),
        18,
        "weight_up",
        prefetch=1,
    )


def weight_qkv_kernel(which, x, grad, out):
    width = out.shape[1]
    chunk = which[0] * 2 + pl.program_id(0)

    @pl.when(chunk < 3)
    def _():
        cols = pl.ds(pl.multiple_of(chunk * width, 128), width)
        out[...] = dot(x[...], grad[:, cols], TN).astype(bf16)

    @pl.when(chunk == 3)
    def _():
        last = grad.shape[1] - 3 * width
        out[:, 0:last] = dot(x[...], grad[:, 3 * width :], TN).astype(bf16)
        out[:, last:] = jnp.zeros((out.shape[0], width - last), bf16)


def weight_qkv(order, x, grad, which):
    d = x.shape[1]
    width = (grad.shape[1] + 256) // 4
    return order.run(
        weight_qkv_kernel,
        [which, x, grad],
        [whole(x, 1), whole(grad, 1)],
        pl.BlockSpec((d, width), lambda j, w: (j, 0)),
        jax.ShapeDtypeStruct((2 * d, width), bf16),
        (2,),
        16,
        "weight_qkv",
        prefetch=1,
    )


def add_kernel(bit, keep_a, got_a, keep_b, got_b, send, keep):
    send[...] = (keep_a[...].astype(f32) + got_a[...].astype(f32)).astype(bf16)
    keep[...] = (keep_b[...].astype(f32) + got_b[...].astype(f32)).astype(bf16)


def add_halves(order, keep, got, bit):
    rows, width = keep.shape
    half = rows // 2
    if half % 16:
        total = (keep.astype(f32) + got.astype(f32)).astype(bf16).reshape(2, half, width)
        return (
            lax.dynamic_index_in_dim(total, 1 - bit[0], 0, False),
            lax.dynamic_index_in_dim(total, bit[0], 0, False),
        )
    steps = 2 if half * width > 400_000 else 1
    block = half // steps
    away = pl.BlockSpec((block, width), lambda i, b: ((1 - b[0]) * steps + i, 0))
    stay = pl.BlockSpec((block, width), lambda i, b: (b[0] * steps + i, 0))
    out = pl.BlockSpec((block, width), lambda i, b: (i, 0))
    return order.run(
        add_kernel,
        [bit, keep, got, keep, got],
        [away, away, stay, stay],
        [out, out],
        [jax.ShapeDtypeStruct((half, width), bf16)] * 2,
        (steps,),
        12,
        "add_halves",
        prefetch=1,
    )


def add_last_kernel(keep, got, out):
    out[...] = (keep[...].astype(f32) + got[...].astype(f32)).astype(bf16)


def add_last(order, keep, got):
    if keep.shape[0] % 16:
        return (keep.astype(f32) + got.astype(f32)).astype(bf16)
    return order.run(
        add_last_kernel,
        [keep, got],
        [whole(keep, 1), whole(got, 1)],
        pl.BlockSpec(keep.shape, lambda i: (0, 0)),
        jax.ShapeDtypeStruct(keep.shape, bf16),
        (1,),
        8,
        "add_last",
    )


def pair_kernel(bit, mine, other, out):
    rows = mine.shape[0]
    out[pl.ds(pl.multiple_of(bit[0] * rows, 16), rows), :] = mine[...]
    out[pl.ds(pl.multiple_of((1 - bit[0]) * rows, 16), rows), :] = other[...]


def pair(order, mine, other, bit):
    rows, width = mine.shape
    if rows % 16:
        first = bit[0] == 0
        return jnp.concatenate([jnp.where(first, mine, other), jnp.where(first, other, mine)])
    return order.run(
        pair_kernel,
        [bit, mine, other],
        [pl.BlockSpec((rows, width), lambda i, b: (0, 0))] * 2,
        pl.BlockSpec((2 * rows, width), lambda i, b: (0, 0)),
        jax.ShapeDtypeStruct((2 * rows, width), bf16),
        (1,),
        8,
        "pair",
        prefetch=1,
    )


def join_kernel(where, *refs):
    for i in range(4):

        @pl.when(pl.program_id(0) == where[i])
        def _():
            refs[4][...] = refs[i][...].astype(f32)


def join_rows(order, pieces, where, block=384):
    rows, width = pieces[0].shape
    steps = rows // block
    return order.run(
        join_kernel,
        [where, *pieces],
        [piece_spec(i, block, width, steps) for i in range(4)],
        pl.BlockSpec((block, width), lambda c, j, w: (c * steps + j, 0)),
        pltpu.HBM((4 * rows, width), f32),
        (4, steps),
        12,
        "join_rows",
        prefetch=1,
    )


def piece_spec(i, block, width, steps):
    def place(c, j, w):
        return (jnp.where(c == w[i], j, jnp.where(c < w[i], 0, steps - 1)), 0)

    return pl.BlockSpec((block, width), place)


def join_columns_kernel(whole_chunks, left, extra, where, *refs):
    pieces, outs = refs[:4], refs[4:]
    chunk = pl.program_id(0)
    for i in range(4):

        @pl.when(jnp.logical_and(chunk == where[i], chunk < whole_chunks))
        def _():
            outs[0][...] = pieces[i][...].astype(f32)

        @pl.when(jnp.logical_and(chunk == where[i], chunk >= whole_chunks))
        def _():
            if left:
                outs[0][:, 0:left] = pieces[i][:, 0:left].astype(f32)
            if extra:
                outs[1][...] = pieces[i][:, left : left + extra].astype(f32)


def join_columns(order, pieces, where, width_out, extra=0, block=384):
    rows, width = pieces[0].shape
    steps = rows // block
    whole_chunks = width_out // width
    left = width_out - whole_chunks * width
    end = whole_chunks if left else whole_chunks - 1

    def place(c, j, w):
        return (jnp.where(c > end, steps - 1, j), jnp.minimum(c, end))

    def at_last(c, j):
        return jnp.where(c == 3, j, 0)

    out_specs = [pl.BlockSpec((block, width), place)]
    out_shape = [pltpu.HBM((rows, width_out), f32)]
    if extra:
        out_specs.append(pl.BlockSpec((block, extra), lambda c, j, w: (at_last(c, j), 0)))
        out_shape.append(pltpu.HBM((rows, extra), f32))
    return order.run(
        functools.partial(join_columns_kernel, whole_chunks, left, extra),
        [where, *pieces],
        [piece_spec(i, block, width, steps) for i in range(4)],
        out_specs,
        out_shape,
        (4, steps),
        14,
        "join_columns",
        prefetch=1,
    )


def hold_kernel(array, out):
    pass


def hold(order, array):
    return order.run(
        hold_kernel,
        [array],
        [pl.BlockSpec(memory_space=pl.ANY)],
        pl.BlockSpec(memory_space=pl.ANY),
        jax.ShapeDtypeStruct(array.shape, array.dtype),
        (1,),
        4,
        "hold",
        input_output_aliases={0: 0},
    )


def pick_kernel(order, *refs):
    k = pl.program_id(0)
    for i, out in enumerate(refs[1:]):

        @pl.when(k == i)
        def _():
            out[...] = refs[0][...]


def pick(order, local, places, first, count):
    nz = places.shape[0]
    own_rows = local.shape[0] // nz
    shape = (count,) + local.shape[1:]
    return order.run(
        pick_kernel,
        [places, local],
        [pl.BlockSpec(shape, lambda k, o: ((o[k] * own_rows + first) // count, 0, 0))],
        [pl.BlockSpec(shape, lambda k, o: (0, 0, 0))] * nz,
        [jax.ShapeDtypeStruct(shape, local.dtype)] * nz,
        (nz,),
        8,
        "pick",
        prefetch=1,
    )


def place_kernel(nz, order, *refs):
    outs = refs[-2:] if len(refs[-1].shape) == 3 else refs[-1:]
    seg_len = outs[0].shape[2]
    for i in range(nz):

        @pl.when(pl.program_id(0) == i)
        def _():
            block = refs[i]
            outs[0][0] = block[:, 0:seg_len, :].astype(outs[0].dtype)
            if len(outs) > 1:
                for r in range(block.shape[0]):
                    outs[1][0, r : r + 1, :] = join_term(block[r, seg_len:, 0:seg_len])


def place(order, blocks, places, own_rows, seg_len, dtype, row=0, before=(), with_term=False):
    nz = len(blocks)
    count, _, d = blocks[0].shape
    out_shape = [pltpu.HBM((nz, own_rows, seg_len, d), dtype)]
    out_specs = [pl.BlockSpec((1, count, seg_len, d), lambda k, o: (o[k], row, 0, 0))]
    if with_term:
        out_shape.append(jax.ShapeDtypeStruct((nz, own_rows, seg_len), f32))
        out_specs.append(pl.BlockSpec((1, count, seg_len), lambda k, o: (o[k], row, 0)))
    return order.run(
        functools.partial(place_kernel, nz),
        [places, *blocks, *before],
        [whole(b, 1) for b in blocks] + [pl.BlockSpec(memory_space=pl.ANY)] * len(before),
        out_specs,
        out_shape,
        (nz,),
        10,
        "place",
        prefetch=1,
        input_output_aliases={1 + nz + i: i for i in range(len(before))},
    )


def bits_of(count):
    return max(count - 1, 0).bit_length()


def move(array, sizes, partner):
    pairs = []
    for b in range(sizes[0]):
        for z in range(sizes[1]):
            to_b, to_z = partner(b, z)
            pairs.append((b * sizes[1] + z, to_b * sizes[1] + to_z))
    return lax.ppermute(array, AXES, pairs)


def send_round(blocks, sizes, sign):
    nz = sizes[1]
    return [blocks[0]] + [
        move(blocks[k], sizes, lambda b, z, k=k: (b, (z + sign * k) % nz)) for k in range(1, nz)
    ]


def halving_steps(sizes):
    batch_bits, blk_bits = bits_of(sizes[0]), bits_of(sizes[1])
    middle = [("b", bit) for bit in range(1, batch_bits)]
    steps = [(("b", 0), ("b", 0))] if batch_bits else []
    steps += list(zip(middle, reversed(middle)))
    return steps + [(("z", bit), ("z", bit)) for bit in range(blk_bits)]


def step_partner(step):
    def partner(b, z):
        axis, bit = step[b & 1]
        return (b ^ (1 << bit), z) if axis == "b" else (b, z ^ (1 << bit))

    return partner


def own_bit(step):
    b, z = lax.axis_index("batch"), lax.axis_index("blk")

    def value(part):
        return ((b if part[0] == "b" else z) >> part[1]) & 1

    bit = jnp.where(b & 1 == 1, value(step[1]), value(step[0]))
    return bit.astype(jnp.int32).reshape(1)


def add_small_kernel(mine, got, out):
    out[...] = mine[...] + got[...]


class SmallSum:
    def __init__(self, order, sizes, array):
        self.order, self.sizes, self.array = order, sizes, array
        self.steps = halving_steps(sizes)
        self.at = -1
        self.send()

    def send(self):
        self.at += 1
        if self.at < len(self.steps):
            self.got = move(self.array, self.sizes, step_partner(self.steps[self.at]))

    def ready(self):
        return self.at == len(self.steps)

    def advance(self):
        self.array = self.order.run(
            add_small_kernel,
            [self.array, self.got],
            [whole(self.array, 1), whole(self.array, 1)],
            pl.BlockSpec(self.array.shape, lambda i: (0, 0)),
            jax.ShapeDtypeStruct(self.array.shape, f32),
            (1,),
            8,
            "add_small",
        )
        self.send()


class Sum:
    def __init__(self, order, sizes, send, keep):
        self.order, self.sizes = order, sizes
        self.steps = halving_steps(sizes)
        self.bits = [own_bit(step) for step in self.steps]
        self.at, self.down = 0, True
        self.part, self.got = keep, self.swap(send, 0)

    def swap(self, array, at):
        return move(array, self.sizes, step_partner(self.steps[at]))

    def ready(self):
        return not self.down and self.at == 1

    def advance(self):
        if not self.down:
            self.part = pair(self.order, self.part, self.got, self.bits[self.at])
            self.at -= 1
        elif self.at + 1 < len(self.steps):
            self.at += 1
            send, self.part = add_halves(self.order, self.part, self.got, self.bits[self.at])
            self.got = self.swap(send, self.at)
            return
        else:
            self.part = add_last(self.order, self.part, self.got)
            self.down = False
        self.got = self.swap(self.part, self.at)

    def send_far(self):
        self.far = self.swap(self.part, 0)

    def pieces(self):
        self.got = hold(self.order, self.got)
        return [self.part, self.got, self.far, self.swap(self.got, 0)]

    def where(self):
        other = own_bit([half[::-1] for half in self.steps][1])
        core, bit = self.bits[0], self.bits[1]
        half, far = core * 2, (1 - core) * 2
        return jnp.concatenate([half + bit, half + 1 - bit, far + other, far + 1 - other])


def per_device(
    hidden_in,
    lengths,
    qkv_weight,
    qv_bias,
    out_weight,
    out_bias,
    attn_gain,
    attn_shift,
    up_weight,
    up_bias,
    down_weight,
    down_bias,
    ffn_gain,
    ffn_shift,
    head_weight,
    head_bias,
    hidden_cot,
    term_cot,
):
    row_count, seg_len, width = hidden_in.shape
    hidden = up_weight.shape[1]
    parts = hidden // width
    sizes = (lax.axis_size("batch"), lax.axis_size("blk"))
    nz = sizes[1]
    own_rows = row_count // nz
    n = seg_len * nz
    rows = range(own_rows)
    core = own_bit(halving_steps(sizes)[0])
    order = Order()
    places = lax.rem(lax.axis_index("blk") + jnp.arange(nz), nz).astype(jnp.int32)

    vec = jnp.concatenate(
        [
            qv_bias,
            out_bias[None],
            attn_gain[None],
            attn_shift[None],
            down_bias[None],
            ffn_gain[None],
            ffn_shift[None],
            head_weight[None],
            jnp.broadcast_to(head_bias[None], (1, width)),
            up_bias.reshape(parts, width),
            jnp.zeros((-(V_UP + parts) % 8, width), bf16),
        ],
        axis=0,
    ).astype(f32)
    high = term_cot.astype(bf16)
    rest = (term_cot - high.astype(f32)).astype(bf16)
    terms = jnp.pad(jnp.stack([high, rest], axis=1), ((0, 0), (0, PACK - 2), (0, width - seg_len)))
    packed_cot = jnp.concatenate([hidden_cot, terms], axis=1)

    blocks = []
    for r in rows:
        got = send_round(pick(order, hidden_in, places, r, 1), sizes, 1)
        got[1] = hold(order, got[1])
        blocks.append([b[0] for b in got])
    held = ()
    for r in rows:
        held = attend(order, blocks[r], lengths, qkv_weight, vec, own_rows, r, held)
        if r == 0:
            cots = send_round(pick(order, packed_cot, places, 0, own_rows), sizes, 1)
    x, q, k, v, att, probs = held
    act, slope, low, n1, n2, stats, *hid = feed(
        order, x, att, out_weight, up_weight, down_weight, vec, nz, own_rows
    )
    outs = send_round(hid, sizes, -1)
    fg, head_sums = head_back(order, cots, n2, stats, vec)
    d_send = weight_rows(order, act, fg, 1 - core, 384)
    d = Sum(order, sizes, d_send, weight_rows(order, act, fg, core, 384))
    d.advance()
    gate_grad, ag, feed_sums = feed_back(
        order, fg, slope, n1, stats, up_weight, down_weight, vec, n // 2
    )
    d.advance()
    hidden_out, term_weight = place(
        order, outs, places, own_rows, seg_len, bf16, with_term=True
    )
    up_args = (low, att, gate_grad, ag)
    u_send = weight_up(order, *up_args, 1 - core)
    u = Sum(order, sizes, u_send, weight_up(order, *up_args, core))
    u.advance()
    d.advance()
    held, grads = (), []
    for r in rows:
        *held, b0, b1, b2, b3 = attend_back(
            order, ag, out_weight, q, k, v, att, probs, qkv_weight, nz, own_rows, r, held
        )
        if r == 0:
            d.advance()
        u.advance()
        grads.append(send_round([b0, b1, b2, b3], sizes, -1))
    proj_grad, qv_sums = held
    grad_hidden = place(order, grads[0], places, own_rows, seg_len, f32)
    q_send = weight_qkv(order, x, proj_grad, 1 - core)
    q = Sum(order, sizes, q_send, weight_qkv(order, x, proj_grad, core))
    where = q.where()
    q.advance()
    u.advance()
    for r in rows[1:]:
        grad_hidden = place(order, grads[r], places, own_rows, seg_len, f32, r, grad_hidden)
    (grad_hidden,) = grad_hidden
    d.advance()
    small = SmallSum(order, sizes, jnp.concatenate([head_sums, feed_sums, qv_sums], axis=0))
    q.advance()
    u.advance()
    small.advance()
    q.advance()
    d.advance()
    small.advance()
    u.advance()
    q.advance()
    small.advance()
    d.advance()
    small.advance()
    q.advance()
    u.advance()
    while not small.ready():
        small.advance()
    while not d.ready():
        d.advance()
    d.send_far()
    q.advance()
    while not u.ready():
        u.advance()
    u.send_far()
    d_pieces = d.pieces()
    q.advance()
    grad_down = join_rows(order, d_pieces, where)
    while not q.ready():
        q.advance()
    q.send_far()
    grad_up, grad_out = join_columns(order, u.pieces(), where, hidden, width)
    early, late = small.array[0:16], small.array[16:]
    grad_qv = sum(late[8 * r : 8 * r + 2] for r in rows)
    vectors = [early[i] for i in (10, 8, 9)]
    vectors += [early[11 : 11 + parts].reshape(hidden)]
    vectors += [early[i] for i in (3, 0, 1, 2)] + [early[4, 0:1]]
    (grad_qkv,) = join_columns(order, q.pieces(), where, 3 * width)
    return (
        hidden_out.reshape(hidden_in.shape),
        term_weight.reshape(row_count, seg_len),
        grad_hidden.reshape(hidden_in.shape),
        grad_qkv,
        grad_qv,
        grad_out,
        vectors[0],
        vectors[1],
        vectors[2],
        grad_up,
        vectors[3],
        grad_down,
        vectors[4],
        vectors[5],
        vectors[6],
        vectors[7],
        vectors[8],
    )


def solution(mesh):
    split = P("batch", "blk", None)
    flat = P("batch", "blk")
    return jax.shard_map(
        per_device,
        mesh=mesh,
        in_specs=(split, P("batch", None)) + (P(),) * 14 + (split, flat),
        out_specs=(split, flat, split) + (P(),) * 14,
        check_vma=False,
    )
```

time: 528 us -> 351 us (0.66)
  waiting for transfers between devices: 193 us -> 98.4 us
  local copies, waits for them, and re-layouts: 54.3 us -> 11.1 us
  blocking collectives: 31.1 us -> 0 us
  Pallas kernels: 135 us -> 157 us
  other arithmetic: 19.9 us -> 2.24 us
  starting transfers between devices: 86.3 us -> 75.7 us
    ppermute x80 -> x56, waiting for transfers between devices: 193 us -> 98.4 us  [move(): return lax.ppermute(array, AXES, pairs)]
    all_gather x1 -> x0, blocking collectives: 31.1 us -> none  [per_device(): own_slots = lax.all_gather(term_cot, 'blk', axis=0)]
    unnamed x180 -> x62, local copies, waits for them, and re-layouts: 32.3 us -> 9.16 us
    pallas_call x22 -> x56, Pallas kernels: 135 us -> 157 us  [run(): pl.pallas_call(body, grid_spec=pltpu.PrefetchScalarGridSpec(num_scalar_pr...]
    dynamic_update_slice x24 -> x0, local copies, waits for them, and re-layouts: 10.9 us -> none  [to_segments(): lax.dynamic_update_index_in_dim(out, got[r][k], (z + k) % nz * own_rows +...]
    ppermute x80 -> x56, starting transfers between devices: 86.3 us -> 75.7 us  [move(): return lax.ppermute(array, AXES, pairs)]
    concatenate x21 -> x2, other arithmetic: 8.22 us -> 1.6 us  [the longest x1 1.53 us: per_device(): packed_cot = jnp.concatenate([hidden_cot, terms], axis=1)]
    convert_element_type x21 -> x0, other arithmetic: 5.66 us -> none  [the longest x16 3.52 us: half(): return (mine.astype(f32) + other.astype(f32)).astype(bf16)]
  transfers between devices with their start and end apart: 80 -> 56, of which waited for: 41 -> 19; matrix products, arithmetic and copies ran while one was open for 7% -> 2% of each run, Pallas kernels for 20% -> 43%
where the time goes in v3:
time: 351 us; the launch traced here: 347 us
  Pallas kernels  157 us (45%)
  waiting for transfers between devices  98.4 us (28%)
  starting transfers between devices  75.7 us (22%)
  local copies, waits for them, and re-layouts  11.1 us (3%)
    pallas_call x56, Pallas kernels, run(): pl.pallas_call(body, grid_spec=pltpu.PrefetchScalarGridSpec(num_scalar_pr...  157 us
    ppermute x56, waiting for transfers between devices, move(): return lax.ppermute(array, AXES, pairs)  98.4 us
    ppermute x56, starting transfers between devices, move(): return lax.ppermute(array, AXES, pairs)  75.7 us
    unnamed x62, local copies, waits for them, and re-layouts  9.16 us
  transfers between devices with their start and end apart: 56, of which 19 were waited for; matrix products, arithmetic and copies ran while one was open for 2% of the time, Pallas kernels for 43%

profile of v3, /device:TPU:0, one launch (start us, length us, event | category | flops | bytes accessed | tf_op | source)
XLA Modules:
  0.0 347.0 jit_solution(17906366048830077461)
XLA Ops:
  0.7 1.4 copy-done.1
  2.8 3.1 collective-permute-start
  5.9 2.6 collective-permute-start.4
  8.5 1.3 collective-permute-start.5
  9.9 3.9 %collective-permute-done.refs_0_ = bf16[1,128,768]{2,1,0:T(8,128)(2,1)S(1)} collective-permute-done((bf16[1,128,768]{2,1,0:T(8,128)(2,1)S(1)}, bf16[1,128,768]{2,1,0:T(8,128)(2,1)S(1)}, u32[]{:S(2)}, u32[]{:S(2)}) %collective-permute-start) | collective-permute-done | bytes 196640 | tf_op jit(solution)/shard_map/ppermute | solution.py:840
  13.8 1.4 copy-done.2
  16.0 7.1 %collective-permute-start.1 = (bf16[1,128,768]{2,1,0:T(8,128)(2,1)S(1)}, bf16[1,128,768]{2,1,0:T(8,128)(2,1)S(1)}, u32[]{:S(2)}, u32[]{:S(2)}) collective-permute-start(bf16[1,128,768]{2,1,0:T(8,128)(2,1)S(1)} %get-tuple-element.187), channel_id=1, source_target_pairs={{0,1},{1,2},{2,3},{3,0},{4,5},{5,6},{6,7},{7,4},{8,9},{9,10},{10,1... | collective-permute-start | bytes 589832 | tf_op jit(solution)/shard_map/ppermute | solution.py:840
  24.1 1.5 pad_maximum_fusion.refs_1_
  25.6 2.4 collective-permute-start.2
  28.1 2.9 collective-permute-start.3
  31.7 11.8 %attend.2 = (bf16[1024,768]{1,0:T(8,128)(2,1)S(1)}, bf16[1024,768]{1,0:T(8,128)(2,1)S(1)}, bf16[1024,768]{1,0:T(8,128)(2,1)S(1)}, bf16[1024,768]{1,0:T(8,128)(2,...) custom-call(s32[8,8]{1,0:T(8,128)S(1)} %copy-done.5, ...), custom_call_target="tpu_custom_call" | custom-call | flops 109999996928 | bytes 1000 | tf_op jit(solution)/shard_map/attend/pallas_call | solution.py:75
  43.5 1.9 pick.5
  45.4 7.2 %collective-permute-start.9 = (bf16[2,144,768]{2,1,0:T(8,128)(2,1)}, bf16[2,144,768]{2,1,0:T(8,128)(2,1)}, u32[]{:S(2)}, u32[]{:S(2)}) collective-permute-start(bf16[2,144,768]{2,1,0:T(8,128)(2,1)} %get-tuple-element.216), channel_id=1, source_target_pairs={{0,1},{1,2},{2,3},{3,0},{4,5},{5,6},{6,7},{7,4},{8,9},{9,10},{10,1... | collective-permute-start | bytes 1327112 | tf_op jit(solution)/shard_map/ppermute | solution.py:840
  52.5 1.9 collective-permute-start.10
  54.4 3.4 collective-permute-start.11
  57.9 12.0 %attend.3 = (bf16[1024,768]{1,0:T(8,128)(2,1)S(1)}, bf16[1024,768]{1,0:T(8,128)(2,1)S(1)}, bf16[1024,768]{1,0:T(8,128)(2,1)S(1)}, bf16[1024,768]{1,0:T(8,128)(2,...) custom-call(s32[8,8]{1,0:T(8,128)S(1)} %copy-done.5, ...), custom_call_target="tpu_custom_call", output_to_operand_aliasing={{0}: (9, {}), {1}: (10, {}), {2}: (11, {}), {3}: (12, {}), ... | custom-call | flops 109999996928 | bytes 1000 | tf_op jit(solution)/shard_map/attend/pallas_call | solution.py:75
  73.4 19.2 %feed.1 = (bf16[1024,3072]{1,0:T(8,128)(2,1)}, bf16[1024,3072]{1,0:T(8,128)(2,1)}, bf16[1024,768]{1,0:T(8,128)(2,1)S(1)}, bf16[1024,768]{1,0:T(8,128)(2,1)S(1)},...) custom-call(bf16[1024,768]{1,0:T(8,128)(2,1)S(1)} %get-tuple-element, ...), custom_call_target="tpu_custom_call" | custom-call | flops 199999995904 | bytes 1000 | tf_op jit(solution)/shard_map/feed/pallas_call | solution.py:75
  93.2 1.6 collective-permute-start.8
  94.9 4.5 %head_back.1 = (bf16[1024,768]{1,0:T(8,128)(2,1)S(1)}, f32[8,768]{1,0:T(8,128)S(1)}, f32[8,128]{1,0:T(8,128)S(1)}) custom-call(bf16[1024,768]{1,0:T(8,128)(2,1)S(1)} %get-tuple-element.213.refs_0_, f32[1024,128]{1,0:T(8,128)S(1)} %get-tuple-element.214.refs_1_.refs_3_, f32[16,768]{1,0:T(8,128)S(1)} %convert_element_type.14.refs_8_.refs_5_.refs_2_.refs_6_, ...), custom_call_target="tpu_custom_call" | custom-call | flops 20000000000 | bytes 1000 | tf_op jit(solution)/shard_map/head_back/pallas_call | solution.py:75
  99.4 4.8 %weight_rows.2 = (bf16[1536,768]{1,0:T(8,128)(2,1)S(1)}, f32[8,128]{1,0:T(8,128)S(1)}) custom-call(s32[1]{0:T(128)S(6)} %sub.16.refs_0_, bf16[1024,3072]{1,0:T(8,128)(2,1)} %get-tuple-element.212.refs_1_, bf16[1024,768]{1,0:T(8,128)(2,1)S(1)} %get-tuple-element.220.refs_2_.refs_0_, f32[8,128]{1,0:T(8,128)S(1)} %get-tuple-element.221.refs_3_), custom_call_target="tpu_custom_call" | custom-call | flops 49999998976 | bytes 1000 | tf_op jit(solution)/shard_map/weight_rows/pallas_call | solution.py:75
  104.3 4.8 %weight_rows.3 = (bf16[1536,768]{1,0:T(8,128)(2,1)S(1)}, f32[8,128]{1,0:T(8,128)S(1)}) custom-call(s32[1]{0:T(128)} %bitcast.13.refs_0_, bf16[1024,3072]{1,0:T(8,128)(2,1)} %get-tuple-element.212.refs_1_, bf16[1024,768]{1,0:T(8,128)(2,1)S(1)} %get-tuple-element.220.refs_2_.refs_0_, f32[8,128]{1,0:T(8,128)S(1)} %get-tuple-element.222.refs_3_), custom_call_target="tpu_custom_call" | custom-call | flops 49999998976 | bytes 1000 | tf_op jit(solution)/shard_map/weight_rows/pallas_call | solution.py:75
  111.0 1.5 collective-permute-start.13
  112.5 14.7 %feed_back.1 = (bf16[1024,3072]{1,0:T(8,128)(2,1)}, bf16[1024,768]{1,0:T(8,128)(2,1)S(1)}, f32[8,768]{1,0:T(8,128)S(1)}, f32[8,128]{1,0:T(8,128)S(1)}) custom-call(bf16[1024,768]{1,0:T(8,128)(2,1)S(1)} %get-tuple-element.220.refs_2_.refs_0_, bf16[1024,3072]{1,0:T(8,128)(2,1)} %get-tuple-element.228.refs_1_, ...), custom_call_target="tpu_custom_call" | custom-call | flops 179999997952 | bytes 1000 | tf_op jit(solution)/shard_map/feed_back/pallas_call | solution.py:75
  127.8 1.5 add_halves.13
  129.3 1.6 collective-permute-start.14
  130.9 3.6 %place.3 = (bf16[4,2,128,768]{3,2,1,0:T(8,128)(2,1)}, f32[4,2,128]{2,1,0:T(2,128)}, f32[8,128]{1,0:T(8,128)S(1)}) custom-call(s32[4]{0:T(128)S(1)} %compare_select_fusion.refs_0_, bf16[2,144,768]{2,1,0:T(8,128)(2,1)S(1)} %get-tuple-element.208.refs_1_, bf16[2,144,768]{2,1,0:T(8,128)(2,1)} %collective-permute-done.6.refs_2_, ...), custom_call_target="tpu_custom_call" | custom-call | flops 10000000000 | bytes 1000 | tf_op jit(solution)/shard_map/place/pallas_call | solution.py:75
  134.5 4.9 %weight_up.2 = (bf16[1536,1024]{1,0:T(8,128)(2,1)S(1)}, f32[8,128]{1,0:T(8,128)S(1)}) custom-call(s32[1]{0:T(128)S(6)} %sub.16.refs_0_, bf16[1024,768]{1,0:T(8,128)(2,1)S(1)} %get-tuple-element.242.refs_1_, bf16[1024,768]{1,0:T(8,128)(2,1)S(1)} %copy-done.9, bf16[1024,3072]{1,0:T(8,128)(2,1)} %get-tuple-element.243.refs_3_, ...), custom_call_target="tpu_custom_call" | custom-call | flops 49999998976 | bytes 1000 | tf_op jit(solution)/shard_map/weight_up/pallas_call | solution.py:75
  139.8 5.3 %weight_up.3 = (bf16[1536,1024]{1,0:T(8,128)(2,1)S(1)}, f32[8,128]{1,0:T(8,128)S(1)}) custom-call(s32[1]{0:T(128)} %bitcast.13.refs_0_, bf16[1024,768]{1,0:T(8,128)(2,1)S(1)} %get-tuple-element.242.refs_1_, bf16[1024,768]{1,0:T(8,128)(2,1)S(1)} %copy-done.9, bf16[1024,3072]{1,0:T(8,128)(2,1)} %get-tuple-element.243.refs_3_, ...), custom_call_target="tpu_custom_call" | custom-call | flops 49999998976 | bytes 1000 | tf_op jit(solution)/shard_map/weight_up/pallas_call | solution.py:75
  145.2 1.6 add_halves.14
  148.2 1.6 collective-permute-start.17
  150.8 14.7 %attend_back.2 = (bf16[1024,2304]{1,0:T(8,128)(2,1)S(1)}, f32[16,768]{1,0:T(8,128)S(1)}, bf16[1,128,768]{2,1,0:T(8,128)(2,1)S(1)}, bf16[1,128,768]{2,1,0:T(8,128...) custom-call(bf16[1024,768]{1,0:T(8,128)(2,1)S(1)} %get-tuple-element.235.refs_4_.refs_0_, ...), custom_call_target="tpu_custom_call" | custom-call | flops 130000003072 | bytes 1000 | tf_op jit(solution)/shard_map/attend_back/pallas_call | solution.py:75
  165.4 2.4 collective-permute-start.21
  168.4 1.9 collective-permute-start.23
  171.5 1.7 add_halves.17
  173.8 13.9 %attend_back.3 = (bf16[1024,2304]{1,0:T(8,128)(2,1)S(1)}, f32[16,768]{1,0:T(8,128)S(1)}, bf16[1,128,768]{2,1,0:T(8,128)(2,1)S(1)}, bf16[1,128,768]{2,1,0:T(8,128...) custom-call(bf16[1024,768]{1,0:T(8,128)(2,1)S(1)} %get-tuple-element, ...), custom_call_target="tpu_custom_call", output_to_operand_aliasing={{0}: (10, {}), {1}: (11, {})} | custom-call | flops 130000003072 | bytes 1000 | tf_op jit(solution)/shard_map/attend_back/pallas_call | solution.py:75
  187.7 3.0 collective-permute-start.18
  192.6 3.6 %place.4 = (f32[4,2,128,768]{3,2,1,0:T(8,128)}, f32[8,128]{1,0:T(8,128)S(1)}) custom-call(s32[4]{0:T(128)S(1)} %compare_select_fusion.refs_0_, bf16[1,128,768]{2,1,0:T(8,128)(2,1)S(1)} %get-tuple-element.264.refs_1_, bf16[1,128,768]{2,1,0:T(8,128)(2,1)} %collective-permute-done.21.refs_2_, bf16[1,128,768]{2,1,0:T(8,128)(2,1)} %collective-permute-done.22.refs_3_, ...), custom_call_target="tpu_custom_call" | custom-call | flops 10000000000 | bytes 1000 | tf_op jit(solution)/shard_map/place/pallas_call | solution.py:75
  196.2 2.5 weight_qkv.2
  198.8 2.9 weight_qkv.3
  202.7 1.9 collective-permute-start.25
  205.1 12.0 %collective-permute-done.25.refs_2_.refs_4_ = bf16[192,1024]{1,0:T(8,128)(2,1)S(1)} collective-permute-done((bf16[192,1024]{1,0:T(8,128)(2,1)S(1)}, bf16[192,1024]{1,0:T(8,128)(2,1)S(1)}, u32[]{:S(2)}, u32[]{:S(2)}) %collective-permute-start.25) | collective-permute-done | bytes 393248 | tf_op jit(solution)/shard_map/ppermute | solution.py:840
  218.2 2.3 place.5
  221.5 3.0 collective-permute-start.35
  224.4 6.9 %collective-permute-done.27.refs_2_.refs_4_ = bf16[768,640]{1,0:T(8,128)(2,1)S(1)} collective-permute-done((bf16[768,640]{1,0:T(8,128)(2,1)S(1)}, bf16[768,640]{1,0:T(8,128)(2,1)S(1)}, u32[]{:S(2)}, u32[]{:S(2)}) %collective-permute-start.27) | collective-permute-done | bytes 983072 | tf_op jit(solution)/shard_map/ppermute | solution.py:840
  231.6 1.8 collective-permute-start.29
  234.7 6.9 %collective-permute-done.29.refs_2_.refs_4_ = bf16[384,640]{1,0:T(8,128)(2,1)S(1)} collective-permute-done((bf16[384,640]{1,0:T(8,128)(2,1)S(1)}, bf16[384,640]{1,0:T(8,128)(2,1)S(1)}, u32[]{:S(2)}, u32[]{:S(2)}) %collective-permute-start.29) | collective-permute-done | bytes 491552 | tf_op jit(solution)/shard_map/ppermute | solution.py:840
  241.8 1.5 collective-permute-start.37
  243.2 2.0 collective-permute-start.39
  245.4 5.2 %collective-permute-done.32.refs_2_.refs_4_ = bf16[192,640]{1,0:T(8,128)(2,1)S(1)} collective-permute-done((bf16[192,640]{1,0:T(8,128)(2,1)S(1)}, bf16[192,640]{1,0:T(8,128)(2,1)S(1)}, u32[]{:S(2)}, u32[]{:S(2)}) %collective-permute-start.32) | collective-permute-done | bytes 245792 | tf_op jit(solution)/shard_map/ppermute | solution.py:840
  251.9 7.6 %collective-permute-done.39.refs_2_ = bf16[192,768]{1,0:T(8,128)(2,1)S(1)} collective-permute-done((bf16[192,768]{1,0:T(8,128)(2,1)S(1)}, bf16[192,768]{1,0:T(8,128)(2,1)S(1)}, u32[]{:S(2)}, u32[]{:S(2)}) %collective-permute-start.39) | collective-permute-done | bytes 294944 | tf_op jit(solution)/shard_map/ppermute | solution.py:840
  259.6 1.5 collective-permute-start.41
  261.0 8.5 %collective-permute-done.38.refs_1_ = f32[32,768]{1,0:T(8,128)S(1)} collective-permute-done((f32[32,768]{1,0:T(8,128)S(1)}, f32[32,768]{1,0:T(8,128)S(1)}, u32[]{:S(2)}, u32[]{:S(2)}) %collective-permute-start.38) | collective-permute-done | bytes 98336 | tf_op jit(solution)/shard_map/ppermute | solution.py:840
  269.7 3.0 collective-permute-start.40
  273.2 5.5 %collective-permute-done.42.refs_1_ = f32[32,768]{1,0:T(8,128)S(1)} collective-permute-done((f32[32,768]{1,0:T(8,128)S(1)}, f32[32,768]{1,0:T(8,128)S(1)}, u32[]{:S(2)}, u32[]{:S(2)}) %collective-permute-start.42) | collective-permute-done | bytes 98336 | tf_op jit(solution)/shard_map/ppermute | solution.py:840
  281.3 6.9 %collective-permute-done.46.refs_2_ = bf16[384,1024]{1,0:T(8,128)(2,1)S(1)} collective-permute-done((bf16[384,1024]{1,0:T(8,128)(2,1)S(1)}, bf16[384,1024]{1,0:T(8,128)(2,1)S(1)}, u32[]{:S(2)}, u32[]{:S(2)}) %collective-permute-start.46) | collective-permute-done | bytes 786464 | tf_op jit(solution)/shard_map/ppermute | solution.py:840
  288.3 7.2 %collective-permute-done.45.refs_0_ = bf16[768,768]{1,0:T(8,128)(2,1)S(1)} collective-permute-done((bf16[768,768]{1,0:T(8,128)(2,1)S(1)}, bf16[768,768]{1,0:T(8,128)(2,1)S(1)}, u32[]{:S(2)}, u32[]{:S(2)}) %collective-permute-start.45) | collective-permute-done | bytes 1179680 | tf_op jit(solution)/shard_map/ppermute | solution.py:840
  295.5 1.8 collective-permute-start.49
  299.7 5.4 %join_rows.1 = (f32[3072,768]{1,0:T(8,128)}, f32[8,128]{1,0:T(8,128)S(1)}) custom-call(s32[4]{0:T(128)S(1)} %pad_add_fusion.refs_0_, bf16[768,768]{1,0:T(8,128)(2,1)S(1)} %get-tuple-element.327.refs_1_, bf16[768,768]{1,0:T(8,128)(2,1)S(1)} %get-tuple-element.333.refs_2_, bf16[768,768]{1,0:T(8,128)(2,1)S(1)} %collective-permute-done.48.refs_3_, ...), custom_call_target="tpu_custom_call" | custom-call | flops 10000000000 | bytes 1000 | tf_op jit(solution)/shard_map/join_rows/pallas_call | solution.py:75
  305.1 7.6 %collective-permute-done.47.refs_2_ = bf16[384,640]{1,0:T(8,128)(2,1)S(1)} collective-permute-done((bf16[384,640]{1,0:T(8,128)(2,1)S(1)}, bf16[384,640]{1,0:T(8,128)(2,1)S(1)}, u32[]{:S(2)}, u32[]{:S(2)}) %collective-permute-start.47) | collective-permute-done | bytes 491552 | tf_op jit(solution)/shard_map/ppermute | solution.py:840
  312.7 10.3 %collective-permute-done.51.refs_0_ = bf16[768,1024]{1,0:T(8,128)(2,1)S(1)} collective-permute-done((bf16[768,1024]{1,0:T(8,128)(2,1)S(1)}, bf16[768,1024]{1,0:T(8,128)(2,1)S(1)}, u32[]{:S(2)}, u32[]{:S(2)}) %collective-permute-start.51) | collective-permute-done | bytes 1572896 | tf_op jit(solution)/shard_map/ppermute | solution.py:840
  324.1 2.3 collective-permute-done.53.refs_4_
  326.4 6.5 %join_columns.2 = (f32[768,3072]{1,0:T(8,128)}, f32[768,768]{1,0:T(8,128)}, f32[8,128]{1,0:T(8,128)S(1)}) custom-call(s32[4]{0:T(128)S(1)} %pad_add_fusion.refs_0_, bf16[768,1024]{1,0:T(8,128)(2,1)S(1)} %get-tuple-element.337.refs_1_, bf16[768,1024]{1,0:T(8,128)(2,1)S(1)} %get-tuple-element.339.refs_2_, ...), custom_call_target="tpu_custom_call" | custom-call | flops 10000000000 | bytes 1000 | tf_op jit(solution)/shard_map/join_columns/pallas_call | solution.py:75
  332.9 4.3 %collective-permute-done.50.refs_0_ = bf16[768,640]{1,0:T(8,128)(2,1)} collective-permute-done((bf16[768,640]{1,0:T(8,128)(2,1)S(1)}, bf16[768,640]{1,0:T(8,128)(2,1)}, u32[]{:S(2)}, u32[]{:S(2)}) %collective-permute-start.50) | collective-permute-done | bytes 983072 | tf_op jit(solution)/shard_map/ppermute | solution.py:840
  340.0 6.7 %join_columns.3 = (f32[768,2304]{1,0:T(8,128)}, f32[8,128]{1,0:T(8,128)}) custom-call(s32[4]{0:T(128)S(1)} %pad_add_fusion.refs_0_, bf16[768,640]{1,0:T(8,128)(2,1)S(1)} %get-tuple-element.336.refs_1_, bf16[768,640]{1,0:T(8,128)(2,1)} %get-tuple-element.342.refs_2_, bf16[768,640]{1,0:T(8,128)(2,1)S(1)} %collective-permute-done.54.refs_3_, ...), custom_call_target="tpu_custom_call" | custom-call | flops 10000000000 | bytes 1000 | tf_op jit(solution)/shard_map/join_columns/pallas_call | solution.py:75
  (193 shorter events, 32.6 us)
Async XLA Ops:
  2.8 11.0 %collective-permute-start = (bf16[1,128,768]{2,1,0:T(8,128)(2,1)S(1)}, bf16[1,128,768]{2,1,0:T(8,128)(2,1)S(1)}, u32[]{:S(2)}, u32[]{:S(2)}) collective-permute-start(bf16[1,128,768]{2,1,0:T(8,128)(2,1)S(1)} %get-tuple-element.183), channel_id=1, source_target_pairs={{0,1},{1,2},{2,3},{3,0},{4,5},{5,6},{6,7},{7,4},{8,9},{9,10},{10,1... | collective-permute-start | bytes 589832 | tf_op jit(solution)/shard_map/ppermute | solution.py:840
  5.9 25.1 %collective-permute-start.4 = (bf16[1,128,768]{2,1,0:T(8,128)(2,1)S(1)}, bf16[1,128,768]{2,1,0:T(8,128)(2,1)S(1)}, u32[]{:S(2)}, u32[]{:S(2)}) collective-permute-start(bf16[1,128,768]{2,1,0:T(8,128)(2,1)S(1)} %get-tuple-element.194), channel_id=1, source_target_pairs={{0,2},{1,3},{2,0},{3,1},{4,6},{5,7},{6,4},{7,5},{8,10},{9,11},{10,... | collective-permute-start | bytes 589832 | tf_op jit(solution)/shard_map/ppermute | solution.py:840
  8.5 22.5 %collective-permute-start.5 = (bf16[1,128,768]{2,1,0:T(8,128)(2,1)S(1)}, bf16[1,128,768]{2,1,0:T(8,128)(2,1)S(1)}, u32[]{:S(2)}, u32[]{:S(2)}) collective-permute-start(bf16[1,128,768]{2,1,0:T(8,128)(2,1)S(1)} %get-tuple-element.195), channel_id=1, source_target_pairs={{0,3},{1,0},{2,1},{3,2},{4,7},{5,4},{6,5},{7,6},{8,11},{9,8},{10,9... | collective-permute-start | bytes 589832 | tf_op jit(solution)/shard_map/ppermute | solution.py:840
  16.0 15.0 %collective-permute-start.1 = (bf16[1,128,768]{2,1,0:T(8,128)(2,1)S(1)}, bf16[1,128,768]{2,1,0:T(8,128)(2,1)S(1)}, u32[]{:S(2)}, u32[]{:S(2)}) collective-permute-start(bf16[1,128,768]{2,1,0:T(8,128)(2,1)S(1)} %get-tuple-element.187), channel_id=1, source_target_pairs={{0,1},{1,2},{2,3},{3,0},{4,5},{5,6},{6,7},{7,4},{8,9},{9,10},{10,1... | collective-permute-start | bytes 589832 | tf_op jit(solution)/shard_map/ppermute | solution.py:840
  25.6 32.2 %collective-permute-start.2 = (bf16[1,128,768]{2,1,0:T(8,128)(2,1)S(1)}, bf16[1,128,768]{2,1,0:T(8,128)(2,1)S(1)}, u32[]{:S(2)}, u32[]{:S(2)}) collective-permute-start(bf16[1,128,768]{2,1,0:T(8,128)(2,1)S(1)} %get-tuple-element.190), channel_id=1, source_target_pairs={{0,2},{1,3},{2,0},{3,1},{4,6},{5,7},{6,4},{7,5},{8,10},{9,11},{10,... | collective-permute-start | bytes 589832 | tf_op jit(solution)/shard_map/ppermute | solution.py:840
  28.1 29.8 %collective-permute-start.3 = (bf16[1,128,768]{2,1,0:T(8,128)(2,1)S(1)}, bf16[1,128,768]{2,1,0:T(8,128)(2,1)S(1)}, u32[]{:S(2)}, u32[]{:S(2)}) collective-permute-start(bf16[1,128,768]{2,1,0:T(8,128)(2,1)S(1)} %get-tuple-element.191), channel_id=1, source_target_pairs={{0,3},{1,0},{2,1},{3,2},{4,7},{5,4},{6,5},{7,6},{8,11},{9,8},{10,9... | collective-permute-start | bytes 589832 | tf_op jit(solution)/shard_map/ppermute | solution.py:840
  43.5 29.9 %slice-start = ((s8[4718592]{0:T(1024)(128)(4,1)}), s8[4194304]{0:T(1024)(128)(4,1)S(1)}, s32[]{:S(2)}) async-start(s8[4718592]{0:T(1024)(128)(4,1)} %bitcast.23), calls=%async_computation | async-start | bytes 8388608
  43.5 29.9 %slice-start.2 = ((s8[4718592]{0:T(1024)(128)(4,1)}), s8[4194304]{0:T(1024)(128)(4,1)S(1)}, s32[]{:S(2)}) async-start(s8[4718592]{0:T(1024)(128)(4,1)} %bitcast.25), calls=%async_computation.2 | async-start | bytes 8388608
  45.4 47.9 %collective-permute-start.9 = (bf16[2,144,768]{2,1,0:T(8,128)(2,1)}, bf16[2,144,768]{2,1,0:T(8,128)(2,1)}, u32[]{:S(2)}, u32[]{:S(2)}) collective-permute-start(bf16[2,144,768]{2,1,0:T(8,128)(2,1)} %get-tuple-element.216), channel_id=1, source_target_pairs={{0,1},{1,2},{2,3},{3,0},{4,5},{5,6},{6,7},{7,4},{8,9},{9,10},{10,1... | collective-permute-start | bytes 1327112 | tf_op jit(solution)/shard_map/ppermute | solution.py:840
  52.5 42.4 %collective-permute-start.10 = (bf16[2,144,768]{2,1,0:T(8,128)(2,1)}, bf16[2,144,768]{2,1,0:T(8,128)(2,1)}, u32[]{:S(2)}, u32[]{:S(2)}) collective-permute-start(bf16[2,144,768]{2,1,0:T(8,128)(2,1)} %get-tuple-element.217), channel_id=1, source_target_pairs={{0,2},{1,3},{2,0},{3,1},{4,6},{5,7},{6,4},{7,5},{8,10},{9,11},{10,... | collective-permute-start | bytes 1327112 | tf_op jit(solution)/shard_map/ppermute | solution.py:840
  54.4 40.4 %collective-permute-start.11 = (bf16[2,144,768]{2,1,0:T(8,128)(2,1)}, bf16[2,144,768]{2,1,0:T(8,128)(2,1)}, u32[]{:S(2)}, u32[]{:S(2)}) collective-permute-start(bf16[2,144,768]{2,1,0:T(8,128)(2,1)} %get-tuple-element.218), channel_id=1, source_target_pairs={{0,3},{1,0},{2,1},{3,2},{4,7},{5,4},{6,5},{7,6},{8,11},{9,8},{10,9... | collective-permute-start | bytes 1327112 | tf_op jit(solution)/shard_map/ppermute | solution.py:840
  57.9 15.5 %slice-start.1 = ((s8[4718592]{0:T(1024)(128)(4,1)}), s8[524288]{0:T(1024)(128)(4,1)S(1)}, s32[]{:S(2)}) async-start(s8[4718592]{0:T(1024)(128)(4,1)} %bitcast.23), calls=%async_computation.1 | async-start | bytes 1048576
  57.9 15.5 %slice-start.3 = ((s8[4718592]{0:T(1024)(128)(4,1)}), s8[524288]{0:T(1024)(128)(4,1)S(1)}, s32[]{:S(2)}) async-start(s8[4718592]{0:T(1024)(128)(4,1)} %bitcast.25), calls=%async_computation.3 | async-start | bytes 1048576
  57.9 15.5 %copy-start.3 = (bf16[768,768]{1,0:T(8,128)(2,1)S(1)}, bf16[768,768]{1,0:T(8,128)(2,1)}, u32[]{:S(2)}) copy-start(bf16[768,768]{1,0:T(8,128)(2,1)} %refs_1_.7) | copy-start | bytes 3538948
  73.4 19.3 %copy-start.6 = (bf16[1024,768]{1,0:T(8,128)(2,1)}, bf16[1024,768]{1,0:T(8,128)(2,1)S(1)}, u32[]{:S(2)}) copy-start(bf16[1024,768]{1,0:T(8,128)(2,1)S(1)} %get-tuple-element.205.refs_0_.refs_1_) | copy-start | bytes 4718596
  73.4 19.3 %copy-start.8 = (bf16[1024,768]{1,0:T(8,128)(2,1)}, bf16[1024,768]{1,0:T(8,128)(2,1)S(1)}, u32[]{:S(2)}) copy-start(bf16[1024,768]{1,0:T(8,128)(2,1)S(1)} %get-tuple-element.206.refs_1_.refs_2_.refs_5_) | copy-start | bytes 4718596
  92.6 38.3 %collective-permute-start.6 = (bf16[2,144,768]{2,1,0:T(8,128)(2,1)}, bf16[2,144,768]{2,1,0:T(8,128)(2,1)}, u32[]{:S(2)}, u32[]{:S(2)}) collective-permute-start(bf16[2,144,768]{2,1,0:T(8,128)(2,1)} %get-tuple-element.209), channel_id=1, source_target_pairs={{0,3},{1,0},{2,1},{3,2},{4,7},{5,4},{6,5},{7,6},{8,11},{9,8},{10,9... | collective-permute-start | bytes 1327112 | tf_op jit(solution)/shard_map/ppermute | solution.py:840
  92.7 38.2 %collective-permute-start.7 = (bf16[2,144,768]{2,1,0:T(8,128)(2,1)}, bf16[2,144,768]{2,1,0:T(8,128)(2,1)}, u32[]{:S(2)}, u32[]{:S(2)}) collective-permute-start(bf16[2,144,768]{2,1,0:T(8,128)(2,1)} %get-tuple-element.210), channel_id=1, source_target_pairs={{0,2},{1,3},{2,0},{3,1},{4,6},{5,7},{6,4},{7,5},{8,10},{9,11},{10,... | collective-permute-start | bytes 1327112 | tf_op jit(solution)/shard_map/ppermute | solution.py:840
  93.2 37.7 %collective-permute-start.8 = (bf16[2,144,768]{2,1,0:T(8,128)(2,1)}, bf16[2,144,768]{2,1,0:T(8,128)(2,1)}, u32[]{:S(2)}, u32[]{:S(2)}) collective-permute-start(bf16[2,144,768]{2,1,0:T(8,128)(2,1)} %get-tuple-element.211), channel_id=1, source_target_pairs={{0,1},{1,2},{2,3},{3,0},{4,5},{5,6},{6,7},{7,4},{8,9},{9,10},{10,1... | collective-permute-start | bytes 1327112 | tf_op jit(solution)/shard_map/ppermute | solution.py:840
  104.2 5.5 %collective-permute-start.12 = (bf16[1536,768]{1,0:T(8,128)(2,1)S(1)}, bf16[1536,768]{1,0:T(8,128)(2,1)S(1)}, u32[]{:S(2)}, u32[]{:S(2)}) collective-permute-start(bf16[1536,768]{1,0:T(8,128)(2,1)S(1)} %get-tuple-element.224), channel_id=1, source_target_pairs={{0,4},{1,5},{2,6},{3,7},{4,0},{5,1},{6,2},{7,3},{8,12},{9,13},{10,... | collective-permute-start | bytes 7077896 | tf_op jit(solution)/shard_map/ppermute | solution.py:840
  111.0 16.8 %collective-permute-start.13 = (bf16[768,768]{1,0:T(8,128)(2,1)}, bf16[768,768]{1,0:T(8,128)(2,1)}, u32[]{:S(2)}, u32[]{:S(2)}) collective-permute-start(bf16[768,768]{1,0:T(8,128)(2,1)} %get-tuple-element.227), channel_id=1, source_target_pairs={{0,8},{1,9},{2,10},{3,11},{4,20},{5,21},{6,22},{7,23},{8,0},{9,1},... | collective-permute-start | bytes 3538952 | tf_op jit(solution)/shard_map/ppermute | solution.py:840
  129.3 18.7 %collective-permute-start.14 = (bf16[384,768]{1,0:T(8,128)(2,1)S(1)}, bf16[384,768]{1,0:T(8,128)(2,1)S(1)}, u32[]{:S(2)}, u32[]{:S(2)}) collective-permute-start(bf16[384,768]{1,0:T(8,128)(2,1)S(1)} %get-tuple-element.241), channel_id=1, source_target_pairs={{0,16},{1,17},{2,18},{3,19},{4,12},{5,13},{6,14},{7,15},{8,24},{9,... | collective-permute-start | bytes 1769480 | tf_op jit(solution)/shard_map/ppermute | solution.py:840
  139.4 5.7 %collective-permute-start.15 = (bf16[1536,1024]{1,0:T(8,128)(2,1)S(1)}, bf16[1536,1024]{1,0:T(8,128)(2,1)S(1)}, u32[]{:S(2)}, u32[]{:S(2)}) collective-permute-start(bf16[1536,1024]{1,0:T(8,128)(2,1)S(1)} %get-tuple-element.247), channel_id=1, source_target_pairs={{0,4},{1,5},{2,6},{3,7},{4,0},{5,1},{6,2},{7,3},{8,12},{9,13},{10,... | collective-permute-start | bytes 9437192 | tf_op jit(solution)/shard_map/ppermute | solution.py:840
  146.8 24.7 %collective-permute-start.16 = (bf16[768,1024]{1,0:T(8,128)(2,1)}, bf16[768,1024]{1,0:T(8,128)(2,1)}, u32[]{:S(2)}, u32[]{:S(2)}) collective-permute-start(bf16[768,1024]{1,0:T(8,128)(2,1)} %get-tuple-element.254), channel_id=1, source_target_pairs={{0,8},{1,9},{2,10},{3,11},{4,20},{5,21},{6,22},{7,23},{8,0},{9,1},... | collective-permute-start | bytes 4718600 | tf_op jit(solution)/shard_map/ppermute | solution.py:840
  148.2 22.2 %collective-permute-start.17 = (bf16[192,768]{1,0:T(8,128)(2,1)S(1)}, bf16[192,768]{1,0:T(8,128)(2,1)S(1)}, u32[]{:S(2)}, u32[]{:S(2)}) collective-permute-start(bf16[192,768]{1,0:T(8,128)(2,1)S(1)} %get-tuple-element.256), channel_id=1, source_target_pairs={{0,1},{1,0},{2,3},{3,2},{4,5},{5,4},{6,7},{7,6},{8,9},{9,8},{10,11... | collective-permute-start | bytes 884744 | tf_op jit(solution)/shard_map/ppermute | solution.py:840
  165.4 25.4 %collective-permute-start.21 = (bf16[1,128,768]{2,1,0:T(8,128)(2,1)}, bf16[1,128,768]{2,1,0:T(8,128)(2,1)}, u32[]{:S(2)}, u32[]{:S(2)}) collective-permute-start(bf16[1,128,768]{2,1,0:T(8,128)(2,1)} %get-tuple-element.265), channel_id=1, source_target_pairs={{0,3},{1,0},{2,1},{3,2},{4,7},{5,4},{6,5},{7,6},{8,11},{9,8},{10,9... | collective-permute-start | bytes 589832 | tf_op jit(solution)/shard_map/ppermute | solution.py:840
  167.8 23.7 %collective-permute-start.22 = (bf16[1,128,768]{2,1,0:T(8,128)(2,1)}, bf16[1,128,768]{2,1,0:T(8,128)(2,1)}, u32[]{:S(2)}, u32[]{:S(2)}) collective-permute-start(bf16[1,128,768]{2,1,0:T(8,128)(2,1)} %get-tuple-element.266), channel_id=1, source_target_pairs={{0,2},{1,3},{2,0},{3,1},{4,6},{5,7},{6,4},{7,5},{8,10},{9,11},{10,... | collective-permute-start | bytes 589832 | tf_op jit(solution)/shard_map/ppermute | solution.py:840
  168.4 24.1 %collective-permute-start.23 = (bf16[1,128,768]{2,1,0:T(8,128)(2,1)}, bf16[1,128,768]{2,1,0:T(8,128)(2,1)}, u32[]{:S(2)}, u32[]{:S(2)}) collective-permute-start(bf16[1,128,768]{2,1,0:T(8,128)(2,1)} %get-tuple-element.267), channel_id=1, source_target_pairs={{0,1},{1,2},{2,3},{3,0},{4,5},{5,6},{6,7},{7,4},{8,9},{9,10},{10,1... | collective-permute-start | bytes 589832 | tf_op jit(solution)/shard_map/ppermute | solution.py:840
  171.1 49.4 %collective-permute-start.28 = (bf16[96,768]{1,0:T(8,128)(2,1)}, bf16[96,768]{1,0:T(8,128)(2,1)}, u32[]{:S(2)}, u32[]{:S(2)}) collective-permute-start(bf16[96,768]{1,0:T(8,128)(2,1)} %get-tuple-element.287), channel_id=1, source_target_pairs={{0,2},{1,3},{2,0},{3,1},{4,6},{5,7},{6,4},{7,5},{8,10},{9,11},{10,... | collective-permute-start | bytes 442376 | tf_op jit(solution)/shard_map/ppermute | solution.py:840
  173.2 14.5 %collective-permute-start.24 = (bf16[384,1024]{1,0:T(8,128)(2,1)S(1)}, bf16[384,1024]{1,0:T(8,128)(2,1)S(1)}, u32[]{:S(2)}, u32[]{:S(2)}) collective-permute-start(bf16[384,1024]{1,0:T(8,128)(2,1)S(1)} %get-tuple-element.269), channel_id=1, source_target_pairs={{0,16},{1,17},{2,18},{3,19},{4,12},{5,13},{6,14},{7,15},{8,24},{9,... | collective-permute-start | bytes 2359304 | tf_op jit(solution)/shard_map/ppermute | solution.py:840
  173.8 13.9 %copy-start = (f32[32,768]{1,0:T(8,128)S(1)}, f32[32,768]{1,0:T(8,128)}, u32[]{:S(2)}) copy-start(f32[32,768]{1,0:T(8,128)} %constant_dynamic-update-slice_fusion.1) | copy-start | bytes 294916
  187.7 29.4 %collective-permute-start.18 = (bf16[1,128,768]{2,1,0:T(8,128)(2,1)S(1)}, bf16[1,128,768]{2,1,0:T(8,128)(2,1)S(1)}, u32[]{:S(2)}, u32[]{:S(2)}) collective-permute-start(bf16[1,128,768]{2,1,0:T(8,128)(2,1)S(1)} %get-tuple-element.261), channel_id=1, source_target_pairs={{0,3},{1,0},{2,1},{3,2},{4,7},{5,4},{6,5},{7,6},{8,11},{9,8},{10,9... | collective-permute-start | bytes 589832 | tf_op jit(solution)/shard_map/ppermute | solution.py:840
  190.9 27.3 %collective-permute-start.19 = (bf16[1,128,768]{2,1,0:T(8,128)(2,1)S(1)}, bf16[1,128,768]{2,1,0:T(8,128)(2,1)S(1)}, u32[]{:S(2)}, u32[]{:S(2)}) collective-permute-start(bf16[1,128,768]{2,1,0:T(8,128)(2,1)S(1)} %get-tuple-element.262), channel_id=1, source_target_pairs={{0,2},{1,3},{2,0},{3,1},{4,6},{5,7},{6,4},{7,5},{8,10},{9,11},{10,... | collective-permute-start | bytes 589832 | tf_op jit(solution)/shard_map/ppermute | solution.py:840
  191.6 26.7 %collective-permute-start.20 = (bf16[1,128,768]{2,1,0:T(8,128)(2,1)S(1)}, bf16[1,128,768]{2,1,0:T(8,128)(2,1)S(1)}, u32[]{:S(2)}, u32[]{:S(2)}) collective-permute-start(bf16[1,128,768]{2,1,0:T(8,128)(2,1)S(1)} %get-tuple-element.263), channel_id=1, source_target_pairs={{0,1},{1,2},{2,3},{3,0},{4,5},{5,6},{6,7},{7,4},{8,9},{9,10},{10,1... | collective-permute-start | bytes 589832 | tf_op jit(solution)/shard_map/ppermute | solution.py:840
  198.7 4.0 %collective-permute-start.26 = (bf16[1536,640]{1,0:T(8,128)(2,1)S(1)}, bf16[1536,640]{1,0:T(8,128)(2,1)S(1)}, u32[]{:S(2)}, u32[]{:S(2)}) collective-permute-start(bf16[1536,640]{1,0:T(8,128)(2,1)S(1)} %get-tuple-element.279), channel_id=1, source_target_pairs={{0,4},{1,5},{2,6},{3,7},{4,0},{5,1},{6,2},{7,3},{8,12},{9,13},{10,... | collective-permute-start | bytes 5898248 | tf_op jit(solution)/shard_map/ppermute | solution.py:840
  202.7 14.3 %collective-permute-start.25 = (bf16[192,1024]{1,0:T(8,128)(2,1)S(1)}, bf16[192,1024]{1,0:T(8,128)(2,1)S(1)}, u32[]{:S(2)}, u32[]{:S(2)}) collective-permute-start(bf16[192,1024]{1,0:T(8,128)(2,1)S(1)} %get-tuple-element.274), channel_id=1, source_target_pairs={{0,1},{1,0},{2,3},{3,2},{4,5},{5,4},{6,7},{7,6},{8,9},{9,8},{10,11... | collective-permute-start | bytes 1179656 | tf_op jit(solution)/shard_map/ppermute | solution.py:840
  217.1 16.5 %collective-permute-start.30 = (f32[32,768]{1,0:T(8,128)S(1)}, f32[32,768]{1,0:T(8,128)S(1)}, u32[]{:S(2)}, u32[]{:S(2)}) collective-permute-start(f32[32,768]{1,0:T(8,128)S(1)} %constant_dynamic-update-slice_fusion.refs_0_), channel_id=1, source_target_pairs={{0,4},{1,5},{2,6},{3,7},{4,0},{5,1},{6,2},{7,3},{8,12},{9,13},{10,... | collective-permute-start | bytes 294920 | tf_op jit(solution)/shard_map/ppermute | solution.py:840
  217.2 14.2 %collective-permute-start.27 = (bf16[768,640]{1,0:T(8,128)(2,1)S(1)}, bf16[768,640]{1,0:T(8,128)(2,1)S(1)}, u32[]{:S(2)}, u32[]{:S(2)}) collective-permute-start(bf16[768,640]{1,0:T(8,128)(2,1)S(1)} %get-tuple-element.285), channel_id=1, source_target_pairs={{0,8},{1,9},{2,10},{3,11},{4,20},{5,21},{6,22},{7,23},{8,0},{9,1},... | collective-permute-start | bytes 2949128 | tf_op jit(solution)/shard_map/ppermute | solution.py:840
  218.2 15.1 %collective-permute-start.31 = (bf16[96,1024]{1,0:T(8,128)(2,1)S(1)}, bf16[96,1024]{1,0:T(8,128)(2,1)S(1)}, u32[]{:S(2)}, u32[]{:S(2)}) collective-permute-start(bf16[96,1024]{1,0:T(8,128)(2,1)S(1)} %get-tuple-element.296), channel_id=1, source_target_pairs={{0,2},{1,3},{2,0},{3,1},{4,6},{5,7},{6,4},{7,5},{8,10},{9,11},{10,... | collective-permute-start | bytes 589832 | tf_op jit(solution)/shard_map/ppermute | solution.py:840
  221.5 20.3 %collective-permute-start.35 = (bf16[96,768]{1,0:T(8,128)(2,1)S(1)}, bf16[96,768]{1,0:T(8,128)(2,1)S(1)}, u32[]{:S(2)}, u32[]{:S(2)}) collective-permute-start(bf16[96,768]{1,0:T(8,128)(2,1)S(1)} %get-tuple-element.304.refs_1_), channel_id=1, source_target_pairs={{0,2},{1,3},{2,0},{3,1},{4,6},{5,7},{6,4},{7,5},{8,10},{9,11},{10,... | collective-permute-start | bytes 442376 | tf_op jit(solution)/shard_map/ppermute | solution.py:840
  231.6 9.9 %collective-permute-start.29 = (bf16[384,640]{1,0:T(8,128)(2,1)S(1)}, bf16[384,640]{1,0:T(8,128)(2,1)S(1)}, u32[]{:S(2)}, u32[]{:S(2)}) collective-permute-start(bf16[384,640]{1,0:T(8,128)(2,1)S(1)} %get-tuple-element.291), channel_id=1, source_target_pairs={{0,16},{1,17},{2,18},{3,19},{4,12},{5,13},{6,14},{7,15},{8,24},{9,... | collective-permute-start | bytes 1474568 | tf_op jit(solution)/shard_map/ppermute | solution.py:840
  233.4 11.8 %collective-permute-start.33 = (bf16[96,1024]{1,0:T(8,128)(2,1)S(1)}, bf16[96,1024]{1,0:T(8,128)(2,1)S(1)}, u32[]{:S(2)}, u32[]{:S(2)}) collective-permute-start(bf16[96,1024]{1,0:T(8,128)(2,1)S(1)} %get-tuple-element.302.refs_1_), channel_id=1, source_target_pairs={{0,2},{1,3},{2,0},{3,1},{4,6},{5,7},{6,4},{7,5},{8,10},{9,11},{10,... | collective-permute-start | bytes 589832 | tf_op jit(solution)/shard_map/ppermute | solution.py:840
  233.5 8.2 %collective-permute-start.34 = (f32[32,768]{1,0:T(8,128)S(1)}, f32[32,768]{1,0:T(8,128)S(1)}, u32[]{:S(2)}, u32[]{:S(2)}) collective-permute-start(f32[32,768]{1,0:T(8,128)S(1)} %get-tuple-element.303.refs_0_), channel_id=1, source_target_pairs={{0,8},{1,9},{2,10},{3,11},{4,20},{5,21},{6,22},{7,23},{8,0},{9,1},... | collective-permute-start | bytes 294920 | tf_op jit(solution)/shard_map/ppermute | solution.py:840
  241.6 9.0 %collective-permute-start.32 = (bf16[192,640]{1,0:T(8,128)(2,1)S(1)}, bf16[192,640]{1,0:T(8,128)(2,1)S(1)}, u32[]{:S(2)}, u32[]{:S(2)}) collective-permute-start(bf16[192,640]{1,0:T(8,128)(2,1)S(1)} %get-tuple-element.301), channel_id=1, source_target_pairs={{0,1},{1,0},{2,3},{3,2},{4,5},{5,4},{6,7},{7,6},{8,9},{9,8},{10,11... | collective-permute-start | bytes 737288 | tf_op jit(solution)/shard_map/ppermute | solution.py:840
  241.8 9.0 %collective-permute-start.37 = (f32[32,768]{1,0:T(8,128)S(1)}, f32[32,768]{1,0:T(8,128)S(1)}, u32[]{:S(2)}, u32[]{:S(2)}) collective-permute-start(f32[32,768]{1,0:T(8,128)S(1)} %get-tuple-element.311.refs_0_), channel_id=1, source_target_pairs={{0,16},{1,17},{2,18},{3,19},{4,12},{5,13},{6,14},{7,15},{8,24},{9,... | collective-permute-start | bytes 294920 | tf_op jit(solution)/shard_map/ppermute | solution.py:840
  243.2 16.3 %collective-permute-start.39 = (bf16[192,768]{1,0:T(8,128)(2,1)S(1)}, bf16[192,768]{1,0:T(8,128)(2,1)S(1)}, u32[]{:S(2)}, u32[]{:S(2)}) collective-permute-start(bf16[192,768]{1,0:T(8,128)(2,1)S(1)} %get-tuple-element.314.refs_1_), channel_id=1, source_target_pairs={{0,1},{1,0},{2,3},{3,2},{4,5},{5,4},{6,7},{7,6},{8,9},{9,8},{10,11... | collective-permute-start | bytes 884744 | tf_op jit(solution)/shard_map/ppermute | solution.py:840
  245.3 27.4 %collective-permute-start.43 = (bf16[192,1024]{1,0:T(8,128)(2,1)S(1)}, bf16[192,1024]{1,0:T(8,128)(2,1)S(1)}, u32[]{:S(2)}, u32[]{:S(2)}) collective-permute-start(bf16[192,1024]{1,0:T(8,128)(2,1)S(1)} %get-tuple-element.321.refs_1_), channel_id=1, source_target_pairs={{0,1},{1,0},{2,3},{3,2},{4,5},{5,4},{6,7},{7,6},{8,9},{9,8},{10,11... | collective-permute-start | bytes 1179656 | tf_op jit(solution)/shard_map/ppermute | solution.py:840
  250.7 19.0 %collective-permute-start.36 = (bf16[96,640]{1,0:T(8,128)(2,1)S(1)}, bf16[96,640]{1,0:T(8,128)(2,1)S(1)}, u32[]{:S(2)}, u32[]{:S(2)}) collective-permute-start(bf16[96,640]{1,0:T(8,128)(2,1)S(1)} %get-tuple-element.310), channel_id=1, source_target_pairs={{0,2},{1,3},{2,0},{3,1},{4,6},{5,7},{6,4},{7,5},{8,10},{9,11},{10,... | collective-permute-start | bytes 368648 | tf_op jit(solution)/shard_map/ppermute | solution.py:840
  250.8 18.8 %collective-permute-start.38 = (f32[32,768]{1,0:T(8,128)S(1)}, f32[32,768]{1,0:T(8,128)S(1)}, u32[]{:S(2)}, u32[]{:S(2)}) collective-permute-start(f32[32,768]{1,0:T(8,128)S(1)} %get-tuple-element.313.refs_0_), channel_id=1, source_target_pairs={{0,1},{1,0},{2,3},{3,2},{4,5},{5,4},{6,7},{7,6},{8,9},{9,8},{10,11... | collective-permute-start | bytes 294920 | tf_op jit(solution)/shard_map/ppermute | solution.py:840
  259.6 19.1 %collective-permute-start.41 = (bf16[384,768]{1,0:T(8,128)(2,1)S(1)}, bf16[384,768]{1,0:T(8,128)(2,1)S(1)}, u32[]{:S(2)}, u32[]{:S(2)}) collective-permute-start(bf16[384,768]{1,0:T(8,128)(2,1)S(1)} %get-tuple-element.319.refs_1_), channel_id=1, source_target_pairs={{0,16},{1,17},{2,18},{3,19},{4,12},{5,13},{6,14},{7,15},{8,24},{9,... | collective-permute-start | bytes 1769480 | tf_op jit(solution)/shard_map/ppermute | solution.py:840
  269.6 9.1 %collective-permute-start.42 = (f32[32,768]{1,0:T(8,128)S(1)}, f32[32,768]{1,0:T(8,128)S(1)}, u32[]{:S(2)}, u32[]{:S(2)}) collective-permute-start(f32[32,768]{1,0:T(8,128)S(1)} %get-tuple-element.320.refs_0_), channel_id=1, source_target_pairs={{0,2},{1,3},{2,0},{3,1},{4,6},{5,7},{6,4},{7,5},{8,10},{9,11},{10,... | collective-permute-start | bytes 294920 | tf_op jit(solution)/shard_map/ppermute | solution.py:840
  269.7 11.5 %collective-permute-start.40 = (bf16[96,640]{1,0:T(8,128)(2,1)S(1)}, bf16[96,640]{1,0:T(8,128)(2,1)S(1)}, u32[]{:S(2)}, u32[]{:S(2)}) collective-permute-start(bf16[96,640]{1,0:T(8,128)(2,1)S(1)} %get-tuple-element.318.refs_1_), channel_id=1, source_target_pairs={{0,2},{1,3},{2,0},{3,1},{4,6},{5,7},{6,4},{7,5},{8,10},{9,11},{10,... | collective-permute-start | bytes 368648 | tf_op jit(solution)/shard_map/ppermute | solution.py:840
  272.7 15.4 %collective-permute-start.46 = (bf16[384,1024]{1,0:T(8,128)(2,1)S(1)}, bf16[384,1024]{1,0:T(8,128)(2,1)S(1)}, u32[]{:S(2)}, u32[]{:S(2)}) collective-permute-start(bf16[384,1024]{1,0:T(8,128)(2,1)S(1)} %get-tuple-element.328.refs_1_), channel_id=1, source_target_pairs={{0,16},{1,17},{2,18},{3,19},{4,12},{5,13},{6,14},{7,15},{8,24},{9,... | collective-permute-start | bytes 2359304 | tf_op jit(solution)/shard_map/ppermute | solution.py:840
  278.8 16.7 %collective-permute-start.45 = (bf16[768,768]{1,0:T(8,128)(2,1)S(1)}, bf16[768,768]{1,0:T(8,128)(2,1)S(1)}, u32[]{:S(2)}, u32[]{:S(2)}) collective-permute-start(bf16[768,768]{1,0:T(8,128)(2,1)S(1)} %get-tuple-element.327.refs_1_), channel_id=1, source_target_pairs={{0,8},{1,9},{2,10},{3,11},{4,20},{5,21},{6,22},{7,23},{8,0},{9,1},... | collective-permute-start | bytes 3538952 | tf_op jit(solution)/shard_map/ppermute | solution.py:840
  279.9 19.3 %collective-permute-start.48 = (bf16[768,768]{1,0:T(8,128)(2,1)S(1)}, bf16[768,768]{1,0:T(8,128)(2,1)S(1)}, u32[]{:S(2)}, u32[]{:S(2)}) collective-permute-start(bf16[768,768]{1,0:T(8,128)(2,1)S(1)} %get-tuple-element.327.refs_1_), channel_id=1, source_target_pairs={{0,4},{1,5},{2,6},{3,7},{4,0},{5,1},{6,2},{7,3},{8,12},{9,13},{10,... | collective-permute-start | bytes 3538952 | tf_op jit(solution)/shard_map/ppermute | solution.py:840
  281.2 17.2 %collective-permute-start.44 = (bf16[192,640]{1,0:T(8,128)(2,1)S(1)}, bf16[192,640]{1,0:T(8,128)(2,1)S(1)}, u32[]{:S(2)}, u32[]{:S(2)}) collective-permute-start(bf16[192,640]{1,0:T(8,128)(2,1)S(1)} %get-tuple-element.326.refs_1_), channel_id=1, source_target_pairs={{0,1},{1,0},{2,3},{3,2},{4,5},{5,4},{6,7},{7,6},{8,9},{9,8},{10,11... | collective-permute-start | bytes 737288 | tf_op jit(solution)/shard_map/ppermute | solution.py:840
  295.5 4.2 %collective-permute-start.49 = (bf16[768,768]{1,0:T(8,128)(2,1)S(1)}, bf16[768,768]{1,0:T(8,128)(2,1)S(1)}, u32[]{:S(2)}, u32[]{:S(2)}) collective-permute-start(bf16[768,768]{1,0:T(8,128)(2,1)S(1)} %get-tuple-element.333.refs_2_), channel_id=1, source_target_pairs={{0,4},{1,5},{2,6},{3,7},{4,0},{5,1},{6,2},{7,3},{8,12},{9,13},{10,... | collective-permute-start | bytes 3538952 | tf_op jit(solution)/shard_map/ppermute | solution.py:840
  297.3 25.7 %collective-permute-start.51 = (bf16[768,1024]{1,0:T(8,128)(2,1)S(1)}, bf16[768,1024]{1,0:T(8,128)(2,1)S(1)}, u32[]{:S(2)}, u32[]{:S(2)}) collective-permute-start(bf16[768,1024]{1,0:T(8,128)(2,1)S(1)} %get-tuple-element.337.refs_1_), channel_id=1, source_target_pairs={{0,8},{1,9},{2,10},{3,11},{4,20},{5,21},{6,22},{7,23},{8,0},{9,1},... | collective-permute-start | bytes 4718600 | tf_op jit(solution)/shard_map/ppermute | solution.py:840
  298.4 25.7 %collective-permute-start.52 = (bf16[768,1024]{1,0:T(8,128)(2,1)S(1)}, bf16[768,1024]{1,0:T(8,128)(2,1)S(1)}, u32[]{:S(2)}, u32[]{:S(2)}) collective-permute-start(bf16[768,1024]{1,0:T(8,128)(2,1)S(1)} %get-tuple-element.337.refs_1_), channel_id=1, source_target_pairs={{0,4},{1,5},{2,6},{3,7},{4,0},{5,1},{6,2},{7,3},{8,12},{9,13},{10,... | collective-permute-start | bytes 4718600 | tf_op jit(solution)/shard_map/ppermute | solution.py:840
  298.4 14.2 %collective-permute-start.47 = (bf16[384,640]{1,0:T(8,128)(2,1)S(1)}, bf16[384,640]{1,0:T(8,128)(2,1)S(1)}, u32[]{:S(2)}, u32[]{:S(2)}) collective-permute-start(bf16[384,640]{1,0:T(8,128)(2,1)S(1)} %get-tuple-element.332.refs_1_), channel_id=1, source_target_pairs={{0,16},{1,17},{2,18},{3,19},{4,12},{5,13},{6,14},{7,15},{8,24},{9,... | collective-permute-start | bytes 1474568 | tf_op jit(solution)/shard_map/ppermute | solution.py:840
  323.0 3.4 collective-permute-start.53
  323.0 14.2 %collective-permute-start.50 = (bf16[768,640]{1,0:T(8,128)(2,1)S(1)}, bf16[768,640]{1,0:T(8,128)(2,1)}, u32[]{:S(2)}, u32[]{:S(2)}) collective-permute-start(bf16[768,640]{1,0:T(8,128)(2,1)S(1)} %get-tuple-element.336.refs_1_), channel_id=1, source_target_pairs={{0,8},{1,9},{2,10},{3,11},{4,20},{5,21},{6,22},{7,23},{8,0},{9,1},... | collective-permute-start | bytes 2949128 | tf_op jit(solution)/shard_map/ppermute | solution.py:840
  324.1 15.5 %collective-permute-start.54 = (bf16[768,640]{1,0:T(8,128)(2,1)S(1)}, bf16[768,640]{1,0:T(8,128)(2,1)S(1)}, u32[]{:S(2)}, u32[]{:S(2)}) collective-permute-start(bf16[768,640]{1,0:T(8,128)(2,1)S(1)} %get-tuple-element.336.refs_1_), channel_id=1, source_target_pairs={{0,4},{1,5},{2,6},{3,7},{4,0},{5,1},{6,2},{7,3},{8,12},{9,13},{10,... | collective-permute-start | bytes 2949128 | tf_op jit(solution)/shard_map/ppermute | solution.py:840
  337.2 2.8 collective-permute-start.55
  (22 other events, 103.8 us)
